TPU v7x, 512 devices: a whole 4x8x8 slice. The times are simulated.
512 devices in a mesh: seq: 32 (over z, x), tensor: 16 (over y, core).
Axes of the slice: x: 4, y: 8, z: 8, core: 2. Of those that a mesh axis runs over, the one named last changes fastest.
Arguments:
- queries: bfloat16 [65536, 4096], P('seq', 'tensor'), may hold values from -30 to 30
- latents: bfloat16 [32, 64, 1280], P('seq'), may hold values from -6 to 6
- key_weight: bfloat16 [1280, 4096], P('seq', 'tensor'), may hold values from -0.15625 to 0.15625
- value_weight: bfloat16 [1280, 4096], P('seq', 'tensor'), may hold values from -0.15625 to 0.15625
- grad_out: bfloat16 [65536, 4096], P('seq', 'tensor'), may hold values from -6 to 6
- pairs: int32 [256, 4], P('seq'), may hold values from -1 to 31, as said below
- image_slot: int32 [32], replicated, may hold values from 0 to 31, each once
- token_doc: int32 [65536], P('seq'), may hold values from 0 to 7, as said below
Outputs:
- attended: bfloat16 [65536, 4096], P('seq', 'tensor')
- grad_queries: bfloat16 [65536, 4096], P('seq', 'tensor')
- grad_latents: bfloat16 [32, 64, 1280], P('seq')
Inputs may be any that keep to these rules, and one draw needn't show every extreme that they name: `pairs`: row c lists the images whose latents group c attends; -1 marks an empty slot, empty slots come last, listed images of a row are distinct, image i belongs to document i // 4; every token's document has an image listed in its group's row; some row is full. How many images a row lists is very uneven from device to device. `token_doc`: documents are runs of tokens in order, of uneven lengths; a group holds tokens of at most two documents.
All inputs are finite; a program needn't handle non-finite values.
Results may differ from a plain program's by a relative error of at most 0.029.
Values may be sent and summed in bfloat16 or wider, within the bound.
No kernel may reach another device: no remote copies, remote signals or barrier semaphores. Data moves between devices by JAX's collectives and lax.ppermute only.
A program may use at most 64 MiB of HBM per device.

v0:
```python
import jax
import jax.numpy as jnp
from jax import lax
from jax.sharding import PartitionSpec as P

HEAD = 128


MASKED_SCORE = -1e30


def lookup(slot_table, image_ids):
    matches = image_ids[..., None] == jnp.arange(slot_table.shape[0], dtype=jnp.int32)
    return jnp.sum(jnp.where(matches, slot_table, 0), axis=-1)


def softmax_probs(query_block, key_rows, visible, score_scale):
    scores = (
        jnp.einsum("cthd,ckhd->chtk", query_block, key_rows, preferred_element_type=jnp.float32)
        * score_scale
    )
    scores = jnp.where(visible, scores, MASKED_SCORE)
    row_max = jnp.max(scores, axis=-1, keepdims=True)
    exponent = jnp.where(visible, jnp.exp(scores - row_max), 0.0)
    return exponent / jnp.sum(exponent, axis=-1, keepdims=True)


def local(queries, latents, key_weight, value_weight, grad_out, pairs, image_slot, token_doc):
    head_cols = queries.shape[1]
    heads_here = head_cols // HEAD
    group_count = pairs.shape[0]
    slot_count = pairs.shape[1]
    latent_rows = latents.shape[1]
    images = image_slot.shape[0]
    seq_size = lax.axis_size("seq")
    per_doc = images // (seq_size // 4)
    group_len = queries.shape[0] // group_count
    score_scale = HEAD ** (-0.5)
    own_latents = latents[0]
    full_key, full_value = (
        lax.all_gather(key_weight, "seq", axis=0, tiled=True),
        lax.all_gather(value_weight, "seq", axis=0, tiled=True),
    )
    key_proj = jnp.dot(own_latents, full_key, preferred_element_type=jnp.float32).astype(
        jnp.bfloat16
    )
    value_proj = jnp.dot(own_latents, full_value, preferred_element_type=jnp.float32).astype(
        jnp.bfloat16
    )
    all_keys, all_values = (
        lax.all_gather(key_proj, "seq", axis=0, tiled=True),
        lax.all_gather(value_proj, "seq", axis=0, tiled=True),
    )
    slot_ids = lookup(image_slot, pairs)
    key_index = (
        slot_ids[:, :, None] * latent_rows + jnp.arange(latent_rows, dtype=jnp.int32)
    ).reshape(group_count, slot_count * latent_rows)
    key_rows = all_keys[key_index].reshape(group_count, slot_count * latent_rows, heads_here, HEAD)
    value_rows = all_values[key_index].reshape(
        group_count, slot_count * latent_rows, heads_here, HEAD
    )
    token_docs = token_doc.reshape(group_count, group_len)
    visible = (pairs >= 0)[:, None, :] & ((pairs // per_doc)[:, None, :] == token_docs[:, :, None])
    visible = jnp.repeat(visible, latent_rows, axis=2)[:, None]
    query_block = queries.reshape(group_count, group_len, heads_here, HEAD)
    cotangent = grad_out.reshape(group_count, group_len, heads_here, HEAD)
    attn_prob = softmax_probs(query_block, key_rows, visible, score_scale)
    prob_low = attn_prob.astype(jnp.bfloat16)
    attended = jnp.einsum(
        "chtk,ckhd->cthd", prob_low, value_rows, preferred_element_type=jnp.float32
    ).astype(jnp.bfloat16)
    prob_grad = jnp.einsum(
        "cthd,ckhd->chtk", cotangent, value_rows, preferred_element_type=jnp.float32
    )
    centre = jnp.sum(attn_prob * prob_grad, axis=-1, keepdims=True)
    score_grad = (attn_prob * (prob_grad - centre) * score_scale).astype(jnp.bfloat16)
    grad_queries = jnp.einsum(
        "chtk,ckhd->cthd", score_grad, key_rows, preferred_element_type=jnp.float32
    ).astype(jnp.bfloat16)
    key_grad_rows = jnp.einsum(
        "chtk,cthd->ckhd", score_grad, query_block, preferred_element_type=jnp.float32
    )
    value_grad_rows = jnp.einsum(
        "chtk,cthd->ckhd", prob_low, cotangent, preferred_element_type=jnp.float32
    )
    onehot = (slot_ids[:, :, None] == jnp.arange(images, dtype=jnp.int32)) & (pairs >= 0)[
        :, :, None
    ]
    onehot = onehot.astype(jnp.float32).reshape(group_count * slot_count, images)
    key_term = jnp.einsum(
        "ps,plx->slx",
        onehot,
        key_grad_rows.reshape(group_count * slot_count, latent_rows, head_cols),
        precision=lax.Precision.HIGHEST,
    )
    value_term = jnp.einsum(
        "ps,plx->slx",
        onehot,
        value_grad_rows.reshape(group_count * slot_count, latent_rows, head_cols),
        precision=lax.Precision.HIGHEST,
    )
    key_flat = key_term.reshape(images * latent_rows, head_cols)
    value_flat = value_term.reshape(images * latent_rows, head_cols)
    key_sum, value_sum = (
        lax.psum_scatter(
            key_flat.astype(jnp.bfloat16), "seq", scatter_dimension=0, tiled=True
        ).astype(jnp.float32),
        lax.psum_scatter(
            value_flat.astype(jnp.bfloat16), "seq", scatter_dimension=0, tiled=True
        ).astype(jnp.float32),
    )
    key_grad = key_sum.astype(jnp.bfloat16)
    value_grad = value_sum.astype(jnp.bfloat16)
    contract = (((1,), (1,)), ((), ()))
    latent_term = lax.dot_general(key_grad, full_key, contract, preferred_element_type=jnp.float32)
    latent_term = latent_term + lax.dot_general(
        value_grad, full_value, contract, preferred_element_type=jnp.float32
    )
    latent_total = lax.psum(latent_term.astype(jnp.bfloat16), "tensor")
    return (
        attended.reshape(-1, head_cols),
        grad_queries.reshape(-1, head_cols),
        latent_total[None],
    )


def solution(mesh):
    in_specs = (
        P("seq", "tensor"),
        P("seq", None, None),
        P("seq", "tensor"),
        P("seq", "tensor"),
        P("seq", "tensor"),
        P("seq", None),
        P(),
        P("seq"),
    )
    out_specs = (P("seq", "tensor"), P("seq", "tensor"), P("seq", None, None))
    return jax.shard_map(local, mesh=mesh, in_specs=in_specs, out_specs=out_specs, check_vma=False)
```

profile of v0, /device:TPU:1, one launch (start us, length us, event | category | flops | bytes accessed | tf_op | source)
XLA Modules:
  0.0 825.3 jit_solution(203886224160263837)
XLA Ops:
  7.2 0.0 copy-start
  7.2 0.0 copy-start.11
  7.2 0.0 all-gather.5.cloned.1.call-start
  7.3 44.6 %all_gather.14 = bf16[1280,256]{1,0:T(8,128)(2,1)S(1)} all-gather(bf16[40,256]{1,0:T(8,128)(2,1)} %param.10), channel_id=1, replica_groups=mesh['seq'=32,'tensor'=16] {'seq'}, dimensions={0}, use_global_device_ids=true | all-gather | bytes 675840 | tf_op jit(solution)/shard_map/all_gather | solution.py:41
  51.9 0.8 copy-done.1
  52.7 0.9 convolution_convert_fusion.1
  53.6 0.0 all-gather.5.cloned.1.call-update
  53.6 0.0 all-gather.3.cloned.1.call-start
  53.7 37.8 %all_gather.12 = bf16[1280,256]{1,0:T(8,128)(2,1)S(1)} all-gather(bf16[40,256]{1,0:T(8,128)(2,1)} %param.11), channel_id=1, replica_groups=mesh['seq'=32,'tensor'=16] {'seq'}, dimensions={0}, use_global_device_ids=true | all-gather | bytes 675840 | tf_op jit(solution)/shard_map/all_gather | solution.py:42
  91.5 0.9 convolution_convert_fusion.2
  92.3 0.0 all-gather.3.cloned.1.call-update
  92.4 0.0 reduce-scatter.3.cloned.1.call-start
  92.4 0.9 select_reduce_fusion
  93.3 0.1 copy.65
  93.4 0.1 copy.51
  93.5 0.1 add.48
  93.6 0.1 add.49
  93.7 0.1 add.51
  93.8 2.1 reshape.105
  95.9 0.1 copy.52
  96.0 0.1 copy.53
  96.1 1.1 reshape.107
  97.2 0.1 eq.51
  97.3 0.1 and.27
  97.4 0.1 compare_and_fusion
  97.5 43.0 %all-gather.5.cloned.1.call-done = bf16[2048,256]{1,0:T(8,128)(2,1)} async-done(((bf16[64,256]{1,0:T(8,128)(2,1)}), bf16[2048,256]{1,0:T(8,128)(2,1)}) %all-gather.5.cloned.1.call-update) | async-done | bytes 1048592 | tf_op jit(solution)/shard_map/all_gather | solution.py:51
  140.4 8.0 gather_fusion.1
  148.5 0.3 reshape.104
  148.7 0.7 copy.62
  149.5 0.0 copy-start.3
  149.5 73.7 %all-gather.3.cloned.1.call-done = bf16[2048,256]{1,0:T(8,128)(2,1)} async-done(((bf16[64,256]{1,0:T(8,128)(2,1)}), bf16[2048,256]{1,0:T(8,128)(2,1)}) %all-gather.3.cloned.1.call-update) | async-done | bytes 1048592 | tf_op jit(solution)/shard_map/all_gather | solution.py:52
  223.2 9.9 %gather_fusion = bf16[2048,256]{1,0:T(8,128)(2,1)} fusion(bf16[2048,256]{1,0:T(8,128)(2,1)} %all-gather.3.cloned.1.call-done, s32[2048]{0:T(1024)S(1)} %broadcast_clamp_fusion), kind=kCustom, calls=%fused_computation | custom fusion | bytes 2105344 | tf_op jit(solution)/shard_map/gather | solution.py:59
  233.0 1.3 reshape.103
  234.4 2.4 fusion.36
  236.7 0.1 broadcast_in_dim.50
  236.9 0.0 copy-start.4
  236.9 3.6 fusion.57
  240.5 2.7 fusion.31
  243.2 8.7 %fusion.18 = f32[8,256,2,128]{3,1,2,0:T(8,128)} fusion(f32[8,2,256,256]{3,2,1,0:T(8,128)} %fusion.31, bf16[8,256,2,128]{3,2,1,0:T(2,128)(2,1)S(1)} %copy-done.8, f32[8,2,256,256]{2,3,1,0:T(8,128)} %get-tuple-element.10, f32[8,2,256]{2,1,0:T(2,128)S(1)} %get-tuple-element.9), kind=kOutput, calls=%fused_computation.26 | convolution fusion | flops 275779840 | bytes 11550720 | tf_op jit(solution)/shard_map/chtk,cthd->ckhd/dot_general | solution.py:80
  251.9 3.2 copy.68
  255.1 2.7 reshape.109
  257.8 4.0 fusion.20
  261.8 1.6 copy.70
  263.4 0.0 reduce-scatter.3.cloned.1.call-update
  263.4 0.2 reduce-scatter.5.cloned.1.call-start
  263.6 2.9 convolution_bitcast_fusion
  266.5 3.0 copy.72
  269.6 2.9 reshape.110
  272.5 2.4 fusion.23
  274.9 1.6 copy.74
  276.5 0.0 reduce-scatter.5.cloned.1.call-update
  276.6 0.0 all-reduce.2.cloned.1.call-start
  276.6 8.6 %fusion.27 = bf16[8,256,2,128]{1,3,2,0:T(8,128)(2,1)} fusion(bf16[8,256,2,128]{1,3,2,0:T(8,128)(2,1)} %copy-done.3, f32[8,2,256,256]{3,2,1,0:T(8,128)} %fusion.31, f32[8,2,256,256]{2,3,1,0:T(8,128)} %get-tuple-element.10, f32[8,2,256]{2,1,0:T(2,128)S(1)} %get-tuple-element.9), kind=kOutput, calls=%fused_computation.33 | convolution fusion | flops 276304128 | bytes 10502144 | tf_op jit(solution)/shard_map/chtk,ckhd->cthd/dot_general | solution.py:77
  285.2 3.7 copy.80
  288.9 3.8 fusion.26
  292.7 3.8 copy.79
  296.5 184.0 %reduce-scatter.3.cloned.1.call-done = bf16[64,256]{1,0:T(8,128)(2,1)} async-done(((bf16[2048,256]{1,0:T(8,128)(2,1)}), bf16[64,256]{1,0:T(8,128)(2,1)}) %reduce-scatter.3.cloned.1.call-update) | async-done | bytes 32784 | tf_op jit(solution)/shard_map/reduce_scatter | solution.py:105
  480.5 1.1 fusion.58
  481.6 221.5 %reduce-scatter.5.cloned.1.call-done = bf16[64,256]{1,0:T(8,128)(2,1)} async-done(((bf16[2048,256]{1,0:T(8,128)(2,1)}), bf16[64,256]{1,0:T(8,128)(2,1)}) %reduce-scatter.5.cloned.1.call-update) | async-done | bytes 32784 | tf_op jit(solution)/shard_map/reduce_scatter | solution.py:108
  703.0 1.8 fusion.7
  704.8 0.0 all-reduce.2.cloned.1.call-update
  704.8 2.9 copy_bitcast_fusion
  707.7 109.4 %all-reduce.2.cloned.1.call-done = bf16[1,64,1280]{2,1,0:T(8,128)(2,1)} async-done(((bf16[1,64,1280]{2,1,0:T(8,128)(2,1)}), bf16[1,64,1280]{2,1,0:T(8,128)(2,1)}) %all-reduce.2.cloned.1.call-update) | async-done | bytes 163856 | tf_op jit(solution)/shard_map/psum | solution.py:119
  817.1 1.6 copy.109
  (29 shorter events, 0.1 us)
Async XLA Ops:
  7.2 45.6 %copy-start = (bf16[1,64,1280]{2,1,0:T(8,128)(2,1)S(1)}, bf16[1,64,1280]{2,1,0:T(8,128)(2,1)}, u32[]{:S(2)}) copy-start(bf16[1,64,1280]{2,1,0:T(8,128)(2,1)} %param.9) | copy-start | bytes 491524
  7.2 88.7 %copy-start.11 = (s32[8,4]{0,1:T(4,128)S(1)}, s32[8,4]{0,1:T(4,128)}, u32[]{:S(2)}) copy-start(s32[8,4]{0,1:T(4,128)} %param.13) | copy-start | bytes 388
  7.2 88.8 %copy-start.12 = (s32[2048]{0:T(1024)S(1)}, s32[2048]{0:T(1024)}, u32[]{:S(2)}) copy-start(s32[2048]{0:T(1024)} %param.15) | copy-start | bytes 24580
  7.2 88.9 %copy-start.10 = (bf16[2048,256]{1,0:T(8,128)(2,1)S(1)}, bf16[2048,256]{1,0:T(8,128)(2,1)}, u32[]{:S(2)}) copy-start(bf16[2048,256]{1,0:T(8,128)(2,1)} %param.12) | copy-start | bytes 3145732
  7.2 133.2 %all-gather.5.cloned.1.call-start = ((), (), s32[]{:S(2)}) async-start(), calls=%async_computation.3 | async-start | bytes 1081344 | tf_op jit(solution)/shard_map/all_gather | solution.py:51
  51.9 0.8 copy-start.1
  53.6 169.5 %all-gather.3.cloned.1.call-start = ((), (), s32[]{:S(2)}) async-start(), calls=%async_computation.2 | async-start | bytes 1081344 | tf_op jit(solution)/shard_map/all_gather | solution.py:52
  92.4 388.1 %reduce-scatter.3.cloned.1.call-start = ((), (), s32[]{:S(2)}) async-start(), calls=%async_computation.4 | async-start | bytes 1081344 | tf_op jit(solution)/shard_map/reduce_scatter | solution.py:105
  149.5 84.9 %copy-start.3 = (bf16[8,256,2,128]{1,3,2,0:T(8,128)(2,1)}, bf16[8,256,2,128]{1,3,2,0:T(8,128)(2,1)S(1)}, u32[]{:S(2)}) copy-start(bf16[8,256,2,128]{1,3,2,0:T(8,128)(2,1)S(1)} %copy.62) | copy-start | bytes 3145732
  234.4 6.1 copy-start.6
  236.9 3.6 copy-start.4
  240.5 2.7 copy-start.8
  257.8 5.8 copy-start.5
  263.4 439.6 %reduce-scatter.5.cloned.1.call-start = ((), (), s32[]{:S(2)}) async-start(), calls=%async_computation.5 | async-start | bytes 1081344 | tf_op jit(solution)/shard_map/reduce_scatter | solution.py:108
  276.5 12.3 %copy-start.7 = (bf16[8,256,2,128]{3,2,1,0:T(2,128)(2,1)S(1)}, bf16[8,256,2,128]{3,2,1,0:T(2,128)(2,1)}, u32[]{:S(2)}) copy-start(bf16[8,256,2,128]{3,2,1,0:T(2,128)(2,1)} %copy-done.6) | copy-start | bytes 3145732
  276.6 540.6 %all-reduce.2.cloned.1.call-start = ((), (), s32[]{:S(2)}) async-start(), calls=%async_computation.6 | async-start | bytes 327680 | tf_op jit(solution)/shard_map/psum | solution.py:119
  288.9 191.6 %copy-start.2 = (bf16[1280,256]{1,0:T(8,128)(2,1)S(1)}, bf16[1280,256]{1,0:T(8,128)(2,1)}, u32[]{:S(2)}) copy-start(bf16[1280,256]{1,0:T(8,128)(2,1)} %copy-done.1) | copy-start | bytes 1966084
  292.7 412.1 %copy-start.9 = (bf16[8,256,2,128]{3,2,1,0:T(2,128)(2,1)S(1)}, bf16[8,256,2,128]{3,2,1,0:T(2,128)(2,1)}, u32[]{:S(2)}) copy-start(bf16[8,256,2,128]{3,2,1,0:T(2,128)(2,1)} %copy.80) | copy-start | bytes 3145732
Sparse Core Ops, SparseCore 0:
  53.7 86.6 all-gather.4
  143.6 79.5 all-gather.2
  263.5 216.9 reduce-scatter.2
  484.7 218.2 reduce-scatter.4
  705.8 111.3 all-reduce.1
where the time goes:
time: 826 us; the launch traced here: 825 us
  waiting for transfers between devices  632 us (77%)
  blocking collectives  82.4 us (10%)
  local copies, waits for them, and re-layouts  52.1 us (6%)
  matrix products  40.1 us (5%)
  between operations  14 us (2%)
    reduce_scatter x1, waiting for transfers between devices, local(): lax.psum_scatter(value_flat.astype(jnp.bfloat16), 'seq', scatter_dimensio...  221 us
    reduce_scatter x1, waiting for transfers between devices, local(): lax.psum_scatter(key_flat.astype(jnp.bfloat16), 'seq', scatter_dimension=...  184 us
    psum x1, waiting for transfers between devices, local(): latent_total = lax.psum(latent_term.astype(jnp.bfloat16), 'tensor')  109 us
    all_gather x1, waiting for transfers between devices, local(): lax.all_gather(value_proj, 'seq', axis=0, tiled=True)  73.7 us
    all_gather x1, blocking collectives, local(): lax.all_gather(key_weight, 'seq', axis=0, tiled=True)  44.6 us
    all_gather x1, waiting for transfers between devices, local(): lax.all_gather(key_proj, 'seq', axis=0, tiled=True)  43 us
    all_gather x1, blocking collectives, local(): lax.all_gather(value_weight, 'seq', axis=0, tiled=True)  37.8 us
  transfers between devices with their start and end apart: 5, of which 5 were waited for; matrix products, arithmetic and copies ran while one was open for 6% of the time, Pallas kernels for 0%

commit v1 on v0

v1 whole, which is shorter than its diff:
```python
import jax
import jax.numpy as jnp
from jax import lax
from jax.experimental import pallas as pl
from jax.experimental.pallas import tpu as pltpu
from jax.sharding import Mesh
from jax.sharding import PartitionSpec as P

HEAD = 128
LAT = 64
GROUP = 256
GROUPS = 8
SLOTS = 4
IPD = 4
NX = 4
NZ = 8
NT = 16
COLS = 256
WIDE = 2 * COLS
VIS = 1280
IMAGES = 32
MASKED = -1.0e30
SCALE = HEAD ** -0.5
LOG2E = 1.4426950408889634

NT_DIMS = (((1,), (1,)), ((), ()))
TN_DIMS = (((0,), (0,)), ((), ()))


def attention_kernel(rel_ref, abs_ref, doc_ref, tok_ref, q_ref, g_ref, p0, p1, p2, p3,
                     att_ref, dq_ref, dkv_ref, kv, acc, sem):
    group = pl.program_id(0)

    @pl.when(group == 0)
    def _():
        copies = [
            pltpu.make_async_copy(piece, kv.at[pl.ds(i * NZ, NZ)], sem.at[i])
            for i, piece in enumerate((p0, p1, p2, p3))
        ]
        for copy in copies:
            copy.start()
        acc[...] = jnp.zeros_like(acc)
        for copy in copies:
            copy.wait()

    tok = tok_ref[0]
    rel = [rel_ref[group, j] for j in range(SLOTS)]
    dst = [abs_ref[group, j] for j in range(SLOTS)]
    bias = [jnp.where(tok == doc_ref[group, j], 0.0, MASKED) for j in range(SLOTS)]
    bias = jnp.concatenate([jnp.broadcast_to(b, (LAT, GROUP)) for b in bias], axis=0)
    for head in range(COLS // HEAD):
        lo = head * HEAD
        k = jnp.concatenate([kv[r, :, lo:lo + HEAD] for r in rel], axis=0)
        v = jnp.concatenate([kv[r, :, COLS + lo:COLS + lo + HEAD] for r in rel], axis=0)
        q = q_ref[:, lo:lo + HEAD]
        g = g_ref[:, lo:lo + HEAD]
        s = lax.dot_general(k, q, NT_DIMS, preferred_element_type=jnp.float32) + bias
        top = jnp.max(s, axis=0, keepdims=True)
        e = jnp.exp2((s - top) * (SCALE * LOG2E))
        p = e * (1.0 / jnp.sum(e, axis=0, keepdims=True))
        low = p.astype(jnp.bfloat16)
        dp = lax.dot_general(v, g, NT_DIMS, preferred_element_type=jnp.float32)
        centre = jnp.sum(p * dp, axis=0, keepdims=True)
        sg = (p * (dp - centre) * SCALE).astype(jnp.bfloat16)
        att = lax.dot_general(low, v, TN_DIMS, preferred_element_type=jnp.float32)
        dq = lax.dot_general(sg, k, TN_DIMS, preferred_element_type=jnp.float32)
        att_ref[:, lo:lo + HEAD] = att.astype(jnp.bfloat16)
        dq_ref[:, lo:lo + HEAD] = dq.astype(jnp.bfloat16)
        dk = jnp.dot(sg, q, preferred_element_type=jnp.float32)
        dv = jnp.dot(low, g, preferred_element_type=jnp.float32)
        for j in range(SLOTS):
            rows = slice(j * LAT, (j + 1) * LAT)
            acc[dst[j], :, lo:lo + HEAD] += dk[rows]
            acc[dst[j], :, COLS + lo:COLS + lo + HEAD] += dv[rows]

    @pl.when(group == GROUPS - 1)
    def _():
        dkv_ref[...] = acc[...].astype(jnp.bfloat16)


def attention(rel, dst, docs, tok, queries, grad_out, pieces):
    tokens = queries.shape[0]
    block = pl.BlockSpec((GROUP, COLS), lambda g, *_: (g, 0))
    return pl.pallas_call(
        attention_kernel,
        grid_spec=pltpu.PrefetchScalarGridSpec(
            num_scalar_prefetch=3,
            grid=(GROUPS,),
            in_specs=[
                pl.BlockSpec((1, 1, GROUP), lambda g, *_: (g, 0, 0)),
                block,
                block,
            ] + [pl.BlockSpec(memory_space=pl.ANY)] * NX,
            out_specs=[
                block,
                block,
                pl.BlockSpec((IMAGES, LAT, WIDE), lambda g, *_: (0, 0, 0)),
            ],
            scratch_shapes=[
                pltpu.VMEM((IMAGES, LAT, WIDE), jnp.bfloat16),
                pltpu.VMEM((IMAGES, LAT, WIDE), jnp.float32),
                pltpu.SemaphoreType.DMA((NX,)),
            ],
        ),
        out_shape=[
            jax.ShapeDtypeStruct((tokens, COLS), jnp.bfloat16),
            jax.ShapeDtypeStruct((tokens, COLS), jnp.bfloat16),
            jax.ShapeDtypeStruct((IMAGES, LAT, WIDE), jnp.bfloat16),
        ],
        compiler_params=pltpu.CompilerParams(
            dimension_semantics=("arbitrary",), vmem_limit_bytes=40 * 2**20
        ),
        cost_estimate=pl.CostEstimate(
            flops=12 * tokens * GROUP * COLS, bytes_accessed=9 * 2**20, transcendentals=0
        ),
    )(rel, dst, docs, tok, queries, grad_out, *pieces)


def from_offset(value, axis, size, step):
    return lax.ppermute(value, axis, [(i, (i - step) % size) for i in range(size)])


def local(queries, latents, key_weight, value_weight, grad_out, pairs, image_slot, token_doc):
    x = lax.axis_index("x")
    z = lax.axis_index("z")
    weight = jnp.concatenate([key_weight, value_weight], axis=1)
    weight = lax.all_gather(weight, "x", axis=0, tiled=True)
    weight = lax.all_gather(weight, "z", axis=0, tiled=True)
    kv = jnp.dot(latents[0], weight, preferred_element_type=jnp.float32).astype(jnp.bfloat16)
    column = jnp.stack([kv] + [from_offset(kv, "z", NZ, i) for i in range(1, NZ)])
    pieces = [column] + [from_offset(column, "x", NX, i) for i in range(1, NX)]

    matches = pairs[..., None] == jnp.arange(IMAGES, dtype=jnp.int32)
    slot = jnp.sum(jnp.where(matches, image_slot, 0), axis=-1).astype(jnp.int32)
    slot_z, slot_x = slot // NX, slot % NX
    rel = (slot_x - x) % NX * NZ + (slot_z - z) % NZ
    dst = slot_x * NZ + slot_z
    docs = jnp.where(pairs >= 0, pairs // IPD, -1)
    tok = token_doc.reshape(GROUPS, 1, GROUP)
    attended, grad_queries, dkv = attention(rel, dst, docs, tok, queries, grad_out, pieces)

    dkv = dkv.reshape(NX, NZ, LAT, WIDE)
    dkv = lax.all_to_all(dkv, "x", 0, 0, tiled=True)
    dkv = jnp.sum(dkv.astype(jnp.float32), axis=0).astype(jnp.bfloat16)
    dkv = lax.all_to_all(dkv, "z", 0, 0, tiled=True)
    dkv = jnp.sum(dkv.astype(jnp.float32), axis=0).astype(jnp.bfloat16)

    term = lax.dot_general(dkv, weight, NT_DIMS, preferred_element_type=jnp.float32)
    term = term.astype(jnp.bfloat16).reshape(NT, LAT // NT, VIS)
    term = lax.all_to_all(term, ("y", "core"), 0, 0, tiled=True)
    term = jnp.sum(term.astype(jnp.float32), axis=0).astype(jnp.bfloat16)
    term = lax.all_gather(term, ("y", "core"), axis=0, tiled=True)
    return attended, grad_queries, term[None]


def solution(mesh):
    fine = Mesh(mesh.devices.reshape(NZ, NX, NT // 2, 2), ("z", "x", "y", "core"))
    seq, tensor = ("z", "x"), ("y", "core")
    in_specs = (
        P(seq, tensor),
        P(seq, None, None),
        P(seq, tensor),
        P(seq, tensor),
        P(seq, tensor),
        P(seq, None),
        P(),
        P(seq),
    )
    out_specs = (P(seq, tensor), P(seq, tensor), P(seq, None, None))
    return jax.shard_map(local, mesh=fine, in_specs=in_specs, out_specs=out_specs, check_vma=False)
```

time: 826 us -> 226 us (0.27)
  waiting for transfers between devices: 632 us -> 67.1 us
  local copies, waits for them, and re-layouts: 52.1 us -> 1.01 us
  matrix products: 40.1 us -> 2.16 us
  starting transfers between devices: 0.38 us -> 35.4 us
  Pallas kernels: 0 us -> 12.3 us
  blocking collectives: 82.4 us -> 91.7 us
    reduce_scatter x2 -> x0, waiting for transfers between devices: 405 us -> none  [the longest x1 221 us: local(): lax.psum_scatter(value_flat.astype(jnp.bfloat16), 'seq', scatter_dimensio...]
    psum x1 -> x0, waiting for transfers between devices: 109 us -> none  [local(): latent_total = lax.psum(latent_term.astype(jnp.bfloat16), 'tensor')]
    all_gather x2 -> x1, waiting for transfers between devices: 117 us -> 45.3 us  [local(): weight = lax.all_gather(weight, 'z', axis=0, tiled=True)]
    all_to_all x0 -> x3, blocking collectives: none -> 65.7 us  [the longest x1 25.3 us: local(): dkv = lax.all_to_all(dkv, 'x', 0, 0, tiled=True)]
    all_gather x2, blocking collectives: 82.4 us -> 26 us  [the longest x1 14.9 us: local(): term = lax.all_gather(term, ('y', 'core'), axis=0, tiled=True)]
    dot_general x12 -> x2, matrix products: 40.1 us -> 2.16 us  [the longest x1 1.66 us: local(): jnp.dot(latents[0], weight, preferred_element_type=jnp.float32)]
    ppermute x0 -> x10, starting transfers between devices: none -> 35.3 us  [from_offset(): lax.ppermute(value, axis, [(i, (i - step) % size) for i in range(size)])]
    ppermute x0 -> x10, waiting for transfers between devices: none -> 21.8 us  [from_offset(): lax.ppermute(value, axis, [(i, (i - step) % size) for i in range(size)])]
  transfers between devices with their start and end apart: 5 -> 11, of which waited for: 5 -> 6; matrix products, arithmetic and copies ran while one was open for 6% -> 0% of each run, Pallas kernels for 0% -> 0%
where the time goes in v1:
time: 226 us
  blocking collectives  91.7 us (41%)
  waiting for transfers between devices  67.1 us (30%)
  starting transfers between devices  35.4 us (16%)
  between operations  14.3 us (6%)
  Pallas kernels  12.3 us (5%)
    all_gather x1, waiting for transfers between devices, local(): weight = lax.all_gather(weight, 'z', axis=0, tiled=True)  45.3 us
    ppermute x10, starting transfers between devices, from_offset(): lax.ppermute(value, axis, [(i, (i - step) % size) for i in range(size)])  35.3 us
    all_to_all x1, blocking collectives, local(): dkv = lax.all_to_all(dkv, 'x', 0, 0, tiled=True)  25.3 us
    all_to_all x1, blocking collectives, local(): term = lax.all_to_all(term, ('y', 'core'), 0, 0, tiled=True)  21.9 us
    ppermute x10, waiting for transfers between devices, from_offset(): lax.ppermute(value, axis, [(i, (i - step) % size) for i in range(size)])  21.8 us
    all_to_all x1, blocking collectives, local(): dkv = lax.all_to_all(dkv, 'z', 0, 0, tiled=True)  18.5 us
    all_gather x1, blocking collectives, local(): term = lax.all_gather(term, ('y', 'core'), axis=0, tiled=True)  14.9 us
    pallas_call x1, Pallas kernels, attention(): pl.pallas_call(attention_kernel, grid_spec=pltpu.PrefetchScalarGridSpec(n...  12.3 us
  transfers between devices with their start and end apart: 11, of which 6 were waited for; matrix products, arithmetic and copies ran while one was open for 0% of the time, Pallas kernels for 0%

profile of v1, /device:TPU:1, one launch (start us, length us, event | category | flops | bytes accessed | tf_op | source)
XLA Modules:
  0.0 225.5 jit_solution(18302015309181064125)
XLA Ops:
  7.2 0.0 copy-start
  7.2 0.0 copy-start.5
  7.2 0.0 all-gather.3.cloned.1.call-start
  7.2 0.8 pad_maximum_fusion
  8.0 11.1 %all_gather.9 = bf16[160,512]{1,0:T(8,128)(2,1)} all-gather(bf16[40,512]{1,0:T(8,128)(2,1)S(1)} %pad_maximum_fusion), channel_id=1, replica_groups=mesh['z'=8,'x'=4,'y'=8,'core'=2] {'x'}, dimensions={0}, use_global_device_ids=true | all-gather | bytes 204800 | tf_op jit(solution)/shard_map/all_gather | solution.py:127
  19.1 0.0 all-gather.3.cloned.1.call-update
  19.1 0.0 copy-start.6
  19.1 0.0 copy-start.1
  19.1 0.0 copy-start.2
  19.2 0.0 copy-start.3
  19.2 45.3 %all-gather.3.cloned.1.call-done = bf16[1280,512]{1,0:T(8,128)(2,1)} async-done(((bf16[160,512]{1,0:T(8,128)(2,1)}), bf16[1280,512]{1,0:T(8,128)(2,1)}) %all-gather.3.cloned.1.call-update) | async-done | bytes 1310736 | tf_op jit(solution)/shard_map/all_gather | solution.py:128
  64.4 0.0 copy-done
  64.4 1.7 bitcast_dynamic-update-slice_fusion
  66.1 3.5 %collective-permute-start = (bf16[64,512]{1,0:T(8,128)(2,1)S(1)}, bf16[64,512]{1,0:T(8,128)(2,1)S(1)}, u32[]{:S(2)}, u32[]{:S(2)}) collective-permute-start(bf16[64,512]{1,0:T(8,128)(2,1)S(1)} %bitcast.31), channel_id=1, source_target_pairs={{0,448},{64,0},{128,64},{192,128},{256,192},{320,256},{384,320},{4... | collective-permute-start | bytes 196616 | tf_op jit(solution)/shard_map/ppermute | solution.py:120
  69.6 0.0 copy-done.5
  69.6 0.1 copy.27
  69.7 2.2 collective-permute-start.5
  71.9 4.8 %collective-permute-start.4 = (bf16[64,512]{1,0:T(8,128)(2,1)S(1)}, bf16[64,512]{1,0:T(8,128)(2,1)S(1)}, u32[]{:S(2)}, u32[]{:S(2)}) collective-permute-start(bf16[64,512]{1,0:T(8,128)(2,1)S(1)} %bitcast.33), channel_id=1, source_target_pairs={{0,192},{64,256},{128,320},{192,384},{256,448},{320,0},{384,64},{4... | collective-permute-start | bytes 196616 | tf_op jit(solution)/shard_map/ppermute | solution.py:120
  76.7 4.0 %collective-permute-start.3 = (bf16[64,512]{1,0:T(8,128)(2,1)S(1)}, bf16[64,512]{1,0:T(8,128)(2,1)S(1)}, u32[]{:S(2)}, u32[]{:S(2)}) collective-permute-start(bf16[64,512]{1,0:T(8,128)(2,1)S(1)} %bitcast.34), channel_id=1, source_target_pairs={{0,256},{64,320},{128,384},{192,448},{256,0},{320,64},{384,128},{4... | collective-permute-start | bytes 196616 | tf_op jit(solution)/shard_map/ppermute | solution.py:120
  80.7 4.1 %collective-permute-start.2 = (bf16[64,512]{1,0:T(8,128)(2,1)S(1)}, bf16[64,512]{1,0:T(8,128)(2,1)S(1)}, u32[]{:S(2)}, u32[]{:S(2)}) collective-permute-start(bf16[64,512]{1,0:T(8,128)(2,1)S(1)} %bitcast.35), channel_id=1, source_target_pairs={{0,320},{64,384},{128,448},{192,0},{256,64},{320,128},{384,192},{4... | collective-permute-start | bytes 196616 | tf_op jit(solution)/shard_map/ppermute | solution.py:120
  84.8 0.0 collective-permute-done
  84.8 5.1 %collective-permute-start.1 = (bf16[64,512]{1,0:T(8,128)(2,1)S(1)}, bf16[64,512]{1,0:T(8,128)(2,1)S(1)}, u32[]{:S(2)}, u32[]{:S(2)}) collective-permute-start(bf16[64,512]{1,0:T(8,128)(2,1)S(1)} %bitcast.36), channel_id=1, source_target_pairs={{0,384},{64,448},{128,0},{192,64},{256,128},{320,192},{384,256},{4... | collective-permute-start | bytes 196616 | tf_op jit(solution)/shard_map/ppermute | solution.py:120
  89.9 3.0 %collective-permute-done.1 = bf16[64,512]{1,0:T(8,128)(2,1)S(1)} collective-permute-done((bf16[64,512]{1,0:T(8,128)(2,1)S(1)}, bf16[64,512]{1,0:T(8,128)(2,1)S(1)}, u32[]{:S(2)}, u32[]{:S(2)}) %collective-permute-start.1) | collective-permute-done | bytes 65568 | tf_op jit(solution)/shard_map/ppermute | solution.py:120
  92.9 1.9 collective-permute-start.6
  94.9 0.0 collective-permute-done.2
  94.9 0.0 collective-permute-done.3
  94.9 0.0 collective-permute-done.4
  95.0 0.0 collective-permute-done.5
  95.0 4.2 %collective-permute-done.6 = bf16[64,512]{1,0:T(8,128)(2,1)S(1)} collective-permute-done((bf16[64,512]{1,0:T(8,128)(2,1)S(1)}, bf16[64,512]{1,0:T(8,128)(2,1)S(1)}, u32[]{:S(2)}, u32[]{:S(2)}) %collective-permute-start.6) | collective-permute-done | bytes 65568 | tf_op jit(solution)/shard_map/ppermute | solution.py:120
  99.2 2.3 %collective-permute-start.9 = (bf16[8,64,512]{2,1,0:T(8,128)(2,1)S(1)}, bf16[8,64,512]{2,1,0:T(8,128)(2,1)S(1)}, u32[]{:S(2)}, u32[]{:S(2)}) collective-permute-start(bf16[8,64,512]{2,1,0:T(8,128)(2,1)S(1)} %bitcast_dynamic-update-slice_fusion.1.p0), channel_id=1, source_target_pairs={{0,16},{16,32},{32,48},{48,0},{1,17},{17,33},{33,49},{49,1},{2,18}... | collective-permute-start | bytes 1572872 | tf_op jit(solution)/shard_map/ppermute | solution.py:120
  101.5 4.3 %collective-permute-start.8 = (bf16[8,64,512]{2,1,0:T(8,128)(2,1)S(1)}, bf16[8,64,512]{2,1,0:T(8,128)(2,1)}, u32[]{:S(2)}, u32[]{:S(2)}) collective-permute-start(bf16[8,64,512]{2,1,0:T(8,128)(2,1)S(1)} %bitcast_dynamic-update-slice_fusion.1.p0), channel_id=1, source_target_pairs={{0,32},{16,48},{32,0},{48,16},{1,33},{17,49},{33,1},{49,17},{2,34}... | collective-permute-start | bytes 1572872 | tf_op jit(solution)/shard_map/ppermute | solution.py:120
  105.8 3.1 %collective-permute-start.7 = (bf16[8,64,512]{2,1,0:T(8,128)(2,1)S(1)}, bf16[8,64,512]{2,1,0:T(8,128)(2,1)}, u32[]{:S(2)}, u32[]{:S(2)}) collective-permute-start(bf16[8,64,512]{2,1,0:T(8,128)(2,1)S(1)} %bitcast_dynamic-update-slice_fusion.1.p0), channel_id=1, source_target_pairs={{0,48},{16,0},{32,16},{48,32},{1,49},{17,1},{33,17},{49,33},{2,50}... | collective-permute-start | bytes 1572872 | tf_op jit(solution)/shard_map/ppermute | solution.py:120
  108.9 0.0 copy-done.6
  108.9 0.2 select_reduce_fusion
  109.2 0.1 copy.23
  109.3 1.0 collective-permute-done.9.p3
  110.3 8.2 %collective-permute-done.8.p2 = bf16[8,64,512]{2,1,0:T(8,128)(2,1)} collective-permute-done((bf16[8,64,512]{2,1,0:T(8,128)(2,1)S(1)}, bf16[8,64,512]{2,1,0:T(8,128)(2,1)}, u32[]{:S(2)}, u32[]{:S(2)}) %collective-permute-start.8) | collective-permute-done | bytes 524320 | tf_op jit(solution)/shard_map/ppermute | solution.py:120
  118.5 5.4 %collective-permute-done.7.p1 = bf16[8,64,512]{2,1,0:T(8,128)(2,1)} collective-permute-done((bf16[8,64,512]{2,1,0:T(8,128)(2,1)S(1)}, bf16[8,64,512]{2,1,0:T(8,128)(2,1)}, u32[]{:S(2)}, u32[]{:S(2)}) %collective-permute-start.7) | collective-permute-done | bytes 524320 | tf_op jit(solution)/shard_map/ppermute | solution.py:120
  123.9 0.0 copy-done.1
  123.9 0.0 copy-done.2
  123.9 0.0 copy-done.3
  123.9 12.3 %shard_map.103 = (bf16[2048,256]{1,0:T(8,128)(2,1)}, bf16[2048,256]{1,0:T(8,128)(2,1)}, bf16[32,64,512]{2,1,0:T(8,128)(2,1)S(1)}) custom-call(s32[8,4]{1,0:T(8,128)S(1)} %get-tuple-element.10.rel_ref, s32[8,4]{1,0:T(8,128)S(1)} %get-tuple-element.9.abs_ref, s32[8,4]{1,0:T(8,128)S(1)} %fusion.6.doc_ref, s32[8,1,256]{2,1,0:T(1,128)S(1)} %bitcast.30, ...), custom_call_target="tpu_custom_call" | custom-call | flops 1610612736 | bytes 9437184 | tf_op jit(solution)/shard_map/pallas_call | solution.py:84
  136.3 25.3 %all_to_all.15 = bf16[4,8,64,512]{3,2,1,0:T(8,128)(2,1)S(1)} all-to-all(bf16[4,8,64,512]{3,2,1,0:T(8,128)(2,1)S(1)} %bitcast.29), channel_id=1, replica_groups=mesh['z'=8,'x'=4,'y'=8,'core'=2] {'x'}, dimensions={0} | all-to-all | bytes 4194304 | tf_op jit(solution)/shard_map/all_to_all | solution.py:143
  161.5 0.4 reduce_sum.46
  161.9 0.0 copy-start.4
  161.9 18.5 %all_to_all.16 = bf16[8,64,512]{2,1,0:T(8,128)(2,1)S(1)} all-to-all(bf16[8,64,512]{2,1,0:T(8,128)(2,1)S(1)} %reduce_sum.46), channel_id=1, replica_groups=mesh['z'=8,'x'=4,'y'=8,'core'=2] {'z'}, dimensions={0} | all-to-all | bytes 1048576 | tf_op jit(solution)/shard_map/all_to_all | solution.py:145
  180.4 0.1 reduce_sum.47
  180.5 0.0 copy-done.4
  180.5 0.5 convolution_convert_fusion
  181.1 21.9 %all_to_all.17 = bf16[16,4,1280]{2,1,0:T(4,128)(2,1)S(1)} all-to-all(bf16[16,4,1280]{2,1,0:T(4,128)(2,1)S(1)} %reshape.18), channel_id=1, replica_groups=mesh['z'=8,'x'=4,'y'=8,'core'=2] {'y','core'}, dimensions={0} | all-to-all | bytes 327680 | tf_op jit(solution)/shard_map/all_to_all | solution.py:150
  203.0 0.1 reduce_sum.48
  203.1 14.9 %all-gather = bf16[16,4,1280]{2,1,0:T(4,128)(2,1)S(1)} all-gather(bf16[1,4,1280]{2,1,0:T(4,128)(2,1)S(1)} %bitcast.38), channel_id=1, replica_groups=mesh['z'=8,'x'=4,'y'=8,'core'=2] {'y','core'}, dimensions={0}, use_global_device_ids=true | all-gather | bytes 174080 | tf_op jit(solution)/shard_map/all_gather | solution.py:152
  218.0 0.7 broadcast_in_dim.17
  (10 shorter events, 0.1 us)
Async XLA Ops:
  7.2 57.3 %copy-start = (bf16[1,64,1280]{2,1,0:T(8,128)(2,1)S(1)}, bf16[1,64,1280]{2,1,0:T(8,128)(2,1)}, u32[]{:S(2)}) copy-start(bf16[1,64,1280]{2,1,0:T(8,128)(2,1)} %param.9) | copy-start | bytes 491524
  7.2 62.4 %copy-start.5 = (s32[8,4]{0,1:T(4,128)S(1)}, s32[8,4]{0,1:T(4,128)}, u32[]{:S(2)}) copy-start(s32[8,4]{0,1:T(4,128)} %param.13) | copy-start | bytes 388
  7.2 57.2 %all-gather.3.cloned.1.call-start = ((), (), s32[]{:S(2)}) async-start(), calls=%async_computation.3 | async-start | bytes 1474560 | tf_op jit(solution)/shard_map/all_gather | solution.py:128
  19.1 89.8 %copy-start.6 = (s32[32]{0:T(128)S(1)}, s32[32]{0:T(128)}, u32[]{:S(2)}) copy-start(s32[32]{0:T(128)} %param.14) | copy-start | bytes 388
  19.1 104.8 %copy-start.1 = (bf16[2048,256]{1,0:T(8,128)(2,1)S(1)}, bf16[2048,256]{1,0:T(8,128)(2,1)}, u32[]{:S(2)}) copy-start(bf16[2048,256]{1,0:T(8,128)(2,1)} %q_ref.1) | copy-start | bytes 3145732
  19.1 104.8 %copy-start.2 = (bf16[2048,256]{1,0:T(8,128)(2,1)S(1)}, bf16[2048,256]{1,0:T(8,128)(2,1)}, u32[]{:S(2)}) copy-start(bf16[2048,256]{1,0:T(8,128)(2,1)} %g_ref.1) | copy-start | bytes 3145732
  19.2 104.8 %copy-start.3 = (s32[2048]{0:T(1024)S(1)}, s32[2048]{0:T(1024)}, u32[]{:S(2)}) copy-start(s32[2048]{0:T(1024)} %param.15) | copy-start | bytes 24580
  66.1 18.7 %collective-permute-start = (bf16[64,512]{1,0:T(8,128)(2,1)S(1)}, bf16[64,512]{1,0:T(8,128)(2,1)S(1)}, u32[]{:S(2)}, u32[]{:S(2)}) collective-permute-start(bf16[64,512]{1,0:T(8,128)(2,1)S(1)} %bitcast.31), channel_id=1, source_target_pairs={{0,448},{64,0},{128,64},{192,128},{256,192},{320,256},{384,320},{4... | collective-permute-start | bytes 196616 | tf_op jit(solution)/shard_map/ppermute | solution.py:120
  69.7 25.2 %collective-permute-start.5 = (bf16[64,512]{1,0:T(8,128)(2,1)S(1)}, bf16[64,512]{1,0:T(8,128)(2,1)S(1)}, u32[]{:S(2)}, u32[]{:S(2)}) collective-permute-start(bf16[64,512]{1,0:T(8,128)(2,1)S(1)} %bitcast.32), channel_id=1, source_target_pairs={{0,128},{64,192},{128,256},{192,320},{256,384},{320,448},{384,0},{... | collective-permute-start | bytes 196616 | tf_op jit(solution)/shard_map/ppermute | solution.py:120
  71.9 23.0 %collective-permute-start.4 = (bf16[64,512]{1,0:T(8,128)(2,1)S(1)}, bf16[64,512]{1,0:T(8,128)(2,1)S(1)}, u32[]{:S(2)}, u32[]{:S(2)}) collective-permute-start(bf16[64,512]{1,0:T(8,128)(2,1)S(1)} %bitcast.33), channel_id=1, source_target_pairs={{0,192},{64,256},{128,320},{192,384},{256,448},{320,0},{384,64},{4... | collective-permute-start | bytes 196616 | tf_op jit(solution)/shard_map/ppermute | solution.py:120
  76.7 18.3 %collective-permute-start.3 = (bf16[64,512]{1,0:T(8,128)(2,1)S(1)}, bf16[64,512]{1,0:T(8,128)(2,1)S(1)}, u32[]{:S(2)}, u32[]{:S(2)}) collective-permute-start(bf16[64,512]{1,0:T(8,128)(2,1)S(1)} %bitcast.34), channel_id=1, source_target_pairs={{0,256},{64,320},{128,384},{192,448},{256,0},{320,64},{384,128},{4... | collective-permute-start | bytes 196616 | tf_op jit(solution)/shard_map/ppermute | solution.py:120
  80.7 14.2 %collective-permute-start.2 = (bf16[64,512]{1,0:T(8,128)(2,1)S(1)}, bf16[64,512]{1,0:T(8,128)(2,1)S(1)}, u32[]{:S(2)}, u32[]{:S(2)}) collective-permute-start(bf16[64,512]{1,0:T(8,128)(2,1)S(1)} %bitcast.35), channel_id=1, source_target_pairs={{0,320},{64,384},{128,448},{192,0},{256,64},{320,128},{384,192},{4... | collective-permute-start | bytes 196616 | tf_op jit(solution)/shard_map/ppermute | solution.py:120
  84.8 8.1 %collective-permute-start.1 = (bf16[64,512]{1,0:T(8,128)(2,1)S(1)}, bf16[64,512]{1,0:T(8,128)(2,1)S(1)}, u32[]{:S(2)}, u32[]{:S(2)}) collective-permute-start(bf16[64,512]{1,0:T(8,128)(2,1)S(1)} %bitcast.36), channel_id=1, source_target_pairs={{0,384},{64,448},{128,0},{192,64},{256,128},{320,192},{384,256},{4... | collective-permute-start | bytes 196616 | tf_op jit(solution)/shard_map/ppermute | solution.py:120
  92.9 6.2 %collective-permute-start.6 = (bf16[64,512]{1,0:T(8,128)(2,1)S(1)}, bf16[64,512]{1,0:T(8,128)(2,1)S(1)}, u32[]{:S(2)}, u32[]{:S(2)}) collective-permute-start(bf16[64,512]{1,0:T(8,128)(2,1)S(1)} %bitcast.37), channel_id=1, source_target_pairs={{0,64},{64,128},{128,192},{192,256},{256,320},{320,384},{384,448},... | collective-permute-start | bytes 196616 | tf_op jit(solution)/shard_map/ppermute | solution.py:120
  99.2 11.1 %collective-permute-start.9 = (bf16[8,64,512]{2,1,0:T(8,128)(2,1)S(1)}, bf16[8,64,512]{2,1,0:T(8,128)(2,1)S(1)}, u32[]{:S(2)}, u32[]{:S(2)}) collective-permute-start(bf16[8,64,512]{2,1,0:T(8,128)(2,1)S(1)} %bitcast_dynamic-update-slice_fusion.1.p0), channel_id=1, source_target_pairs={{0,16},{16,32},{32,48},{48,0},{1,17},{17,33},{33,49},{49,1},{2,18}... | collective-permute-start | bytes 1572872 | tf_op jit(solution)/shard_map/ppermute | solution.py:120
  101.5 17.0 %collective-permute-start.8 = (bf16[8,64,512]{2,1,0:T(8,128)(2,1)S(1)}, bf16[8,64,512]{2,1,0:T(8,128)(2,1)}, u32[]{:S(2)}, u32[]{:S(2)}) collective-permute-start(bf16[8,64,512]{2,1,0:T(8,128)(2,1)S(1)} %bitcast_dynamic-update-slice_fusion.1.p0), channel_id=1, source_target_pairs={{0,32},{16,48},{32,0},{48,16},{1,33},{17,49},{33,1},{49,17},{2,34}... | collective-permute-start | bytes 1572872 | tf_op jit(solution)/shard_map/ppermute | solution.py:120
  105.8 18.1 %collective-permute-start.7 = (bf16[8,64,512]{2,1,0:T(8,128)(2,1)S(1)}, bf16[8,64,512]{2,1,0:T(8,128)(2,1)}, u32[]{:S(2)}, u32[]{:S(2)}) collective-permute-start(bf16[8,64,512]{2,1,0:T(8,128)(2,1)S(1)} %bitcast_dynamic-update-slice_fusion.1.p0), channel_id=1, source_target_pairs={{0,48},{16,0},{32,16},{48,32},{1,49},{17,1},{33,17},{49,33},{2,50}... | collective-permute-start | bytes 1572872 | tf_op jit(solution)/shard_map/ppermute | solution.py:120
  161.9 18.6 %copy-start.4 = (bf16[1280,512]{1,0:T(8,128)(2,1)S(1)}, bf16[1280,512]{1,0:T(8,128)(2,1)}, u32[]{:S(2)}) copy-start(bf16[1280,512]{1,0:T(8,128)(2,1)} %all-gather.3.cloned.1.call-done) | copy-start | bytes 3932164
Sparse Core Ops, SparseCore 0:
  19.2 45.1 all-gather.2

commit v2 on v1

--- a/solution.py
+++ b/solution.py
@@ -14,7 +14,8 @@
 IPD = 4
 NX = 4
 NZ = 8
-NT = 16
+NY = 8
+WROWS = 40
 COLS = 256
 WIDE = 2 * COLS
 VIS = 1280
@@ -122,18 +123,25 @@
 
 def local(queries, latents, key_weight, value_weight, grad_out, pairs, image_slot, token_doc):
     x = lax.axis_index("x")
-    z = lax.axis_index("z")
+    core = lax.axis_index("core")
+
     weight = jnp.concatenate([key_weight, value_weight], axis=1)
-    weight = lax.all_gather(weight, "x", axis=0, tiled=True)
-    weight = lax.all_gather(weight, "z", axis=0, tiled=True)
-    kv = jnp.dot(latents[0], weight, preferred_element_type=jnp.float32).astype(jnp.bfloat16)
-    column = jnp.stack([kv] + [from_offset(kv, "z", NZ, i) for i in range(1, NZ)])
+    part = lax.all_gather(weight, "z", axis=0, tiled=True)
+    own = latents[0].reshape(LAT, NZ, NX, WROWS).transpose(2, 0, 1, 3).reshape(NX, LAT, NZ * WROWS)
+    row = lax.all_to_all(own, "x", 0, 0, tiled=True)
+    kv = jnp.einsum("jlv,vc->jlc", row, part, preferred_element_type=jnp.float32)
+    kv = lax.all_to_all(kv.astype(jnp.bfloat16), "x", 0, 0, tiled=True)
+    kv = jnp.sum(kv.astype(jnp.float32), axis=0).astype(jnp.bfloat16)
+    column = lax.all_gather(kv, "z", axis=0)
     pieces = [column] + [from_offset(column, "x", NX, i) for i in range(1, NX)]
+
+    whole = lax.all_gather(part, "x", axis=0)
+    whole = whole.reshape(NX, NZ, WROWS, WIDE).transpose(1, 0, 2, 3).reshape(VIS, WIDE)
 
     matches = pairs[..., None] == jnp.arange(IMAGES, dtype=jnp.int32)
     slot = jnp.sum(jnp.where(matches, image_slot, 0), axis=-1).astype(jnp.int32)
     slot_z, slot_x = slot // NX, slot % NX
-    rel = (slot_x - x) % NX * NZ + (slot_z - z) % NZ
+    rel = (slot_x - x) % NX * NZ + slot_z
     dst = slot_x * NZ + slot_z
     docs = jnp.where(pairs >= 0, pairs // IPD, -1)
     tok = token_doc.reshape(GROUPS, 1, GROUP)
@@ -145,16 +153,23 @@
     dkv = lax.all_to_all(dkv, "z", 0, 0, tiled=True)
     dkv = jnp.sum(dkv.astype(jnp.float32), axis=0).astype(jnp.bfloat16)
 
-    term = lax.dot_general(dkv, weight, NT_DIMS, preferred_element_type=jnp.float32)
-    term = term.astype(jnp.bfloat16).reshape(NT, LAT // NT, VIS)
-    term = lax.all_to_all(term, ("y", "core"), 0, 0, tiled=True)
+    term = lax.dot_general(dkv, whole, NT_DIMS, preferred_element_type=jnp.float32)
+    half = LAT // 2
+    keep = jnp.where(core == 0, term[:half], term[half:])
+    give = jnp.where(core == 0, term[half:], term[:half]).astype(jnp.bfloat16)
+    term = keep + from_offset(give, "core", 2, 1).astype(jnp.float32)
+    term = term.astype(jnp.bfloat16).reshape(NY, half // NY, VIS)
+    term = lax.all_to_all(term, "y", 0, 0, tiled=True)
     term = jnp.sum(term.astype(jnp.float32), axis=0).astype(jnp.bfloat16)
-    term = lax.all_gather(term, ("y", "core"), axis=0, tiled=True)
-    return attended, grad_queries, term[None]
+    term = lax.all_gather(term, "y", axis=0, tiled=True)
+    other = from_offset(term, "core", 2, 1)
+    first = jnp.where(core == 0, term, other)
+    second = jnp.where(core == 0, other, term)
+    return attended, grad_queries, jnp.concatenate([first, second])[None]
 
 
 def solution(mesh):
-    fine = Mesh(mesh.devices.reshape(NZ, NX, NT // 2, 2), ("z", "x", "y", "core"))
+    fine = Mesh(mesh.devices.reshape(NZ, NX, NY, 2), ("z", "x", "y", "core"))
     seq, tensor = ("z", "x"), ("y", "core")
     in_specs = (
         P(seq, tensor),

time: 226 us -> 213 us (0.942)
  blocking collectives: 91.7 us -> 77.7 us
  waiting for transfers between devices: 67.1 us -> 59.6 us
  starting transfers between devices: 35.4 us -> 39.8 us
  local copies, waits for them, and re-layouts: 1.01 us -> 3.71 us
    all_to_all x3 -> x1, blocking collectives: 65.7 us -> 13.9 us  [local(): term = lax.all_to_all(term, 'y', 0, 0, tiled=True)]
    all_gather x2 -> x3, blocking collectives: 26 us -> 63.8 us  [the longest x1 25.7 us: local(): part = lax.all_gather(weight, 'z', axis=0, tiled=True)]
    all_gather x1, waiting for transfers between devices: 45.3 us -> 25.1 us  [local(): whole = lax.all_gather(part, 'x', axis=0)]
    all_to_all x0 -> x4, waiting for transfers between devices: none -> 20 us  [the longest x1 14.6 us: local(): dkv = lax.all_to_all(dkv, 'x', 0, 0, tiled=True)]
    all_to_all x0 -> x4, starting transfers between devices: none -> 16.6 us  [the longest x1 4.84 us: local(): row = lax.all_to_all(own, 'x', 0, 0, tiled=True)]
    ppermute x10 -> x5, starting transfers between devices: 35.3 us -> 23.1 us  [from_offset(): lax.ppermute(value, axis, [(i, (i - step) % size) for i in range(size)])]
    ppermute x10 -> x5, waiting for transfers between devices: 21.8 us -> 13.8 us  [from_offset(): lax.ppermute(value, axis, [(i, (i - step) % size) for i in range(size)])]
  transfers between devices with their start and end apart: 11 -> 10, of which waited for: 6 -> 8; matrix products, arithmetic and copies ran while one was open for 0% -> 1% of each run, Pallas kernels for 0% -> 0%
where the time goes in v2:
time: 213 us; the launch traced here: 212 us
  blocking collectives  77.7 us (36%)
  waiting for transfers between devices  59.6 us (28%)
  starting transfers between devices  39.8 us (19%)
  between operations  14.2 us (7%)
  Pallas kernels  13.1 us (6%)
  local copies, waits for them, and re-layouts  3.71 us (2%)
  other arithmetic  2.44 us (1%)
    all_gather x1, blocking collectives, local(): part = lax.all_gather(weight, 'z', axis=0, tiled=True)  25.7 us
    all_gather x1, waiting for transfers between devices, local(): whole = lax.all_gather(part, 'x', axis=0)  25.1 us
    ppermute x5, starting transfers between devices, from_offset(): lax.ppermute(value, axis, [(i, (i - step) % size) for i in range(size)])  23.1 us
    all_gather x1, blocking collectives, local(): column = lax.all_gather(kv, 'z', axis=0)  19.7 us
    all_gather x1, blocking collectives, local(): term = lax.all_gather(term, 'y', axis=0, tiled=True)  18.5 us
    all_to_all x1, waiting for transfers between devices, local(): dkv = lax.all_to_all(dkv, 'x', 0, 0, tiled=True)  14.6 us
    all_to_all x1, blocking collectives, local(): term = lax.all_to_all(term, 'y', 0, 0, tiled=True)  13.9 us
    ppermute x5, waiting for transfers between devices, from_offset(): lax.ppermute(value, axis, [(i, (i - step) % size) for i in range(size)])  13.8 us
  transfers between devices with their start and end apart: 10, of which 8 were waited for; matrix products, arithmetic and copies ran while one was open for 1% of the time, Pallas kernels for 0%

profile of v2, /device:TPU:1, one launch (start us, length us, event | category | flops | bytes accessed | tf_op | source)
XLA Modules:
  0.0 212.2 jit_solution(6025817735325321420)
XLA Ops:
  7.2 0.0 copy-start.5
  7.2 0.0 copy-start.4
  7.2 1.1 copy.47
  8.4 0.0 copy-start.6
  8.4 0.8 copy.49
  9.2 4.8 %all-to-all-start = ((bf16[4,64,320]{2,1,0:T(8,128)(2,1)}), bf16[4,64,320]{2,1,0:T(8,128)(2,1)S(1)}, u32[]{:S(2)}, u32[]{:S(2)}) async-start(bf16[4,64,320]{2,1,0:T(8,128)(2,1)} %copy.49), calls=%async_computation | async-start | bytes 393216 | tf_op jit(solution)/shard_map/all_to_all | solution.py:131
  14.1 0.0 copy-done.5
  14.1 0.0 copy-done.4
  14.1 0.0 copy-start.7
  14.1 0.0 copy-start
  14.1 0.0 copy-start.1
  14.1 0.0 copy-start.2
  14.1 25.7 %all_gather.18 = bf16[320,512]{1,0:T(8,128)(2,1)S(1)} all-gather(bf16[40,512]{1,0:T(8,128)(2,1)S(1)} %pad_maximum_fusion), channel_id=1, replica_groups=mesh['z'=8,'x'=4,'y'=8,'core'=2] {'z'}, dimensions={0}, use_global_device_ids=true | all-gather | bytes 368640 | tf_op jit(solution)/shard_map/all_gather | solution.py:129
  39.8 0.0 copy-start.3
  39.8 0.0 all-to-all-done
  39.8 1.0 fusion
  40.8 3.9 %all-to-all-start.1 = ((bf16[4,64,512]{2,1,0:T(8,128)(2,1)}), bf16[4,64,512]{2,1,0:T(8,128)(2,1)S(1)}, u32[]{:S(2)}, u32[]{:S(2)}) async-start(bf16[4,64,512]{2,1,0:T(8,128)(2,1)} %fusion), calls=%async_computation.1 | async-start | bytes 524288 | tf_op jit(solution)/shard_map/all_to_all | solution.py:133
  44.7 0.0 copy-done.6
  44.7 0.1 copy.42
  44.8 5.4 %all-to-all-done.1 = bf16[4,64,512]{2,1,0:T(8,128)(2,1)S(1)} async-done(((bf16[4,64,512]{2,1,0:T(8,128)(2,1)}), bf16[4,64,512]{2,1,0:T(8,128)(2,1)S(1)}, u32[]{:S(2)}, u32[]{:S(2)}) %all-to-all-start.1) | async-done | bytes 262176 | tf_op jit(solution)/shard_map/all_to_all | solution.py:133
  50.3 19.7 %all-gather = bf16[512,512]{1,0:T(8,128)(2,1)S(1)} all-gather(bf16[64,512]{1,0:T(8,128)(2,1)S(1)} %reduce_sum.58), channel_id=2, replica_groups=mesh['z'=8,'x'=4,'y'=8,'core'=2] {'z'}, dimensions={0}, use_global_device_ids=true | all-gather | bytes 589824 | tf_op jit(solution)/shard_map/all_gather | solution.py:135
  69.9 3.0 %collective-permute-start = (bf16[8,64,512]{2,1,0:T(8,128)(2,1)S(1)}, bf16[8,64,512]{2,1,0:T(8,128)(2,1)S(1)}, u32[]{:S(2)}, u32[]{:S(2)}) collective-permute-start(bf16[8,64,512]{2,1,0:T(8,128)(2,1)S(1)} %bitcast.22), channel_id=1, source_target_pairs={{0,48},{16,0},{32,16},{48,32},{1,49},{17,1},{33,17},{49,33},{2,50}... | collective-permute-start | bytes 1572872 | tf_op jit(solution)/shard_map/ppermute | solution.py:121
  72.9 2.9 %collective-permute-start.1 = (bf16[8,64,512]{2,1,0:T(8,128)(2,1)S(1)}, bf16[8,64,512]{2,1,0:T(8,128)(2,1)}, u32[]{:S(2)}, u32[]{:S(2)}) collective-permute-start(bf16[8,64,512]{2,1,0:T(8,128)(2,1)S(1)} %bitcast.23), channel_id=1, source_target_pairs={{0,32},{16,48},{32,0},{48,16},{1,33},{17,49},{33,1},{49,17},{2,34}... | collective-permute-start | bytes 1572872 | tf_op jit(solution)/shard_map/ppermute | solution.py:121
  75.8 1.9 collective-permute-start.2
  77.8 0.0 copy-done.7
  77.8 0.2 select_reduce_fusion
  78.0 0.1 copy.38
  78.1 1.7 collective-permute-done.p1
  79.9 4.7 %collective-permute-done.1.p2 = bf16[8,64,512]{2,1,0:T(8,128)(2,1)} collective-permute-done((bf16[8,64,512]{2,1,0:T(8,128)(2,1)S(1)}, bf16[8,64,512]{2,1,0:T(8,128)(2,1)}, u32[]{:S(2)}, u32[]{:S(2)}) %collective-permute-start.1) | collective-permute-done | bytes 524320 | tf_op jit(solution)/shard_map/ppermute | solution.py:121
  84.6 5.5 %collective-permute-done.2.p3 = bf16[8,64,512]{2,1,0:T(8,128)(2,1)} collective-permute-done((bf16[8,64,512]{2,1,0:T(8,128)(2,1)S(1)}, bf16[8,64,512]{2,1,0:T(8,128)(2,1)}, u32[]{:S(2)}, u32[]{:S(2)}) %collective-permute-start.2) | collective-permute-done | bytes 524320 | tf_op jit(solution)/shard_map/ppermute | solution.py:121
  90.1 0.0 copy-done
  90.1 0.0 copy-done.1
  90.1 0.0 copy-done.2
  90.1 13.1 %shard_map.103 = (bf16[2048,256]{1,0:T(8,128)(2,1)}, bf16[2048,256]{1,0:T(8,128)(2,1)}, bf16[32,64,512]{2,1,0:T(8,128)(2,1)}) custom-call(s32[8,4]{1,0:T(8,128)S(1)} %get-tuple-element.12.rel_ref, s32[8,4]{1,0:T(8,128)S(1)} %get-tuple-element.11.abs_ref, s32[8,4]{1,0:T(8,128)S(1)} %fusion.6.doc_ref, s32[8,1,256]{2,1,0:T(1,128)S(1)} %bitcast.26, ...), custom_call_target="tpu_custom_call" | custom-call | flops 1610612736 | bytes 9437184 | tf_op jit(solution)/shard_map/pallas_call | solution.py:85
  103.2 0.0 copy-done.3
  103.2 3.6 %all-to-all-start.2 = ((bf16[4,8,64,512]{3,2,1,0:T(8,128)(2,1)}), bf16[4,8,64,512]{3,2,1,0:T(8,128)(2,1)S(1)}, u32[]{:S(2)}, u32[]{:S(2)}) async-start(bf16[4,8,64,512]{3,2,1,0:T(8,128)(2,1)} %bitcast.7), calls=%async_computation.2 | async-start | bytes 4194304 | tf_op jit(solution)/shard_map/all_to_all | solution.py:151
  106.8 0.0 all-gather.5.cloned.1.call-start
  106.9 0.7 all-gather.5.cloned.1.call-update
  107.6 14.6 %all-to-all-done.2 = bf16[4,8,64,512]{3,2,1,0:T(8,128)(2,1)S(1)} async-done(((bf16[4,8,64,512]{3,2,1,0:T(8,128)(2,1)}), bf16[4,8,64,512]{3,2,1,0:T(8,128)(2,1)S(1)}, u32[]{:S(2)}, u32[]{:S(2)}) %all-to-all-start.2) | async-done | bytes 2097184 | tf_op jit(solution)/shard_map/all_to_all | solution.py:151
  122.2 1.3 reduce_sum.59
  123.4 4.3 %all-to-all-start.3 = ((bf16[8,64,512]{2,1,0:T(8,128)(2,1)}), bf16[8,64,512]{2,1,0:T(8,128)(2,1)S(1)}, u32[]{:S(2)}, u32[]{:S(2)}) async-start(bf16[8,64,512]{2,1,0:T(8,128)(2,1)} %reduce_sum.59), calls=%async_computation.3 | async-start | bytes 1048576 | tf_op jit(solution)/shard_map/all_to_all | solution.py:153
  127.7 25.1 %all-gather.5.cloned.1.call-done = bf16[1280,512]{1,0:T(8,128)(2,1)} async-done(((bf16[320,512]{1,0:T(8,128)(2,1)}), bf16[1280,512]{1,0:T(8,128)(2,1)}) %all-gather.5.cloned.1.call-update) | async-done | bytes 1310736 | tf_op jit(solution)/shard_map/all_gather | solution.py:138
  152.9 1.4 copy.50
  154.3 0.0 all-to-all-done.3
  154.3 0.1 reduce_sum.60
  154.4 0.5 fusion.10
  155.0 5.4 %collective-permute-start.3 = (bf16[32,1280]{1,0:T(8,128)(2,1)S(1)}, bf16[32,1280]{1,0:T(8,128)(2,1)S(1)}, u32[]{:S(2)}, u32[]{:S(2)}) collective-permute-start(bf16[32,1280]{1,0:T(8,128)(2,1)S(1)} %select_convert_fusion), channel_id=1, source_target_pairs={{0,1},{1,0},{2,3},{3,2},{4,5},{5,4},{6,7},{7,6},{8,9},{9,8},{10,11... | collective-permute-start | bytes 245768 | tf_op jit(solution)/shard_map/ppermute | solution.py:121
  160.3 0.9 collective-permute-done.3
  161.3 13.9 %all_to_all.25 = bf16[8,4,1280]{2,1,0:T(4,128)(2,1)S(1)} all-to-all(bf16[8,4,1280]{2,1,0:T(4,128)(2,1)S(1)} %reshape.30), channel_id=1, replica_groups=mesh['z'=8,'x'=4,'y'=8,'core'=2] {'y'}, dimensions={0} | all-to-all | bytes 163840 | tf_op jit(solution)/shard_map/all_to_all | solution.py:162
  175.3 18.5 %all-gather.2 = bf16[8,4,1280]{2,1,0:T(4,128)(2,1)S(1)} all-gather(bf16[1,4,1280]{2,1,0:T(4,128)(2,1)S(1)} %bitcast.31), channel_id=1, replica_groups=mesh['z'=8,'x'=4,'y'=8,'core'=2] {'y'}, dimensions={0}, use_global_device_ids=true | all-gather | bytes 92160 | tf_op jit(solution)/shard_map/all_gather | solution.py:164
  193.8 10.0 %collective-permute-start.4 = (bf16[32,1280]{1,0:T(8,128)(2,1)S(1)}, bf16[32,1280]{1,0:T(8,128)(2,1)S(1)}, u32[]{:S(2)}, u32[]{:S(2)}) collective-permute-start(bf16[32,1280]{1,0:T(8,128)(2,1)S(1)} %reshape.35), channel_id=1, source_target_pairs={{0,1},{1,0},{2,3},{3,2},{4,5},{5,4},{6,7},{7,6},{8,9},{9,8},{10,11... | collective-permute-start | bytes 245768 | tf_op jit(solution)/shard_map/ppermute | solution.py:121
  203.7 0.9 collective-permute-done.4
  204.6 0.7 maximum_bitcast_fusion
  (11 shorter events, 0.3 us)
Async XLA Ops:
  7.2 6.9 %copy-start.5 = (bf16[40,256]{1,0:T(8,128)(2,1)S(1)}, bf16[40,256]{1,0:T(8,128)(2,1)}, u32[]{:S(2)}) copy-start(bf16[40,256]{1,0:T(8,128)(2,1)} %param.10) | copy-start | bytes 61444
  7.2 6.9 %copy-start.4 = (bf16[40,256]{1,0:T(8,128)(2,1)S(1)}, bf16[40,256]{1,0:T(8,128)(2,1)}, u32[]{:S(2)}) copy-start(bf16[40,256]{1,0:T(8,128)(2,1)} %param.11) | copy-start | bytes 61444
  8.4 36.3 %copy-start.6 = (s32[8,4]{0,1:T(4,128)S(1)}, s32[8,4]{0,1:T(4,128)}, u32[]{:S(2)}) copy-start(s32[8,4]{0,1:T(4,128)} %param.13) | copy-start | bytes 388
  9.2 30.6 %all-to-all-start = ((bf16[4,64,320]{2,1,0:T(8,128)(2,1)}), bf16[4,64,320]{2,1,0:T(8,128)(2,1)S(1)}, u32[]{:S(2)}, u32[]{:S(2)}) async-start(bf16[4,64,320]{2,1,0:T(8,128)(2,1)} %copy.49), calls=%async_computation | async-start | bytes 393216 | tf_op jit(solution)/shard_map/all_to_all | solution.py:131
  14.1 63.7 %copy-start.7 = (s32[32]{0:T(128)S(1)}, s32[32]{0:T(128)}, u32[]{:S(2)}) copy-start(s32[32]{0:T(128)} %param.14) | copy-start | bytes 388
  14.1 76.0 %copy-start = (bf16[2048,256]{1,0:T(8,128)(2,1)S(1)}, bf16[2048,256]{1,0:T(8,128)(2,1)}, u32[]{:S(2)}) copy-start(bf16[2048,256]{1,0:T(8,128)(2,1)} %q_ref.1) | copy-start | bytes 3145732
  14.1 76.0 %copy-start.1 = (bf16[2048,256]{1,0:T(8,128)(2,1)S(1)}, bf16[2048,256]{1,0:T(8,128)(2,1)}, u32[]{:S(2)}) copy-start(bf16[2048,256]{1,0:T(8,128)(2,1)} %g_ref.1) | copy-start | bytes 3145732
  14.1 76.0 %copy-start.2 = (s32[2048]{0:T(1024)S(1)}, s32[2048]{0:T(1024)}, u32[]{:S(2)}) copy-start(s32[2048]{0:T(1024)} %param.15) | copy-start | bytes 24580
  39.8 63.4 %copy-start.3 = (bf16[320,512]{1,0:T(8,128)(2,1)}, bf16[320,512]{1,0:T(8,128)(2,1)S(1)}, u32[]{:S(2)}) copy-start(bf16[320,512]{1,0:T(8,128)(2,1)S(1)} %all_gather.18) | copy-start | bytes 983044
  40.8 9.4 %all-to-all-start.1 = ((bf16[4,64,512]{2,1,0:T(8,128)(2,1)}), bf16[4,64,512]{2,1,0:T(8,128)(2,1)S(1)}, u32[]{:S(2)}, u32[]{:S(2)}) async-start(bf16[4,64,512]{2,1,0:T(8,128)(2,1)} %fusion), calls=%async_computation.1 | async-start | bytes 524288 | tf_op jit(solution)/shard_map/all_to_all | solution.py:133
  69.9 9.9 %collective-permute-start = (bf16[8,64,512]{2,1,0:T(8,128)(2,1)S(1)}, bf16[8,64,512]{2,1,0:T(8,128)(2,1)S(1)}, u32[]{:S(2)}, u32[]{:S(2)}) collective-permute-start(bf16[8,64,512]{2,1,0:T(8,128)(2,1)S(1)} %bitcast.22), channel_id=1, source_target_pairs={{0,48},{16,0},{32,16},{48,32},{1,49},{17,1},{33,17},{49,33},{2,50}... | collective-permute-start | bytes 1572872 | tf_op jit(solution)/shard_map/ppermute | solution.py:121
  72.9 11.6 %collective-permute-start.1 = (bf16[8,64,512]{2,1,0:T(8,128)(2,1)S(1)}, bf16[8,64,512]{2,1,0:T(8,128)(2,1)}, u32[]{:S(2)}, u32[]{:S(2)}) collective-permute-start(bf16[8,64,512]{2,1,0:T(8,128)(2,1)S(1)} %bitcast.23), channel_id=1, source_target_pairs={{0,32},{16,48},{32,0},{48,16},{1,33},{17,49},{33,1},{49,17},{2,34}... | collective-permute-start | bytes 1572872 | tf_op jit(solution)/shard_map/ppermute | solution.py:121
  75.8 14.2 %collective-permute-start.2 = (bf16[8,64,512]{2,1,0:T(8,128)(2,1)S(1)}, bf16[8,64,512]{2,1,0:T(8,128)(2,1)}, u32[]{:S(2)}, u32[]{:S(2)}) collective-permute-start(bf16[8,64,512]{2,1,0:T(8,128)(2,1)S(1)} %bitcast.24), channel_id=1, source_target_pairs={{0,16},{16,32},{32,48},{48,0},{1,17},{17,33},{33,49},{49,1},{2,18}... | collective-permute-start | bytes 1572872 | tf_op jit(solution)/shard_map/ppermute | solution.py:121
  103.2 19.0 %all-to-all-start.2 = ((bf16[4,8,64,512]{3,2,1,0:T(8,128)(2,1)}), bf16[4,8,64,512]{3,2,1,0:T(8,128)(2,1)S(1)}, u32[]{:S(2)}, u32[]{:S(2)}) async-start(bf16[4,8,64,512]{3,2,1,0:T(8,128)(2,1)} %bitcast.7), calls=%async_computation.2 | async-start | bytes 4194304 | tf_op jit(solution)/shard_map/all_to_all | solution.py:151
  106.8 46.0 %all-gather.5.cloned.1.call-start = ((), (), s32[]{:S(2)}) async-start(), calls=%async_computation.5 | async-start | bytes 1638400 | tf_op jit(solution)/shard_map/all_gather | solution.py:138
  123.4 30.9 %all-to-all-start.3 = ((bf16[8,64,512]{2,1,0:T(8,128)(2,1)}), bf16[8,64,512]{2,1,0:T(8,128)(2,1)S(1)}, u32[]{:S(2)}, u32[]{:S(2)}) async-start(bf16[8,64,512]{2,1,0:T(8,128)(2,1)} %reduce_sum.59), calls=%async_computation.3 | async-start | bytes 1048576 | tf_op jit(solution)/shard_map/all_to_all | solution.py:153
  155.0 6.3 %collective-permute-start.3 = (bf16[32,1280]{1,0:T(8,128)(2,1)S(1)}, bf16[32,1280]{1,0:T(8,128)(2,1)S(1)}, u32[]{:S(2)}, u32[]{:S(2)}) collective-permute-start(bf16[32,1280]{1,0:T(8,128)(2,1)S(1)} %select_convert_fusion), channel_id=1, source_target_pairs={{0,1},{1,0},{2,3},{3,2},{4,5},{5,4},{6,7},{7,6},{8,9},{9,8},{10,11... | collective-permute-start | bytes 245768 | tf_op jit(solution)/shard_map/ppermute | solution.py:121
  193.8 10.9 %collective-permute-start.4 = (bf16[32,1280]{1,0:T(8,128)(2,1)S(1)}, bf16[32,1280]{1,0:T(8,128)(2,1)S(1)}, u32[]{:S(2)}, u32[]{:S(2)}) collective-permute-start(bf16[32,1280]{1,0:T(8,128)(2,1)S(1)} %reshape.35), channel_id=1, source_target_pairs={{0,1},{1,0},{2,3},{3,2},{4,5},{5,4},{6,7},{7,6},{8,9},{9,8},{10,11... | collective-permute-start | bytes 245768 | tf_op jit(solution)/shard_map/ppermute | solution.py:121
Sparse Core Ops, SparseCore 0:
  109.8 43.0 all-gather.4

commit v3 on v2

--- a/solution.py
+++ b/solution.py
@@ -121,48 +121,47 @@
     return lax.ppermute(value, axis, [(i, (i - step) % size) for i in range(size)])
 
 
+def from_partner(value, axis, size, bit):
+    return lax.ppermute(value, axis, [(i, i ^ bit) for i in range(size)])
+
+
+def gather(value, axis, size):
+    copies = jnp.broadcast_to(value[None], (size,) + value.shape)
+    return lax.all_to_all(copies, axis, 0, 0, tiled=True)
+
+
 def local(queries, latents, key_weight, value_weight, grad_out, pairs, image_slot, token_doc):
     x = lax.axis_index("x")
     core = lax.axis_index("core")
 
     weight = jnp.concatenate([key_weight, value_weight], axis=1)
-    part = lax.all_gather(weight, "z", axis=0, tiled=True)
-    own = latents[0].reshape(LAT, NZ, NX, WROWS).transpose(2, 0, 1, 3).reshape(NX, LAT, NZ * WROWS)
-    row = lax.all_to_all(own, "x", 0, 0, tiled=True)
-    kv = jnp.einsum("jlv,vc->jlc", row, part, preferred_element_type=jnp.float32)
-    kv = lax.all_to_all(kv.astype(jnp.bfloat16), "x", 0, 0, tiled=True)
-    kv = jnp.sum(kv.astype(jnp.float32), axis=0).astype(jnp.bfloat16)
-    column = lax.all_gather(kv, "z", axis=0)
+    weight = gather(weight, ("z", "x"), NZ * NX).reshape(VIS, WIDE)
+    kv = jnp.dot(latents[0], weight, preferred_element_type=jnp.float32).astype(jnp.bfloat16)
+    column = gather(kv, "z", NZ)
     pieces = [column] + [from_offset(column, "x", NX, i) for i in range(1, NX)]
-
-    whole = lax.all_gather(part, "x", axis=0)
-    whole = whole.reshape(NX, NZ, WROWS, WIDE).transpose(1, 0, 2, 3).reshape(VIS, WIDE)
 
     matches = pairs[..., None] == jnp.arange(IMAGES, dtype=jnp.int32)
     slot = jnp.sum(jnp.where(matches, image_slot, 0), axis=-1).astype(jnp.int32)
     slot_z, slot_x = slot // NX, slot % NX
     rel = (slot_x - x) % NX * NZ + slot_z
-    dst = slot_x * NZ + slot_z
     docs = jnp.where(pairs >= 0, pairs // IPD, -1)
     tok = token_doc.reshape(GROUPS, 1, GROUP)
-    attended, grad_queries, dkv = attention(rel, dst, docs, tok, queries, grad_out, pieces)
+    attended, grad_queries, dkv = attention(rel, slot, docs, tok, queries, grad_out, pieces)
 
-    dkv = dkv.reshape(NX, NZ, LAT, WIDE)
-    dkv = lax.all_to_all(dkv, "x", 0, 0, tiled=True)
-    dkv = jnp.sum(dkv.astype(jnp.float32), axis=0).astype(jnp.bfloat16)
-    dkv = lax.all_to_all(dkv, "z", 0, 0, tiled=True)
+    dkv = lax.all_to_all(dkv, ("z", "x"), 0, 0, tiled=True)
     dkv = jnp.sum(dkv.astype(jnp.float32), axis=0).astype(jnp.bfloat16)
 
-    term = lax.dot_general(dkv, whole, NT_DIMS, preferred_element_type=jnp.float32)
+    term = lax.dot_general(dkv, weight, NT_DIMS, preferred_element_type=jnp.float32)
     half = LAT // 2
     keep = jnp.where(core == 0, term[:half], term[half:])
-    give = jnp.where(core == 0, term[half:], term[:half]).astype(jnp.bfloat16)
-    term = keep + from_offset(give, "core", 2, 1).astype(jnp.float32)
-    term = term.astype(jnp.bfloat16).reshape(NY, half // NY, VIS)
-    term = lax.all_to_all(term, "y", 0, 0, tiled=True)
-    term = jnp.sum(term.astype(jnp.float32), axis=0).astype(jnp.bfloat16)
-    term = lax.all_gather(term, "y", axis=0, tiled=True)
-    other = from_offset(term, "core", 2, 1)
+    give = jnp.where(core == 0, term[half:], term[:half])
+    term = keep + from_partner(give, "core", 2, 1)
+    term = term + from_partner(term, "y", NY, 1)
+    for bit in (2, 4):
+        low = term.astype(jnp.bfloat16)
+        term = low.astype(jnp.float32) + from_partner(low, "y", NY, bit).astype(jnp.float32)
+    term = term.astype(jnp.bfloat16)
+    other = from_partner(term, "core", 2, 1)
     first = jnp.where(core == 0, term, other)
     second = jnp.where(core == 0, other, term)
     return attended, grad_queries, jnp.concatenate([first, second])[None]

time: 213 us -> 206 us (0.967)
  waiting for transfers between devices: 59.6 us -> 78.4 us
  between operations: 14.2 us -> 0.84 us
  blocking collectives: 77.7 us -> 65.3 us
  local copies, waits for them, and re-layouts: 3.71 us -> 0.34 us
  starting transfers between devices: 39.8 us -> 42.6 us
    all_gather x3 -> x0, blocking collectives: 63.8 us -> none  [the longest x1 25.7 us: local(): part = lax.all_gather(weight, 'z', axis=0, tiled=True)]
    all_to_all x1 -> x2, blocking collectives: 13.9 us -> 65.3 us  [gather(): return lax.all_to_all(copies, axis, 0, 0, tiled=True)]
    all_to_all x4 -> x1, waiting for transfers between devices: 20 us -> 48.3 us  [local(): dkv = lax.all_to_all(dkv, ('z', 'x'), 0, 0, tiled=True)]
    ppermute x0 -> x5, starting transfers between devices: none -> 26.5 us  [from_partner(): return lax.ppermute(value, axis, [(i, i ^ bit) for i in range(size)])]
    all_gather x1 -> x0, waiting for transfers between devices: 25.1 us -> none  [local(): whole = lax.all_gather(part, 'x', axis=0)]
    ppermute x5 -> x3, starting transfers between devices: 23.1 us -> 8.79 us  [from_offset(): lax.ppermute(value, axis, [(i, (i - step) % size) for i in range(size)])]
    ppermute x0 -> x5, waiting for transfers between devices: none -> 9.66 us  [from_partner(): return lax.ppermute(value, axis, [(i, i ^ bit) for i in range(size)])]
    all_to_all x4 -> x1, starting transfers between devices: 16.6 us -> 7.3 us  [local(): dkv = lax.all_to_all(dkv, ('z', 'x'), 0, 0, tiled=True)]
  transfers between devices with their start and end apart: 10 -> 9, of which waited for: 8 -> 9; matrix products, arithmetic and copies ran while one was open for 1% -> 0% of each run, Pallas kernels for 0% -> 0%
where the time goes in v3:
time: 206 us; the launch traced here: 205 us
  waiting for transfers between devices  78.4 us (38%)
  blocking collectives  65.3 us (32%)
  starting transfers between devices  42.6 us (21%)
  Pallas kernels  13.1 us (6%)
  other arithmetic  3.73 us (2%)
    all_to_all x2, blocking collectives, gather(): return lax.all_to_all(copies, axis, 0, 0, tiled=True)  65.3 us
    all_to_all x1, waiting for transfers between devices, local(): dkv = lax.all_to_all(dkv, ('z', 'x'), 0, 0, tiled=True)  48.3 us
    ppermute x5, starting transfers between devices, from_partner(): return lax.ppermute(value, axis, [(i, i ^ bit) for i in range(size)])  26.5 us
    ppermute x3, waiting for transfers between devices, from_offset(): lax.ppermute(value, axis, [(i, (i - step) % size) for i in range(size)])  20.4 us
    pallas_call x1, Pallas kernels, attention(): pl.pallas_call(attention_kernel, grid_spec=pltpu.PrefetchScalarGridSpec(n...  13.1 us
    ppermute x5, waiting for transfers between devices, from_partner(): return lax.ppermute(value, axis, [(i, i ^ bit) for i in range(size)])  9.66 us
    ppermute x3, starting transfers between devices, from_offset(): lax.ppermute(value, axis, [(i, (i - step) % size) for i in range(size)])  8.79 us
    all_to_all x1, starting transfers between devices, local(): dkv = lax.all_to_all(dkv, ('z', 'x'), 0, 0, tiled=True)  7.3 us
  transfers between devices with their start and end apart: 9, of which 9 were waited for; matrix products, arithmetic and copies ran while one was open for 0% of the time, Pallas kernels for 0%

profile of v3, /device:TPU:1, one launch (start us, length us, event | category | flops | bytes accessed | tf_op | source)
XLA Modules:
  0.0 205.1 jit_solution(15816599508888703487)
XLA Ops:
  0.6 0.0 copy-start
  0.6 0.8 pad_maximum_fusion
  1.4 0.1 broadcast_in_dim.29
  1.5 47.3 %all_to_all.15 = bf16[32,40,512]{2,1,0:T(8,128)(2,1)S(1)} all-to-all(bf16[32,40,512]{2,1,0:T(8,128)(2,1)S(1)} %broadcast_in_dim.29), channel_id=1, replica_groups=mesh['z'=8,'x'=4,'y'=8,'core'=2] {'z','x'}, dimensions={0} | all-to-all | bytes 2621440 | tf_op jit(solution)/shard_map/all_to_all | solution.py:130
  48.8 0.0 copy-start.4
  48.8 0.0 copy-done
  48.9 0.0 copy-start.6
  48.9 0.0 copy-start.7
  48.9 0.0 copy-start.1
  48.9 0.0 copy-start.2
  48.9 0.0 copy-start.3
  48.9 0.3 fusion
  49.3 18.0 %all_to_all.16.p0 = bf16[8,64,512]{2,1,0:T(8,128)(2,1)S(1)} all-to-all(bf16[8,64,512]{2,1,0:T(8,128)(2,1)S(1)} %broadcast_in_dim.30), channel_id=1, replica_groups=mesh['z'=8,'x'=4,'y'=8,'core'=2] {'z'}, dimensions={0} | all-to-all | bytes 1048576 | tf_op jit(solution)/shard_map/all_to_all | solution.py:130
  67.3 0.0 copy-done.4
  67.3 2.0 collective-permute-start.2
  69.3 3.9 %collective-permute-start.1 = (bf16[8,64,512]{2,1,0:T(8,128)(2,1)S(1)}, bf16[8,64,512]{2,1,0:T(8,128)(2,1)}, u32[]{:S(2)}, u32[]{:S(2)}) collective-permute-start(bf16[8,64,512]{2,1,0:T(8,128)(2,1)S(1)} %all_to_all.16.p0), channel_id=1, source_target_pairs={{0,32},{16,48},{32,0},{48,16},{1,33},{17,49},{33,1},{49,17},{2,34}... | collective-permute-start | bytes 1572872 | tf_op jit(solution)/shard_map/ppermute | solution.py:121
  73.3 2.8 %collective-permute-start = (bf16[8,64,512]{2,1,0:T(8,128)(2,1)S(1)}, bf16[8,64,512]{2,1,0:T(8,128)(2,1)}, u32[]{:S(2)}, u32[]{:S(2)}) collective-permute-start(bf16[8,64,512]{2,1,0:T(8,128)(2,1)S(1)} %all_to_all.16.p0), channel_id=1, source_target_pairs={{0,48},{16,0},{32,16},{48,32},{1,49},{17,1},{33,17},{49,33},{2,50}... | collective-permute-start | bytes 1572872 | tf_op jit(solution)/shard_map/ppermute | solution.py:121
  76.1 0.0 copy-done.6
  76.1 0.1 copy.21
  76.2 0.0 copy-done.7
  76.2 0.2 select_reduce_fusion
  76.4 0.1 copy.17.abs_ref
  76.5 4.0 %collective-permute-done.2.p3 = bf16[8,64,512]{2,1,0:T(8,128)(2,1)S(1)} collective-permute-done((bf16[8,64,512]{2,1,0:T(8,128)(2,1)S(1)}, bf16[8,64,512]{2,1,0:T(8,128)(2,1)S(1)}, u32[]{:S(2)}, u32[]{:S(2)}) %collective-permute-start.2) | collective-permute-done | bytes 524320 | tf_op jit(solution)/shard_map/ppermute | solution.py:121
  80.5 10.5 %collective-permute-done.1.p2 = bf16[8,64,512]{2,1,0:T(8,128)(2,1)} collective-permute-done((bf16[8,64,512]{2,1,0:T(8,128)(2,1)S(1)}, bf16[8,64,512]{2,1,0:T(8,128)(2,1)}, u32[]{:S(2)}, u32[]{:S(2)}) %collective-permute-start.1) | collective-permute-done | bytes 524320 | tf_op jit(solution)/shard_map/ppermute | solution.py:121
  90.9 6.0 %collective-permute-done.p1 = bf16[8,64,512]{2,1,0:T(8,128)(2,1)} collective-permute-done((bf16[8,64,512]{2,1,0:T(8,128)(2,1)S(1)}, bf16[8,64,512]{2,1,0:T(8,128)(2,1)}, u32[]{:S(2)}, u32[]{:S(2)}) %collective-permute-start) | collective-permute-done | bytes 524320 | tf_op jit(solution)/shard_map/ppermute | solution.py:121
  96.9 0.0 copy-done.1
  96.9 0.0 copy-done.2
  96.9 0.0 copy-done.3
  96.9 13.1 %shard_map.103 = (bf16[2048,256]{1,0:T(8,128)(2,1)}, bf16[2048,256]{1,0:T(8,128)(2,1)}, bf16[32,64,512]{2,1,0:T(8,128)(2,1)}) custom-call(s32[8,4]{1,0:T(8,128)S(1)} %get-tuple-element.11.rel_ref, s32[8,4]{1,0:T(8,128)S(1)} %copy.17.abs_ref, s32[8,4]{1,0:T(8,128)S(1)} %get-tuple-element.12.doc_ref, s32[8,1,256]{2,1,0:T(1,128)S(1)} %bitcast.12, ...), custom_call_target="tpu_custom_call" | custom-call | flops 1610612736 | bytes 9437184 | tf_op jit(solution)/shard_map/pallas_call | solution.py:85
  110.0 7.3 %all-to-all-start.2 = ((bf16[32,64,512]{2,1,0:T(8,128)(2,1)}), bf16[32,64,512]{2,1,0:T(8,128)(2,1)}, u32[]{:S(2)}, u32[]{:S(2)}) async-start(bf16[32,64,512]{2,1,0:T(8,128)(2,1)} %get-tuple-element.8), calls=%async_computation.2 | async-start | bytes 4194304 | tf_op jit(solution)/shard_map/all_to_all | solution.py:151
  117.3 0.0 copy-start.5
  117.3 48.3 %all-to-all-done.2 = bf16[32,64,512]{2,1,0:T(8,128)(2,1)} async-done(((bf16[32,64,512]{2,1,0:T(8,128)(2,1)}), bf16[32,64,512]{2,1,0:T(8,128)(2,1)}, u32[]{:S(2)}, u32[]{:S(2)}) %all-to-all-start.2) | async-done | bytes 2097184 | tf_op jit(solution)/shard_map/all_to_all | solution.py:151
  165.7 1.9 reduce_sum.22
  167.5 0.0 copy-done.5
  167.6 0.5 fusion.11
  168.1 4.7 %collective-permute-start.3 = (f32[32,1280]{1,0:T(8,128)S(1)}, f32[32,1280]{1,0:T(8,128)S(1)}, u32[]{:S(2)}, u32[]{:S(2)}) collective-permute-start(f32[32,1280]{1,0:T(8,128)S(1)} %slice_select_fusion), channel_id=1, source_target_pairs={{0,1},{1,0},{2,3},{3,2},{4,5},{5,4},{6,7},{7,6},{8,9},{9,8},{10,11... | collective-permute-start | bytes 491528 | tf_op jit(solution)/shard_map/ppermute | solution.py:125
  172.8 1.0 collective-permute-done.3
  173.8 3.2 %collective-permute-start.4 = (f32[32,1280]{1,0:T(8,128)S(1)}, f32[32,1280]{1,0:T(8,128)S(1)}, u32[]{:S(2)}, u32[]{:S(2)}) collective-permute-start(f32[32,1280]{1,0:T(8,128)S(1)} %select_add_fusion), channel_id=1, source_target_pairs={{0,2},{2,0},{4,6},{6,4},{8,10},{10,8},{12,14},{14,12},{1,3},{3,1},... | collective-permute-start | bytes 491528 | tf_op jit(solution)/shard_map/ppermute | solution.py:125
  177.0 4.1 %collective-permute-done.4 = f32[32,1280]{1,0:T(8,128)S(1)} collective-permute-done((f32[32,1280]{1,0:T(8,128)S(1)}, f32[32,1280]{1,0:T(8,128)S(1)}, u32[]{:S(2)}, u32[]{:S(2)}) %collective-permute-start.4) | collective-permute-done | bytes 163872 | tf_op jit(solution)/shard_map/ppermute | solution.py:125
  181.1 4.2 %collective-permute-start.5 = (bf16[32,1280]{1,0:T(8,128)(2,1)S(1)}, bf16[32,1280]{1,0:T(8,128)(2,1)S(1)}, u32[]{:S(2)}, u32[]{:S(2)}) collective-permute-start(bf16[32,1280]{1,0:T(8,128)(2,1)S(1)} %add_convert_fusion.2), channel_id=1, source_target_pairs={{0,4},{2,6},{4,0},{6,2},{8,12},{10,14},{12,8},{14,10},{1,5},{3,7},... | collective-permute-start | bytes 245768 | tf_op jit(solution)/shard_map/ppermute | solution.py:125
  185.4 1.8 collective-permute-done.5
  187.2 8.7 %collective-permute-start.6 = (bf16[32,1280]{1,0:T(8,128)(2,1)S(1)}, bf16[32,1280]{1,0:T(8,128)(2,1)S(1)}, u32[]{:S(2)}, u32[]{:S(2)}) collective-permute-start(bf16[32,1280]{1,0:T(8,128)(2,1)S(1)} %add_convert_fusion.1), channel_id=1, source_target_pairs={{0,8},{2,10},{4,12},{6,14},{8,0},{10,2},{12,4},{14,6},{1,9},{3,11}... | collective-permute-start | bytes 245768 | tf_op jit(solution)/shard_map/ppermute | solution.py:125
  195.9 1.8 collective-permute-done.6
  197.8 5.8 %collective-permute-start.7 = (bf16[32,1280]{1,0:T(8,128)(2,1)S(1)}, bf16[32,1280]{1,0:T(8,128)(2,1)S(1)}, u32[]{:S(2)}, u32[]{:S(2)}) collective-permute-start(bf16[32,1280]{1,0:T(8,128)(2,1)S(1)} %add_convert_fusion), channel_id=1, source_target_pairs={{0,1},{1,0},{2,3},{3,2},{4,5},{5,4},{6,7},{7,6},{8,9},{9,8},{10,11... | collective-permute-start | bytes 245768 | tf_op jit(solution)/shard_map/ppermute | solution.py:125
  203.5 0.9 collective-permute-done.7
  204.5 0.7 maximum_bitcast_fusion
  (8 shorter events, 0.2 us)
Async XLA Ops:
  0.6 48.2 %copy-start = (bf16[1,64,1280]{2,1,0:T(8,128)(2,1)S(1)}, bf16[1,64,1280]{2,1,0:T(8,128)(2,1)}, u32[]{:S(2)}) copy-start(bf16[1,64,1280]{2,1,0:T(8,128)(2,1)} %param.9) | copy-start | bytes 491524
  48.8 18.4 %copy-start.4 = (bf16[32,40,512]{2,1,0:T(8,128)(2,1)}, bf16[32,40,512]{2,1,0:T(8,128)(2,1)S(1)}, u32[]{:S(2)}) copy-start(bf16[32,40,512]{2,1,0:T(8,128)(2,1)S(1)} %all_to_all.15) | copy-start | bytes 3932164
  48.9 27.2 %copy-start.6 = (s32[8,4]{0,1:T(4,128)S(1)}, s32[8,4]{0,1:T(4,128)}, u32[]{:S(2)}) copy-start(s32[8,4]{0,1:T(4,128)} %param.13) | copy-start | bytes 388
  48.9 27.3 %copy-start.7 = (s32[32]{0:T(128)S(1)}, s32[32]{0:T(128)}, u32[]{:S(2)}) copy-start(s32[32]{0:T(128)} %param.14) | copy-start | bytes 388
  48.9 48.0 %copy-start.1 = (bf16[2048,256]{1,0:T(8,128)(2,1)S(1)}, bf16[2048,256]{1,0:T(8,128)(2,1)}, u32[]{:S(2)}) copy-start(bf16[2048,256]{1,0:T(8,128)(2,1)} %q_ref.1) | copy-start | bytes 3145732
  48.9 48.0 %copy-start.2 = (bf16[2048,256]{1,0:T(8,128)(2,1)S(1)}, bf16[2048,256]{1,0:T(8,128)(2,1)}, u32[]{:S(2)}) copy-start(bf16[2048,256]{1,0:T(8,128)(2,1)} %g_ref.1) | copy-start | bytes 3145732
  48.9 48.0 %copy-start.3 = (s32[2048]{0:T(1024)S(1)}, s32[2048]{0:T(1024)}, u32[]{:S(2)}) copy-start(s32[2048]{0:T(1024)} %param.15) | copy-start | bytes 24580
  67.3 13.2 %collective-permute-start.2 = (bf16[8,64,512]{2,1,0:T(8,128)(2,1)S(1)}, bf16[8,64,512]{2,1,0:T(8,128)(2,1)S(1)}, u32[]{:S(2)}, u32[]{:S(2)}) collective-permute-start(bf16[8,64,512]{2,1,0:T(8,128)(2,1)S(1)} %all_to_all.16.p0), channel_id=1, source_target_pairs={{0,16},{16,32},{32,48},{48,0},{1,17},{17,33},{33,49},{49,1},{2,18}... | collective-permute-start | bytes 1572872 | tf_op jit(solution)/shard_map/ppermute | solution.py:121
  69.3 21.6 %collective-permute-start.1 = (bf16[8,64,512]{2,1,0:T(8,128)(2,1)S(1)}, bf16[8,64,512]{2,1,0:T(8,128)(2,1)}, u32[]{:S(2)}, u32[]{:S(2)}) collective-permute-start(bf16[8,64,512]{2,1,0:T(8,128)(2,1)S(1)} %all_to_all.16.p0), channel_id=1, source_target_pairs={{0,32},{16,48},{32,0},{48,16},{1,33},{17,49},{33,1},{49,17},{2,34}... | collective-permute-start | bytes 1572872 | tf_op jit(solution)/shard_map/ppermute | solution.py:121
  73.3 23.6 %collective-permute-start = (bf16[8,64,512]{2,1,0:T(8,128)(2,1)S(1)}, bf16[8,64,512]{2,1,0:T(8,128)(2,1)}, u32[]{:S(2)}, u32[]{:S(2)}) collective-permute-start(bf16[8,64,512]{2,1,0:T(8,128)(2,1)S(1)} %all_to_all.16.p0), channel_id=1, source_target_pairs={{0,48},{16,0},{32,16},{48,32},{1,49},{17,1},{33,17},{49,33},{2,50}... | collective-permute-start | bytes 1572872 | tf_op jit(solution)/shard_map/ppermute | solution.py:121
  110.0 55.7 %all-to-all-start.2 = ((bf16[32,64,512]{2,1,0:T(8,128)(2,1)}), bf16[32,64,512]{2,1,0:T(8,128)(2,1)}, u32[]{:S(2)}, u32[]{:S(2)}) async-start(bf16[32,64,512]{2,1,0:T(8,128)(2,1)} %get-tuple-element.8), calls=%async_computation.2 | async-start | bytes 4194304 | tf_op jit(solution)/shard_map/all_to_all | solution.py:151
  117.3 50.2 %copy-start.5 = (bf16[32,40,512]{2,1,0:T(8,128)(2,1)S(1)}, bf16[32,40,512]{2,1,0:T(8,128)(2,1)}, u32[]{:S(2)}) copy-start(bf16[32,40,512]{2,1,0:T(8,128)(2,1)} %copy-done.4) | copy-start | bytes 3932164
  168.1 5.7 %collective-permute-start.3 = (f32[32,1280]{1,0:T(8,128)S(1)}, f32[32,1280]{1,0:T(8,128)S(1)}, u32[]{:S(2)}, u32[]{:S(2)}) collective-permute-start(f32[32,1280]{1,0:T(8,128)S(1)} %slice_select_fusion), channel_id=1, source_target_pairs={{0,1},{1,0},{2,3},{3,2},{4,5},{5,4},{6,7},{7,6},{8,9},{9,8},{10,11... | collective-permute-start | bytes 491528 | tf_op jit(solution)/shard_map/ppermute | solution.py:125
  173.8 7.3 %collective-permute-start.4 = (f32[32,1280]{1,0:T(8,128)S(1)}, f32[32,1280]{1,0:T(8,128)S(1)}, u32[]{:S(2)}, u32[]{:S(2)}) collective-permute-start(f32[32,1280]{1,0:T(8,128)S(1)} %select_add_fusion), channel_id=1, source_target_pairs={{0,2},{2,0},{4,6},{6,4},{8,10},{10,8},{12,14},{14,12},{1,3},{3,1},... | collective-permute-start | bytes 491528 | tf_op jit(solution)/shard_map/ppermute | solution.py:125
  181.1 6.1 %collective-permute-start.5 = (bf16[32,1280]{1,0:T(8,128)(2,1)S(1)}, bf16[32,1280]{1,0:T(8,128)(2,1)S(1)}, u32[]{:S(2)}, u32[]{:S(2)}) collective-permute-start(bf16[32,1280]{1,0:T(8,128)(2,1)S(1)} %add_convert_fusion.2), channel_id=1, source_target_pairs={{0,4},{2,6},{4,0},{6,2},{8,12},{10,14},{12,8},{14,10},{1,5},{3,7},... | collective-permute-start | bytes 245768 | tf_op jit(solution)/shard_map/ppermute | solution.py:125
  187.2 10.5 %collective-permute-start.6 = (bf16[32,1280]{1,0:T(8,128)(2,1)S(1)}, bf16[32,1280]{1,0:T(8,128)(2,1)S(1)}, u32[]{:S(2)}, u32[]{:S(2)}) collective-permute-start(bf16[32,1280]{1,0:T(8,128)(2,1)S(1)} %add_convert_fusion.1), channel_id=1, source_target_pairs={{0,8},{2,10},{4,12},{6,14},{8,0},{10,2},{12,4},{14,6},{1,9},{3,11}... | collective-permute-start | bytes 245768 | tf_op jit(solution)/shard_map/ppermute | solution.py:125
  197.8 6.7 %collective-permute-start.7 = (bf16[32,1280]{1,0:T(8,128)(2,1)S(1)}, bf16[32,1280]{1,0:T(8,128)(2,1)S(1)}, u32[]{:S(2)}, u32[]{:S(2)}) collective-permute-start(bf16[32,1280]{1,0:T(8,128)(2,1)S(1)} %add_convert_fusion), channel_id=1, source_target_pairs={{0,1},{1,0},{2,3},{3,2},{4,5},{5,4},{6,7},{7,6},{8,9},{9,8},{10,11... | collective-permute-start | bytes 245768 | tf_op jit(solution)/shard_map/ppermute | solution.py:125

commit v4 on v3

v4 whole, which is shorter than its diff:
```python
import jax
import jax.numpy as jnp
from jax import lax
from jax.experimental import pallas as pl
from jax.experimental.pallas import tpu as pltpu
from jax.sharding import Mesh
from jax.sharding import PartitionSpec as P

HEAD = 128
LAT = 64
GROUP = 256
GROUPS = 8
SLOTS = 4
IPD = 4
NX = 4
NZ = 8
NY = 8
WROWS = 40
COLS = 256
WIDE = 2 * COLS
VIS = 1280
IMAGES = 32
MASKED = -1.0e30
SCALE = HEAD ** -0.5
LOG2E = 1.4426950408889634

NT_DIMS = (((1,), (1,)), ((), ()))
TN_DIMS = (((0,), (0,)), ((), ()))


def attention_kernel(src_ref, dst_ref, doc_ref, tok_ref, q_ref, g_ref, kv_ref,
                     att_ref, dq_ref, dkv_ref, kv, acc, sem):
    group = pl.program_id(0)

    @pl.when(group == 0)
    def _():
        copy = pltpu.make_async_copy(kv_ref, kv, sem)
        copy.start()
        acc[...] = jnp.zeros_like(acc)
        copy.wait()

    tok = tok_ref[0]
    src = [src_ref[group, j] for j in range(SLOTS)]
    dst = [dst_ref[group, j] for j in range(SLOTS)]
    bias = [jnp.where(tok == doc_ref[group, j], 0.0, MASKED) for j in range(SLOTS)]
    bias = jnp.concatenate([jnp.broadcast_to(b, (LAT, GROUP)) for b in bias], axis=0)
    heads = [head * HEAD for head in range(COLS // HEAD)]
    keys = [jnp.concatenate([kv[r, :, lo:lo + HEAD] for r in src], axis=0) for lo in heads]
    values = [jnp.concatenate([kv[r, :, COLS + lo:COLS + lo + HEAD] for r in src], axis=0) for lo in heads]
    queries = [q_ref[:, lo:lo + HEAD] for lo in heads]
    grads = [g_ref[:, lo:lo + HEAD] for lo in heads]
    scores = [
        lax.dot_general(k, q, NT_DIMS, preferred_element_type=jnp.float32)
        for k, q in zip(keys, queries)
    ]
    prob_grads = [
        lax.dot_general(v, g, NT_DIMS, preferred_element_type=jnp.float32)
        for v, g in zip(values, grads)
    ]
    lows, score_grads = [], []
    for s, dp in zip(scores, prob_grads):
        s = s + bias
        top = jnp.max(s, axis=0, keepdims=True)
        e = jnp.exp2((s - top) * (SCALE * LOG2E))
        p = e * (1.0 / jnp.sum(e, axis=0, keepdims=True))
        lows.append(p.astype(jnp.bfloat16))
        centre = jnp.sum(p * dp, axis=0, keepdims=True)
        score_grads.append((p * (dp - centre) * SCALE).astype(jnp.bfloat16))
    for i, lo in enumerate(heads):
        att = lax.dot_general(lows[i], values[i], TN_DIMS, preferred_element_type=jnp.float32)
        dq = lax.dot_general(score_grads[i], keys[i], TN_DIMS, preferred_element_type=jnp.float32)
        att_ref[:, lo:lo + HEAD] = att.astype(jnp.bfloat16)
        dq_ref[:, lo:lo + HEAD] = dq.astype(jnp.bfloat16)
        dk = jnp.dot(score_grads[i], queries[i], preferred_element_type=jnp.float32)
        dv = jnp.dot(lows[i], grads[i], preferred_element_type=jnp.float32)
        for j in range(SLOTS):
            rows = slice(j * LAT, (j + 1) * LAT)
            acc[dst[j], :, lo:lo + HEAD] += dk[rows]
            acc[dst[j], :, COLS + lo:COLS + lo + HEAD] += dv[rows]

    @pl.when(group == GROUPS - 1)
    def _():
        dkv_ref[...] = acc[...].astype(jnp.bfloat16)


def attention(src, dst, docs, tok, queries, grad_out, kv):
    tokens = queries.shape[0]
    block = pl.BlockSpec((GROUP, COLS), lambda g, *_: (g, 0))
    return pl.pallas_call(
        attention_kernel,
        grid_spec=pltpu.PrefetchScalarGridSpec(
            num_scalar_prefetch=3,
            grid=(GROUPS,),
            in_specs=[
                pl.BlockSpec((1, 1, GROUP), lambda g, *_: (g, 0, 0)),
                block,
                block,
                pl.BlockSpec(memory_space=pl.ANY),
            ],
            out_specs=[
                block,
                block,
                pl.BlockSpec((IMAGES, LAT, WIDE), lambda g, *_: (0, 0, 0)),
            ],
            scratch_shapes=[
                pltpu.VMEM((IMAGES, LAT, WIDE), jnp.bfloat16),
                pltpu.VMEM((IMAGES, LAT, WIDE), jnp.float32),
                pltpu.SemaphoreType.DMA,
            ],
        ),
        out_shape=[
            jax.ShapeDtypeStruct((tokens, COLS), jnp.bfloat16),
            jax.ShapeDtypeStruct((tokens, COLS), jnp.bfloat16),
            jax.ShapeDtypeStruct((IMAGES, LAT, WIDE), jnp.bfloat16),
        ],
        compiler_params=pltpu.CompilerParams(
            dimension_semantics=("arbitrary",), vmem_limit_bytes=40 * 2**20
        ),
        cost_estimate=pl.CostEstimate(
            flops=12 * tokens * GROUP * COLS, bytes_accessed=9 * 2**20, transcendentals=0
        ),
    )(src, dst, docs, tok, queries, grad_out, kv)


def from_partner(value, axis, size, bit):
    return lax.ppermute(value, axis, [(i, i ^ bit) for i in range(size)])


def gather(value, axis, size):
    copies = jnp.broadcast_to(value[None], (size,) + value.shape)
    return lax.all_to_all(copies, axis, 0, 0, tiled=True)


def local(queries, latents, key_weight, value_weight, grad_out, pairs, image_slot, token_doc):
    core = lax.axis_index("core")

    weight = jnp.concatenate([key_weight, value_weight], axis=1)
    weight = gather(weight, "z", NZ).reshape(NZ * WROWS, WIDE)
    weight = gather(weight, "x", NX).reshape(VIS, WIDE)
    own = latents[0].reshape(LAT, NZ, NX, WROWS).transpose(0, 2, 1, 3).reshape(LAT, VIS)
    kv = jnp.dot(own, weight, preferred_element_type=jnp.float32).astype(jnp.bfloat16)
    kv = gather(gather(kv, "z", NZ), "x", NX).reshape(IMAGES, LAT, WIDE)

    matches = pairs[..., None] == jnp.arange(IMAGES, dtype=jnp.int32)
    slot = jnp.sum(jnp.where(matches, image_slot, 0), axis=-1).astype(jnp.int32)
    place = slot % NX * NZ + slot // NX
    docs = jnp.where(pairs >= 0, pairs // IPD, -1)
    tok = token_doc.reshape(GROUPS, 1, GROUP)
    attended, grad_queries, dkv = attention(place, place, docs, tok, queries, grad_out, kv)

    dkv = lax.all_to_all(dkv.reshape(NX, NZ, LAT, WIDE), "x", 0, 0, tiled=True)
    dkv = jnp.sum(dkv.astype(jnp.float32), axis=0).astype(jnp.bfloat16)
    dkv = lax.all_to_all(dkv, "z", 0, 0, tiled=True)
    dkv = jnp.sum(dkv.astype(jnp.float32), axis=0).astype(jnp.bfloat16)

    ordered = weight.reshape(NX, NZ, WROWS, WIDE).transpose(1, 0, 2, 3).reshape(VIS, WIDE)
    term = lax.dot_general(dkv, ordered, NT_DIMS, preferred_element_type=jnp.float32)
    half = LAT // 2
    keep = jnp.where(core == 0, term[:half], term[half:])
    give = jnp.where(core == 0, term[half:], term[:half])
    term = (keep + from_partner(give, "core", 2, 1)).astype(jnp.bfloat16)
    term = gather(term, "y", NY)
    term = jnp.sum(term.astype(jnp.float32), axis=0).astype(jnp.bfloat16)
    other = from_partner(term, "core", 2, 1)
    first = jnp.where(core == 0, term, other)
    second = jnp.where(core == 0, other, term)
    return attended, grad_queries, jnp.concatenate([first, second])[None]


def solution(mesh):
    fine = Mesh(mesh.devices.reshape(NZ, NX, NY, 2), ("z", "x", "y", "core"))
    seq, tensor = ("z", "x"), ("y", "core")
    in_specs = (
        P(seq, tensor),
        P(seq, None, None),
        P(seq, tensor),
        P(seq, tensor),
        P(seq, tensor),
        P(seq, None),
        P(),
        P(seq),
    )
    out_specs = (P(seq, tensor), P(seq, tensor), P(seq, None, None))
    return jax.shard_map(local, mesh=fine, in_specs=in_specs, out_specs=out_specs, check_vma=False)
```

time: 206 us -> 189 us (0.917)
  waiting for transfers between devices: 78.4 us -> 50.3 us
  blocking collectives: 65.3 us -> 91 us
  starting transfers between devices: 42.6 us -> 27.7 us
  local copies, waits for them, and re-layouts: 0.34 us -> 4.68 us
  Pallas kernels: 13.1 us -> 9.58 us
    all_to_all x0 -> x1, blocking collectives: none -> 23.6 us  [local(): dkv = lax.all_to_all(dkv.reshape(NX, NZ, LAT, WIDE), 'x', 0, 0, tiled=True)]
    ppermute x3 -> x0, waiting for transfers between devices: 20.4 us -> none  [from_offset(): lax.ppermute(value, axis, [(i, (i - step) % size) for i in range(size)])]
    ppermute x5 -> x2, starting transfers between devices: 26.5 us -> 12.2 us  [from_partner(): return lax.ppermute(value, axis, [(i, i ^ bit) for i in range(size)])]
    ppermute x3 -> x0, starting transfers between devices: 8.79 us -> none  [from_offset(): lax.ppermute(value, axis, [(i, (i - step) % size) for i in range(size)])]
    all_to_all x1 -> x3, starting transfers between devices: 7.3 us -> 15.5 us  [the longest x2 7.89 us: gather(): return lax.all_to_all(copies, axis, 0, 0, tiled=True)]
    ppermute x5 -> x2, waiting for transfers between devices: 9.66 us -> 1.91 us  [from_partner(): return lax.ppermute(value, axis, [(i, i ^ bit) for i in range(size)])]
    pallas_call x1, Pallas kernels: 13.1 us -> 9.58 us  [attention(): pl.pallas_call(attention_kernel, grid_spec=pltpu.PrefetchScalarGridSpec(n...]
    broadcast_in_dim x2 -> x5, local copies, waits for them, and re-layouts: 0.13 us -> 2.89 us  [gather(): copies = jnp.broadcast_to(value[None], (size,) + value.shape)]
  transfers between devices with their start and end apart: 9 -> 5, of which waited for: 9 -> 5; matrix products, arithmetic and copies ran while one was open for 0% -> 0% of each run, Pallas kernels for 0% -> 0%
where the time goes in v4:
time: 189 us; the launch traced here: 188 us
  blocking collectives  91 us (48%)
  waiting for transfers between devices  50.3 us (27%)
  starting transfers between devices  27.7 us (15%)
  Pallas kernels  9.58 us (5%)
  local copies, waits for them, and re-layouts  4.68 us (2%)
  other arithmetic  3.16 us (2%)
    all_to_all x3, blocking collectives, gather(): return lax.all_to_all(copies, axis, 0, 0, tiled=True)  67.4 us
    all_to_all x2, waiting for transfers between devices, gather(): return lax.all_to_all(copies, axis, 0, 0, tiled=True)  36.7 us
    all_to_all x1, blocking collectives, local(): dkv = lax.all_to_all(dkv.reshape(NX, NZ, LAT, WIDE), 'x', 0, 0, tiled=True)  23.6 us
    ppermute x2, starting transfers between devices, from_partner(): return lax.ppermute(value, axis, [(i, i ^ bit) for i in range(size)])  12.2 us
    all_to_all x1, waiting for transfers between devices, local(): dkv = lax.all_to_all(dkv, 'z', 0, 0, tiled=True)  11.6 us
    pallas_call x1, Pallas kernels, attention(): pl.pallas_call(attention_kernel, grid_spec=pltpu.PrefetchScalarGridSpec(n...  9.58 us
    all_to_all x2, starting transfers between devices, gather(): return lax.all_to_all(copies, axis, 0, 0, tiled=True)  7.89 us
    all_to_all x1, starting transfers between devices, local(): dkv = lax.all_to_all(dkv, 'z', 0, 0, tiled=True)  7.58 us
  transfers between devices with their start and end apart: 5, of which 5 were waited for; matrix products, arithmetic and copies ran while one was open for 0% of the time, Pallas kernels for 0%

profile of v4, /device:TPU:1, one launch (start us, length us, event | category | flops | bytes accessed | tf_op | source)
XLA Modules:
  0.0 188.1 jit_solution(15986913977699170021)
XLA Ops:
  0.6 0.8 pad_maximum_fusion
  1.4 22.3 %all_to_all.35 = bf16[8,40,512]{2,1,0:T(8,128)(2,1)S(1)} all-to-all(bf16[8,40,512]{2,1,0:T(8,128)(2,1)S(1)} %broadcast_in_dim.26), channel_id=1, replica_groups=mesh['z'=8,'x'=4,'y'=8,'core'=2] {'z'}, dimensions={0} | all-to-all | bytes 655360 | tf_op jit(solution)/shard_map/all_to_all | solution.py:131
  23.7 1.2 broadcast_in_dim.50
  24.9 0.0 copy-start.5
  24.9 4.1 %all-to-all-start.1 = ((bf16[4,320,512]{2,1,0:T(8,128)(2,1)}), bf16[4,320,512]{2,1,0:T(8,128)(2,1)S(1)}, u32[]{:S(2)}, u32[]{:S(2)}) async-start(bf16[4,320,512]{2,1,0:T(8,128)(2,1)} %broadcast_in_dim.50), calls=%async_computation.1 | async-start | bytes 2621440 | tf_op jit(solution)/shard_map/all_to_all | solution.py:131
  29.1 0.0 copy-done.5
  29.1 0.2 copy.43
  29.3 14.8 %all-to-all-done.1 = bf16[4,320,512]{2,1,0:T(8,128)(2,1)S(1)} async-done(((bf16[4,320,512]{2,1,0:T(8,128)(2,1)}), bf16[4,320,512]{2,1,0:T(8,128)(2,1)S(1)}, u32[]{:S(2)}, u32[]{:S(2)}) %all-to-all-start.1) | async-done | bytes 1310752 | tf_op jit(solution)/shard_map/all_to_all | solution.py:131
  44.2 0.0 copy-start.3
  44.2 0.4 fusion
  44.6 18.9 %all_to_all.36 = bf16[8,64,512]{2,1,0:T(8,128)(2,1)S(1)} all-to-all(bf16[8,64,512]{2,1,0:T(8,128)(2,1)S(1)} %broadcast_in_dim.51), channel_id=1, replica_groups=mesh['z'=8,'x'=4,'y'=8,'core'=2] {'z'}, dimensions={0} | all-to-all | bytes 1048576 | tf_op jit(solution)/shard_map/all_to_all | solution.py:131
  63.5 0.0 copy-done.3
  63.5 1.6 broadcast_in_dim.52
  65.1 0.0 copy-start.6
  65.1 0.0 copy-start.7
  65.1 0.0 copy-start
  65.1 0.0 copy-start.2
  65.2 3.8 %all-to-all-start.3 = ((bf16[4,8,64,512]{3,2,1,0:T(8,128)(2,1)}), bf16[4,8,64,512]{3,2,1,0:T(8,128)(2,1)S(1)}, u32[]{:S(2)}, u32[]{:S(2)}) async-start(bf16[4,8,64,512]{3,2,1,0:T(8,128)(2,1)} %broadcast_in_dim.52), calls=%async_computation.3 | async-start | bytes 4194304 | tf_op jit(solution)/shard_map/all_to_all | solution.py:131
  68.9 0.0 copy-done.6
  68.9 0.1 copy.38
  69.0 0.0 copy-done.7
  69.0 0.2 select_reduce_fusion
  69.2 0.1 copy.34
  69.3 21.9 %all-to-all-done.3 = bf16[4,8,64,512]{3,2,1,0:T(8,128)(2,1)S(1)} async-done(((bf16[4,8,64,512]{3,2,1,0:T(8,128)(2,1)}), bf16[4,8,64,512]{3,2,1,0:T(8,128)(2,1)S(1)}, u32[]{:S(2)}, u32[]{:S(2)}) %all-to-all-start.3) | async-done | bytes 2097184 | tf_op jit(solution)/shard_map/all_to_all | solution.py:131
  91.2 0.0 copy-done
  91.2 0.0 copy-done.2
  91.2 0.0 copy-start.1
  91.2 1.2 copy-done.1
  92.5 9.6 %shard_map.103 = (bf16[2048,256]{1,0:T(8,128)(2,1)}, bf16[2048,256]{1,0:T(8,128)(2,1)}, bf16[32,64,512]{2,1,0:T(8,128)(2,1)S(1)}) custom-call(s32[8,4]{1,0:T(8,128)S(1)} %get-tuple-element.11.src_ref.dst_ref, s32[8,4]{1,0:T(8,128)S(1)} %get-tuple-element.11.src_ref.dst_ref, s32[8,4]{1,0:T(8,128)S(1)} %get-tuple-element.12.doc_ref, ...), custom_call_target="tpu_custom_call" | custom-call | flops 1610612736 | bytes 9437184 | tf_op jit(solution)/shard_map/pallas_call | solution.py:89
  102.0 23.6 %all_to_all.37 = bf16[4,8,64,512]{3,2,1,0:T(8,128)(2,1)S(1)} all-to-all(bf16[4,8,64,512]{3,2,1,0:T(8,128)(2,1)S(1)} %bitcast.22), channel_id=1, replica_groups=mesh['z'=8,'x'=4,'y'=8,'core'=2] {'x'}, dimensions={0} | all-to-all | bytes 4194304 | tf_op jit(solution)/shard_map/all_to_all | solution.py:151
  125.7 0.0 copy-start.4
  125.7 1.3 reduce_sum.46
  126.9 7.6 %all-to-all-start.5 = ((bf16[8,64,512]{2,1,0:T(8,128)(2,1)}), bf16[8,64,512]{2,1,0:T(8,128)(2,1)S(1)}, u32[]{:S(2)}, u32[]{:S(2)}) async-start(bf16[8,64,512]{2,1,0:T(8,128)(2,1)} %reduce_sum.46), calls=%async_computation.5 | async-start | bytes 1048576 | tf_op jit(solution)/shard_map/all_to_all | solution.py:153
  134.5 0.0 copy-done.4
  134.5 0.1 copy.45
  134.6 11.6 %all-to-all-done.5 = bf16[8,64,512]{2,1,0:T(8,128)(2,1)S(1)} async-done(((bf16[8,64,512]{2,1,0:T(8,128)(2,1)}), bf16[8,64,512]{2,1,0:T(8,128)(2,1)S(1)}, u32[]{:S(2)}, u32[]{:S(2)}) %all-to-all-start.5) | async-done | bytes 524320 | tf_op jit(solution)/shard_map/all_to_all | solution.py:153
  146.3 0.1 reduce_sum.47
  146.3 0.5 fusion.10
  146.9 8.6 %collective-permute-start = (f32[32,1280]{1,0:T(8,128)S(1)}, f32[32,1280]{1,0:T(8,128)S(1)}, u32[]{:S(2)}, u32[]{:S(2)}) collective-permute-start(f32[32,1280]{1,0:T(8,128)S(1)} %slice_select_fusion), channel_id=1, source_target_pairs={{0,1},{1,0},{2,3},{3,2},{4,5},{5,4},{6,7},{7,6},{8,9},{9,8},{10,11... | collective-permute-start | bytes 491528 | tf_op jit(solution)/shard_map/ppermute | solution.py:126
  155.5 1.0 collective-permute-done
  156.6 26.1 %all_to_all.38 = bf16[8,32,1280]{2,1,0:T(8,128)(2,1)S(1)} all-to-all(bf16[8,32,1280]{2,1,0:T(8,128)(2,1)S(1)} %broadcast_in_dim.53), channel_id=1, replica_groups=mesh['z'=8,'x'=4,'y'=8,'core'=2] {'y'}, dimensions={0} | all-to-all | bytes 1310720 | tf_op jit(solution)/shard_map/all_to_all | solution.py:131
  182.7 0.1 reduce_sum.48
  182.8 3.6 %collective-permute-start.1 = (bf16[32,1280]{1,0:T(8,128)(2,1)S(1)}, bf16[32,1280]{1,0:T(8,128)(2,1)S(1)}, u32[]{:S(2)}, u32[]{:S(2)}) collective-permute-start(bf16[32,1280]{1,0:T(8,128)(2,1)S(1)} %reduce_sum.48), channel_id=1, source_target_pairs={{0,1},{1,0},{2,3},{3,2},{4,5},{5,4},{6,7},{7,6},{8,9},{9,8},{10,11... | collective-permute-start | bytes 245768 | tf_op jit(solution)/shard_map/ppermute | solution.py:126
  186.5 0.9 collective-permute-done.1
  187.4 0.7 maximum_bitcast_fusion
  (8 shorter events, 0.2 us)
Async XLA Ops:
  24.9 4.1 %copy-start.5 = (bf16[1,64,1280]{2,1,0:T(8,128)(2,1)S(1)}, bf16[1,64,1280]{2,1,0:T(8,128)(2,1)}, u32[]{:S(2)}) copy-start(bf16[1,64,1280]{2,1,0:T(8,128)(2,1)} %param.9) | copy-start | bytes 491524
  24.9 19.2 %all-to-all-start.1 = ((bf16[4,320,512]{2,1,0:T(8,128)(2,1)}), bf16[4,320,512]{2,1,0:T(8,128)(2,1)S(1)}, u32[]{:S(2)}, u32[]{:S(2)}) async-start(bf16[4,320,512]{2,1,0:T(8,128)(2,1)} %broadcast_in_dim.50), calls=%async_computation.1 | async-start | bytes 2621440 | tf_op jit(solution)/shard_map/all_to_all | solution.py:131
  44.2 19.4 %copy-start.3 = (bf16[4,320,512]{2,1,0:T(8,128)(2,1)}, bf16[4,320,512]{2,1,0:T(8,128)(2,1)S(1)}, u32[]{:S(2)}) copy-start(bf16[4,320,512]{2,1,0:T(8,128)(2,1)S(1)} %all-to-all-done.1) | copy-start | bytes 3932164
  65.1 3.8 %copy-start.6 = (s32[8,4]{0,1:T(4,128)S(1)}, s32[8,4]{0,1:T(4,128)}, u32[]{:S(2)}) copy-start(s32[8,4]{0,1:T(4,128)} %param.13) | copy-start | bytes 388
  65.1 3.9 %copy-start.7 = (s32[32]{0:T(128)S(1)}, s32[32]{0:T(128)}, u32[]{:S(2)}) copy-start(s32[32]{0:T(128)} %param.14) | copy-start | bytes 388
  65.1 26.1 %copy-start = (bf16[2048,256]{1,0:T(8,128)(2,1)S(1)}, bf16[2048,256]{1,0:T(8,128)(2,1)}, u32[]{:S(2)}) copy-start(bf16[2048,256]{1,0:T(8,128)(2,1)} %q_ref.1) | copy-start | bytes 3145732
  65.1 26.1 %copy-start.2 = (s32[2048]{0:T(1024)S(1)}, s32[2048]{0:T(1024)}, u32[]{:S(2)}) copy-start(s32[2048]{0:T(1024)} %param.15) | copy-start | bytes 24580
  65.2 26.1 %all-to-all-start.3 = ((bf16[4,8,64,512]{3,2,1,0:T(8,128)(2,1)}), bf16[4,8,64,512]{3,2,1,0:T(8,128)(2,1)S(1)}, u32[]{:S(2)}, u32[]{:S(2)}) async-start(bf16[4,8,64,512]{3,2,1,0:T(8,128)(2,1)} %broadcast_in_dim.52), calls=%async_computation.3 | async-start | bytes 4194304 | tf_op jit(solution)/shard_map/all_to_all | solution.py:131
  91.2 1.2 copy-start.1
  125.7 8.8 %copy-start.4 = (bf16[4,320,512]{2,1,0:T(8,128)(2,1)S(1)}, bf16[4,320,512]{2,1,0:T(8,128)(2,1)}, u32[]{:S(2)}) copy-start(bf16[4,320,512]{2,1,0:T(8,128)(2,1)} %copy-done.3) | copy-start | bytes 3932164
  126.9 19.3 %all-to-all-start.5 = ((bf16[8,64,512]{2,1,0:T(8,128)(2,1)}), bf16[8,64,512]{2,1,0:T(8,128)(2,1)S(1)}, u32[]{:S(2)}, u32[]{:S(2)}) async-start(bf16[8,64,512]{2,1,0:T(8,128)(2,1)} %reduce_sum.46), calls=%async_computation.5 | async-start | bytes 1048576 | tf_op jit(solution)/shard_map/all_to_all | solution.py:153
  146.9 9.6 %collective-permute-start = (f32[32,1280]{1,0:T(8,128)S(1)}, f32[32,1280]{1,0:T(8,128)S(1)}, u32[]{:S(2)}, u32[]{:S(2)}) collective-permute-start(f32[32,1280]{1,0:T(8,128)S(1)} %slice_select_fusion), channel_id=1, source_target_pairs={{0,1},{1,0},{2,3},{3,2},{4,5},{5,4},{6,7},{7,6},{8,9},{9,8},{10,11... | collective-permute-start | bytes 491528 | tf_op jit(solution)/shard_map/ppermute | solution.py:126
  182.8 4.5 %collective-permute-start.1 = (bf16[32,1280]{1,0:T(8,128)(2,1)S(1)}, bf16[32,1280]{1,0:T(8,128)(2,1)S(1)}, u32[]{:S(2)}, u32[]{:S(2)}) collective-permute-start(bf16[32,1280]{1,0:T(8,128)(2,1)S(1)} %reduce_sum.48), channel_id=1, source_target_pairs={{0,1},{1,0},{2,3},{3,2},{4,5},{5,4},{6,7},{7,6},{8,9},{9,8},{10,11... | collective-permute-start | bytes 245768 | tf_op jit(solution)/shard_map/ppermute | solution.py:126

commit v5 on v4

v5 whole, which is shorter than its diff:
```python
import jax
import jax.numpy as jnp
from jax import lax
from jax.experimental import pallas as pl
from jax.experimental.pallas import tpu as pltpu
from jax.sharding import Mesh
from jax.sharding import PartitionSpec as P

HEAD = 128
LAT = 64
GROUP = 256
GROUPS = 8
SLOTS = 4
IPD = 4
NX = 4
NZ = 8
NT = 16
COLS = 256
WIDE = 2 * COLS
VIS = 1280
WROWS = 40
IMAGES = 32
DOCS = 8
QUARTER = LAT // NX
SPAN = 3
WINDOW = SPAN * IPD
MASKED = -1.0e30
SCALE = HEAD ** -0.5
LOG2E = 1.4426950408889634

NT_DIMS = (((1,), (1,)), ((), ()))
TN_DIMS = (((0,), (0,)), ((), ()))


def attention_kernel(src_ref, doc_ref, tok_ref, q_ref, g_ref, kv_ref,
                     att_ref, dq_ref, dkv_ref, acc):
    group = pl.program_id(0)

    @pl.when(group == 0)
    def _():
        acc[...] = jnp.zeros_like(acc)

    tok = tok_ref[0]
    src = [src_ref[group, j] for j in range(SLOTS)]
    bias = [jnp.where(tok == doc_ref[group, j], 0.0, MASKED) for j in range(SLOTS)]
    bias = jnp.concatenate([jnp.broadcast_to(b, (LAT, GROUP)) for b in bias], axis=0)
    heads = [head * HEAD for head in range(COLS // HEAD)]

    def rows_of(lo):
        return jnp.concatenate(
            [kv_ref[part, r, :, lo:lo + HEAD] for r in src for part in range(NX)], axis=0
        )

    keys = [rows_of(lo) for lo in heads]
    values = [rows_of(COLS + lo) for lo in heads]
    queries = [q_ref[:, lo:lo + HEAD] for lo in heads]
    grads = [g_ref[:, lo:lo + HEAD] for lo in heads]
    scores = [
        lax.dot_general(k, q, NT_DIMS, preferred_element_type=jnp.float32)
        for k, q in zip(keys, queries)
    ]
    prob_grads = [
        lax.dot_general(v, g, NT_DIMS, preferred_element_type=jnp.float32)
        for v, g in zip(values, grads)
    ]
    lows, score_grads = [], []
    for s, dp in zip(scores, prob_grads):
        s = s + bias
        top = jnp.max(s, axis=0, keepdims=True)
        e = jnp.exp2((s - top) * (SCALE * LOG2E))
        p = e * (1.0 / jnp.sum(e, axis=0, keepdims=True))
        lows.append(p.astype(jnp.bfloat16))
        centre = jnp.sum(p * dp, axis=0, keepdims=True)
        score_grads.append((p * (dp - centre) * SCALE).astype(jnp.bfloat16))
    for i, lo in enumerate(heads):
        att = lax.dot_general(lows[i], values[i], TN_DIMS, preferred_element_type=jnp.float32)
        dq = lax.dot_general(score_grads[i], keys[i], TN_DIMS, preferred_element_type=jnp.float32)
        att_ref[:, lo:lo + HEAD] = att.astype(jnp.bfloat16)
        dq_ref[:, lo:lo + HEAD] = dq.astype(jnp.bfloat16)
        dk = jnp.dot(score_grads[i], queries[i], preferred_element_type=jnp.float32)
        dv = jnp.dot(lows[i], grads[i], preferred_element_type=jnp.float32)
        for j in range(SLOTS):
            rows = slice(j * LAT, (j + 1) * LAT)
            acc[src[j], :, lo:lo + HEAD] += dk[rows]
            acc[src[j], :, COLS + lo:COLS + lo + HEAD] += dv[rows]

    @pl.when(group == GROUPS - 1)
    def _():
        for part in range(NX):
            rows = slice(part * QUARTER, (part + 1) * QUARTER)
            dkv_ref[part] = acc[:, rows, :].astype(jnp.bfloat16)


def attention(src, docs, tok, queries, grad_out, kv):
    tokens = queries.shape[0]
    held = kv.shape[1]
    block = pl.BlockSpec((GROUP, COLS), lambda g, *_: (g, 0))
    whole = pl.BlockSpec((NX, held, QUARTER, WIDE), lambda g, *_: (0, 0, 0, 0))
    return pl.pallas_call(
        attention_kernel,
        grid_spec=pltpu.PrefetchScalarGridSpec(
            num_scalar_prefetch=2,
            grid=(GROUPS,),
            in_specs=[pl.BlockSpec((1, 1, GROUP), lambda g, *_: (g, 0, 0)), block, block, whole],
            out_specs=[block, block, whole],
            scratch_shapes=[pltpu.VMEM((held, LAT, WIDE), jnp.float32)],
        ),
        out_shape=[
            jax.ShapeDtypeStruct((tokens, COLS), jnp.bfloat16),
            jax.ShapeDtypeStruct((tokens, COLS), jnp.bfloat16),
            jax.ShapeDtypeStruct((NX, held, QUARTER, WIDE), jnp.bfloat16),
        ],
        compiler_params=pltpu.CompilerParams(
            dimension_semantics=("arbitrary",), vmem_limit_bytes=40 * 2**20
        ),
        cost_estimate=pl.CostEstimate(
            flops=12 * tokens * GROUP * COLS, bytes_accessed=9 * 2**20, transcendentals=0
        ),
    )(src, docs, tok, queries, grad_out, kv)


def pick_kernel(index_ref, all_ref, out_ref):
    for n in range(NX * WINDOW):
        out_ref[n] = all_ref[index_ref[n]]


def add_kernel(index_ref, parts_ref, out_ref, acc):
    acc[...] = jnp.zeros_like(acc)
    for n in range(NX * WINDOW):
        acc[index_ref[n]] += parts_ref[n].astype(jnp.float32)
    out_ref[...] = acc[...].astype(jnp.bfloat16)


def by_index(kernel, index, operand, count, scratch):
    return pl.pallas_call(
        kernel,
        in_specs=[
            pl.BlockSpec(memory_space=pltpu.SMEM),
            pl.BlockSpec(memory_space=pltpu.VMEM),
        ],
        out_specs=pl.BlockSpec(memory_space=pltpu.VMEM),
        out_shape=jax.ShapeDtypeStruct((count, QUARTER, WIDE), jnp.bfloat16),
        scratch_shapes=scratch,
        compiler_params=pltpu.CompilerParams(vmem_limit_bytes=16 * 2**20),
        cost_estimate=pl.CostEstimate(flops=0, bytes_accessed=2**21, transcendentals=0),
    )(index, operand)


def gather(value, axis, size):
    copies = jnp.broadcast_to(value[None], (size,) + value.shape)
    return lax.all_to_all(copies, axis, 0, 0, tiled=True)


def lookup(slot_table, image_ids):
    matches = image_ids[..., None] == jnp.arange(IMAGES, dtype=jnp.int32)
    return jnp.sum(jnp.where(matches, slot_table, 0), axis=-1).astype(jnp.int32)


def local(queries, latents, key_weight, value_weight, grad_out, pairs, image_slot, token_doc):
    z = lax.axis_index("z")
    low_doc, high_doc = jnp.min(token_doc), jnp.max(token_doc)
    start = jnp.minimum(low_doc, DOCS - SPAN)
    note = jnp.stack([start, high_doc - start + 1]).astype(jnp.bfloat16)

    weight = jnp.concatenate([key_weight, value_weight], axis=1)
    extra = jnp.broadcast_to(jnp.tile(note, COLS)[None], (8, WIDE))
    column = gather(jnp.concatenate([weight, extra]), "z", NZ)
    notes = column[:, WROWS, :2].reshape(2 * NZ)
    column = column[:, :WROWS].reshape(NZ * WROWS, WIDE)

    own = latents[0].reshape(LAT, NZ, NX, WROWS).transpose(0, 2, 1, 3).reshape(NX, QUARTER, VIS)
    notes = jnp.broadcast_to(jnp.tile(notes, COLS // (2 * NZ)), (NX, QUARTER, COLS))
    own = jnp.concatenate([own, notes], axis=2)
    sent = [jnp.broadcast_to(column[None], (NX,) + column.shape)]
    sent += [own[:, :, i * WIDE:(i + 1) * WIDE] for i in range(3)]
    row = lax.all_to_all(jnp.concatenate(sent, axis=1), "x", 0, 0, tiled=True)
    tall = NZ * WROWS
    weight = row[:, :tall].reshape(VIS, WIDE)
    images = [row[:, tall + i * QUARTER:tall + (i + 1) * QUARTER] for i in range(3)]
    images = jnp.concatenate(images, axis=2).reshape(LAT, 3 * WIDE)
    notes = row[:, tall + 2 * QUARTER, COLS:COLS + 2 * NZ].reshape(NX, NZ, 2).astype(jnp.int32)

    kv = jnp.dot(images[:, :VIS], weight, preferred_element_type=jnp.float32).astype(jnp.bfloat16)
    kv = gather(kv, "z", NZ).reshape(IMAGES, QUARTER, WIDE)

    docs = jnp.where(pairs >= 0, pairs // IPD, -1)
    tok = token_doc.reshape(GROUPS, 1, GROUP)
    starts = lax.dynamic_index_in_dim(notes[:, :, 0], z, axis=1, keepdims=False)
    wanted = starts[:, None] * IPD + jnp.arange(WINDOW, dtype=jnp.int32)
    wanted = lookup(image_slot, wanted).reshape(NX * WINDOW)

    def narrow():
        picked = by_index(pick_kernel, wanted, kv, NX * WINDOW, [])
        held = lax.all_to_all(picked.reshape(NX, WINDOW, QUARTER, WIDE), "x", 0, 0, tiled=True)
        src = jnp.clip(pairs - start * IPD, 0, WINDOW - 1)
        att, dq, dkv = attention(src, docs, tok, queries, grad_out, held)
        dkv = lax.all_to_all(dkv, "x", 0, 0, tiled=True).reshape(NX * WINDOW, QUARTER, WIDE)
        total = pltpu.VMEM((IMAGES, QUARTER, WIDE), jnp.float32)
        return att, dq, by_index(add_kernel, wanted, dkv, IMAGES, [total])

    def full():
        held = gather(kv, "x", NX)
        att, dq, dkv = attention(lookup(image_slot, pairs), docs, tok, queries, grad_out, held)
        dkv = lax.all_to_all(dkv, "x", 0, 0, tiled=True)
        return att, dq, jnp.sum(dkv.astype(jnp.float32), axis=0).astype(jnp.bfloat16)

    attended, grad_queries, dkv = lax.cond(jnp.max(notes[:, :, 1]) <= SPAN, narrow, full)

    dkv = lax.all_to_all(dkv, ("z", "x"), 0, 0, tiled=True).reshape(NZ, LAT, WIDE)
    dkv = jnp.sum(dkv.astype(jnp.float32), axis=0).astype(jnp.bfloat16)

    ordered = weight.reshape(NX, NZ, WROWS, WIDE).transpose(1, 0, 2, 3).reshape(VIS, WIDE)
    term = lax.dot_general(dkv, ordered, NT_DIMS, preferred_element_type=jnp.float32)
    term = term.astype(jnp.bfloat16).reshape(NT, LAT // NT, VIS)
    term = lax.all_to_all(term, ("y", "core"), 0, 0, tiled=True)
    term = jnp.sum(term.astype(jnp.float32), axis=0).astype(jnp.bfloat16)
    term = gather(term, ("y", "core"), NT).reshape(1, LAT, VIS)
    return attended, grad_queries, term


def solution(mesh):
    fine = Mesh(mesh.devices.reshape(NZ, NX, NT // 2, 2), ("z", "x", "y", "core"))
    seq, tensor = ("z", "x"), ("y", "core")
    in_specs = (
        P(seq, tensor),
        P(seq, None, None),
        P(seq, tensor),
        P(seq, tensor),
        P(seq, tensor),
        P(seq, None),
        P(),
        P(seq),
    )
    out_specs = (P(seq, tensor), P(seq, tensor), P(seq, None, None))
    return jax.shard_map(local, mesh=fine, in_specs=in_specs, out_specs=out_specs, check_vma=False)
```

time: 189 us -> 164 us (0.87)
  blocking collectives: 91 us -> 68.6 us
  starting transfers between devices: 27.7 us -> 21.9 us
  Pallas kernels: 9.58 us -> 13.7 us
  waiting for transfers between devices: 50.3 us -> 46.2 us
  between operations: 0.76 us -> 2.79 us
    all_to_all x3 -> x1, blocking collectives: 67.4 us -> 12.3 us  [gather(): return lax.all_to_all(copies, axis, 0, 0, tiled=True)]
    all_to_all x1 -> x3, blocking collectives: 23.6 us -> 56.3 us  [the longest x1 23.8 us: local(): term = lax.all_to_all(term, ('y', 'core'), 0, 0, tiled=True)]
    ppermute x2 -> x0, starting transfers between devices: 12.2 us -> none  [from_partner(): return lax.ppermute(value, axis, [(i, i ^ bit) for i in range(size)])]
    all_to_all x2, waiting for transfers between devices: 36.7 us -> 25.3 us  [gather(): return lax.all_to_all(copies, axis, 0, 0, tiled=True)]
    all_to_all x1 -> x2, waiting for transfers between devices: 11.6 us -> 20.8 us  [the longest x1 12.6 us: local(): lax.all_to_all(dkv, ('z', 'x'), 0, 0, tiled=True).reshape(NZ, LAT, WIDE)]
    all_to_all x2, starting transfers between devices: 7.89 us -> 14.4 us  [gather(): return lax.all_to_all(copies, axis, 0, 0, tiled=True)]
    pallas_call x0 -> x2, Pallas kernels: none -> 3.23 us  [by_index(): pl.pallas_call(kernel, in_specs=[pl.BlockSpec(memory_space=pltpu.SMEM), p...]
    ppermute x2 -> x0, waiting for transfers between devices: 1.91 us -> none  [from_partner(): return lax.ppermute(value, axis, [(i, i ^ bit) for i in range(size)])]
  transfers between devices with their start and end apart: 5 -> 4, of which waited for: 5 -> 4; matrix products, arithmetic and copies ran while one was open for 0% -> 2% of each run, Pallas kernels for 0% -> 0%
where the time goes in v5:
time: 164 us; the launch traced here: 163 us
  blocking collectives  68.6 us (42%)
  waiting for transfers between devices  46.2 us (28%)
  starting transfers between devices  21.9 us (13%)
  Pallas kernels  13.7 us (8%)
  local copies, waits for them, and re-layouts  5.29 us (3%)
  other arithmetic  3.5 us (2%)
  between operations  2.79 us (2%)
    all_to_all x2, waiting for transfers between devices, gather(): return lax.all_to_all(copies, axis, 0, 0, tiled=True)  25.3 us
    all_to_all x1, blocking collectives, local(): term = lax.all_to_all(term, ('y', 'core'), 0, 0, tiled=True)  23.8 us
    all_to_all x1, blocking collectives, local(): row = lax.all_to_all(jnp.concatenate(sent, axis=1), 'x', 0, 0, tiled=True)  21.8 us
    all_to_all x2, starting transfers between devices, gather(): return lax.all_to_all(copies, axis, 0, 0, tiled=True)  14.4 us
    all_to_all x1, waiting for transfers between devices, local(): lax.all_to_all(dkv, ('z', 'x'), 0, 0, tiled=True).reshape(NZ, LAT, WIDE)  12.6 us
    all_to_all x1, blocking collectives, gather(): return lax.all_to_all(copies, axis, 0, 0, tiled=True)  12.3 us
    all_to_all x1, blocking collectives, narrow(): lax.all_to_all(dkv, 'x', 0, 0, tiled=True)  10.7 us
    pallas_call x1, Pallas kernels, attention(): pl.pallas_call(attention_kernel, grid_spec=pltpu.PrefetchScalarGridSpec(n...  10.5 us
  transfers between devices with their start and end apart: 4, of which 4 were waited for; matrix products, arithmetic and copies ran while one was open for 2% of the time, Pallas kernels for 0%

profile of v5, /device:TPU:1, one launch (start us, length us, event | category | flops | bytes accessed | tf_op | source)
XLA Modules:
  0.0 162.9 jit_solution(12032003002654350329)
XLA Ops:
  0.6 0.0 copy-start
  0.6 1.4 fusion.4
  3.3 0.1 pad_maximum_fusion.4
  3.4 0.1 broadcast_in_dim.68
  3.6 0.8 pad_maximum_fusion.3
  4.3 0.8 broadcast_in_dim.70
  5.1 10.9 %all-to-all-start.4 = ((bf16[8,48,512]{2,1,0:T(8,128)(2,1)}), bf16[8,48,512]{2,1,0:T(8,128)(2,1)S(1)}, u32[]{:S(2)}, u32[]{:S(2)}) async-start(bf16[8,48,512]{2,1,0:T(8,128)(2,1)} %broadcast_in_dim.70), calls=%async_computation.4 | async-start | bytes 786432 | tf_op jit(solution)/shard_map/all_to_all | solution.py:151
  16.0 0.0 copy-done
  16.0 0.2 copy.45
  16.2 0.8 copy.46
  17.0 0.7 reshape.94
  17.7 12.5 %all-to-all-done.4 = bf16[8,48,512]{2,1,0:T(8,128)(2,1)S(1)} async-done(((bf16[8,48,512]{2,1,0:T(8,128)(2,1)}), bf16[8,48,512]{2,1,0:T(8,128)(2,1)S(1)}, u32[]{:S(2)}, u32[]{:S(2)}) %all-to-all-start.4) | async-done | bytes 393248 | tf_op jit(solution)/shard_map/all_to_all | solution.py:151
  30.2 0.1 tile.17
  30.3 0.1 reshape.104
  30.5 0.1 broadcast_in_dim.72
  30.6 0.1 pad_maximum_fusion
  30.7 21.8 %all_to_all.48 = bf16[4,368,512]{2,1,0:T(8,128)(2,1)S(1)} all-to-all(bf16[4,368,512]{2,1,0:T(8,128)(2,1)S(1)} %pad_maximum_fusion), channel_id=1, replica_groups=mesh['z'=8,'x'=4,'y'=8,'core'=2] {'x'}, dimensions={0} | all-to-all | bytes 3014656 | tf_op jit(solution)/shard_map/all_to_all | solution.py:176
  52.6 0.1 slice.63
  52.7 0.0 copy-start.1
  52.7 0.0 copy-start.2
  52.7 0.0 copy-start.3
  52.7 0.3 convolution_convert_fusion.1
  53.1 0.8 broadcast_in_dim.74
  53.9 3.5 %all-to-all-start.6 = ((bf16[8,64,512]{2,1,0:T(8,128)(2,1)}), bf16[8,64,512]{2,1,0:T(8,128)(2,1)S(1)}, u32[]{:S(2)}, u32[]{:S(2)}) async-start(bf16[8,64,512]{2,1,0:T(8,128)(2,1)} %broadcast_in_dim.74), calls=%async_computation.6 | async-start | bytes 1048576 | tf_op jit(solution)/shard_map/all_to_all | solution.py:151
  57.4 0.0 copy-done.1
  57.4 0.1 copy.48
  57.5 0.1 copy.55
  57.7 0.6 slice_reduce_fusion
  59.0 12.9 %all-to-all-done.6 = bf16[8,64,512]{2,1,0:T(8,128)(2,1)S(1)} async-done(((bf16[8,64,512]{2,1,0:T(8,128)(2,1)}), bf16[8,64,512]{2,1,0:T(8,128)(2,1)S(1)}, u32[]{:S(2)}, u32[]{:S(2)}) %all-to-all-start.6) | async-done | bytes 524320 | tf_op jit(solution)/shard_map/all_to_all | solution.py:151
  71.8 0.0 copy-done.2
  71.8 0.0 copy-done.3
  71.8 36.7 %conditional.1 = (bf16[2048,256]{1,0:T(8,128)(2,1)}, bf16[2048,256]{1,0:T(8,128)(2,1)}, bf16[32,16,512]{2,1,0:T(8,128)(2,1)}) conditional(s32[]{:T(128)} %convert_element_type.28, (s32[8,4]{0,1:T(4,128)S(1)}, s32[32]{0:T(128)S(1)}, bf16[8,64,512]{2,1,0:T(8,128)(2,1)S(1)}, s32[8,4]{1,0:T(8,128)S(1)}, s32[8,1,256]{2,1,0:T(1,128)S(1)}, ...), branch_computations={%region_3.6_spmd, %region_6.8_spmd} | conditional | flops 1611402240 | bytes 25166522 | solution.py:207
  71.9 0.1 add_bitcast_fusion
  72.0 0.2 select_reduce_fusion.1
  72.2 0.1 reshape.82.index_ref
  72.3 1.5 branch_1_fun.3
  73.7 3.5 %all-to-all-start.2 = ((bf16[4,12,16,512]{3,2,1,0:T(8,128)(2,1)}), bf16[4,12,16,512]{3,2,1,0:T(8,128)(2,1)S(1)}, u32[]{:S(2)}, u32[]{:S(2)}) async-start(bf16[4,12,16,512]{3,2,1,0:T(8,128)(2,1)} %bitcast.4), calls=%async_computation.2 | async-start | bytes 1572864 | tf_op jit(solution)/shard_map/cond/branch_1_fun/all_to_all | solution.py:194
  77.2 0.1 copy.53
  77.3 8.2 %all-to-all-done.2.kv_ref = bf16[4,12,16,512]{3,2,1,0:T(8,128)(2,1)S(1)} async-done(((bf16[4,12,16,512]{3,2,1,0:T(8,128)(2,1)}), bf16[4,12,16,512]{3,2,1,0:T(8,128)(2,1)S(1)}, u32[]{:S(2)}, u32[]{:S(2)}) %all-to-all-start.2) | async-done | bytes 786464 | tf_op jit(solution)/shard_map/cond/branch_1_fun/all_to_all | solution.py:194
  85.6 10.5 %branch_1_fun.4 = (bf16[2048,256]{1,0:T(8,128)(2,1)}, bf16[2048,256]{1,0:T(8,128)(2,1)}, bf16[4,12,16,512]{3,2,1,0:T(8,128)(2,1)S(1)}) custom-call(s32[8,4]{1,0:T(8,128)S(1)} %subtract_clamp_fusion.src_ref, s32[8,4]{1,0:T(8,128)S(1)} %get-tuple-element.78.doc_ref, s32[8,1,256]{2,1,0:T(1,128)S(1)} %get-tuple-element.79.tok_ref, ...), custom_call_target="tpu_custom_call" | custom-call | flops 1610612736 | bytes 9437184 | tf_op jit(solution)/shard_map/cond/branch_1_fun/pallas_call | solution.py:99
  96.0 10.7 %all_to_all.47 = bf16[4,12,16,512]{3,2,1,0:T(8,128)(2,1)S(1)} all-to-all(bf16[4,12,16,512]{3,2,1,0:T(8,128)(2,1)S(1)} %get-tuple-element.90), channel_id=1, replica_groups=mesh['z'=8,'x'=4,'y'=8,'core'=2] {'x'}, dimensions={0} | all-to-all | bytes 1572864 | tf_op jit(solution)/shard_map/cond/branch_1_fun/all_to_all | solution.py:197
  106.7 1.7 %branch_1_fun.5 = bf16[32,16,512]{2,1,0:T(8,128)(2,1)} custom-call(s32[48]{0:T(128)S(1)} %reshape.82.index_ref, bf16[48,16,512]{2,1,0:T(8,128)(2,1)S(1)} %bitcast.31), custom_call_target="tpu_custom_call" | custom-call | bytes 2097152 | tf_op jit(solution)/shard_map/cond/branch_1_fun/pallas_call | solution.py:135
  108.5 4.1 %all-to-all-start.7 = ((bf16[32,16,512]{2,1,0:T(8,128)(2,1)}), bf16[32,16,512]{2,1,0:T(8,128)(2,1)S(1)}, u32[]{:S(2)}, u32[]{:S(2)}) async-start(bf16[32,16,512]{2,1,0:T(8,128)(2,1)} %get-tuple-element.99), calls=%async_computation.7 | async-start | bytes 1048576 | tf_op jit(solution)/shard_map/all_to_all | solution.py:209
  112.6 0.1 copy.54
  112.7 12.6 %all-to-all-done.7 = bf16[32,16,512]{2,1,0:T(8,128)(2,1)S(1)} async-done(((bf16[32,16,512]{2,1,0:T(8,128)(2,1)}), bf16[32,16,512]{2,1,0:T(8,128)(2,1)S(1)}, u32[]{:S(2)}, u32[]{:S(2)}) %all-to-all-start.7) | async-done | bytes 524320 | tf_op jit(solution)/shard_map/all_to_all | solution.py:209
  125.4 0.1 bitcast_reduce_fusion
  125.4 0.5 convolution_convert_fusion
  126.0 23.8 %all_to_all.49 = bf16[16,4,1280]{2,1,0:T(4,128)(2,1)S(1)} all-to-all(bf16[16,4,1280]{2,1,0:T(4,128)(2,1)S(1)} %reshape.100), channel_id=1, replica_groups=mesh['z'=8,'x'=4,'y'=8,'core'=2] {'y','core'}, dimensions={0} | all-to-all | bytes 327680 | tf_op jit(solution)/shard_map/all_to_all | solution.py:215
  149.8 0.1 reduce_sum.56
  149.9 12.3 %all_to_all.50 = bf16[16,4,1280]{2,1,0:T(4,128)(2,1)S(1)} all-to-all(bf16[16,4,1280]{2,1,0:T(4,128)(2,1)S(1)} %broadcast_in_dim.75), channel_id=1, replica_groups=mesh['z'=8,'x'=4,'y'=8,'core'=2] {'y','core'}, dimensions={0} | all-to-all | bytes 327680 | tf_op jit(solution)/shard_map/all_to_all | solution.py:151
  162.2 0.7 reshape.101
  (19 shorter events, 0.3 us)
Async XLA Ops:
  0.6 15.4 %copy-start = (bf16[1,64,1280]{2,1,0:T(8,128)(2,1)S(1)}, bf16[1,64,1280]{2,1,0:T(8,128)(2,1)}, u32[]{:S(2)}) copy-start(bf16[1,64,1280]{2,1,0:T(8,128)(2,1)} %param.11) | copy-start | bytes 491524
  5.1 25.1 %all-to-all-start.4 = ((bf16[8,48,512]{2,1,0:T(8,128)(2,1)}), bf16[8,48,512]{2,1,0:T(8,128)(2,1)S(1)}, u32[]{:S(2)}, u32[]{:S(2)}) async-start(bf16[8,48,512]{2,1,0:T(8,128)(2,1)} %broadcast_in_dim.70), calls=%async_computation.4 | async-start | bytes 786432 | tf_op jit(solution)/shard_map/all_to_all | solution.py:151
  52.7 4.7 %copy-start.1 = (s32[8,4]{0,1:T(4,128)S(1)}, s32[8,4]{0,1:T(4,128)}, u32[]{:S(2)}) copy-start(s32[8,4]{0,1:T(4,128)} %param.15) | copy-start | bytes 388
  52.7 19.1 %copy-start.2 = (s32[2048]{0:T(1024)S(1)}, s32[2048]{0:T(1024)}, u32[]{:S(2)}) copy-start(s32[2048]{0:T(1024)} %param.17) | copy-start | bytes 24580
  52.7 19.1 %copy-start.3 = (s32[32]{0:T(128)S(1)}, s32[32]{0:T(128)}, u32[]{:S(2)}) copy-start(s32[32]{0:T(128)} %param.16) | copy-start | bytes 388
  53.9 17.9 %all-to-all-start.6 = ((bf16[8,64,512]{2,1,0:T(8,128)(2,1)}), bf16[8,64,512]{2,1,0:T(8,128)(2,1)S(1)}, u32[]{:S(2)}, u32[]{:S(2)}) async-start(bf16[8,64,512]{2,1,0:T(8,128)(2,1)} %broadcast_in_dim.74), calls=%async_computation.6 | async-start | bytes 1048576 | tf_op jit(solution)/shard_map/all_to_all | solution.py:151
  73.7 11.8 %all-to-all-start.2 = ((bf16[4,12,16,512]{3,2,1,0:T(8,128)(2,1)}), bf16[4,12,16,512]{3,2,1,0:T(8,128)(2,1)S(1)}, u32[]{:S(2)}, u32[]{:S(2)}) async-start(bf16[4,12,16,512]{3,2,1,0:T(8,128)(2,1)} %bitcast.4), calls=%async_computation.2 | async-start | bytes 1572864 | tf_op jit(solution)/shard_map/cond/branch_1_fun/all_to_all | solution.py:194
  108.5 16.9 %all-to-all-start.7 = ((bf16[32,16,512]{2,1,0:T(8,128)(2,1)}), bf16[32,16,512]{2,1,0:T(8,128)(2,1)S(1)}, u32[]{:S(2)}, u32[]{:S(2)}) async-start(bf16[32,16,512]{2,1,0:T(8,128)(2,1)} %get-tuple-element.99), calls=%async_computation.7 | async-start | bytes 1048576 | tf_op jit(solution)/shard_map/all_to_all | solution.py:209

commit v6 on v5

--- a/solution.py
+++ b/solution.py
@@ -10,6 +10,7 @@
 LAT = 64
 GROUP = 256
 GROUPS = 8
+BATCH = 2
 SLOTS = 4
 IPD = 4
 NX = 4
@@ -20,6 +21,7 @@
 VIS = 1280
 WROWS = 40
 IMAGES = 32
+TOKENS = 2048
 DOCS = 8
 QUARTER = LAT // NX
 SPAN = 3
@@ -34,27 +36,30 @@
 
 def attention_kernel(src_ref, doc_ref, tok_ref, q_ref, g_ref, kv_ref,
                      att_ref, dq_ref, dkv_ref, acc):
-    group = pl.program_id(0)
-
-    @pl.when(group == 0)
+    step = pl.program_id(0)
+
+    @pl.when(step == 0)
     def _():
         acc[...] = jnp.zeros_like(acc)
 
-    tok = tok_ref[0]
-    src = [src_ref[group, j] for j in range(SLOTS)]
-    bias = [jnp.where(tok == doc_ref[group, j], 0.0, MASKED) for j in range(SLOTS)]
-    bias = jnp.concatenate([jnp.broadcast_to(b, (LAT, GROUP)) for b in bias], axis=0)
-    heads = [head * HEAD for head in range(COLS // HEAD)]
-
-    def rows_of(lo):
+    src = [[src_ref[step * BATCH + i, j] for j in range(SLOTS)] for i in range(BATCH)]
+    bias = [
+        [jnp.where(tok_ref[i] == doc_ref[step * BATCH + i, j], 0.0, MASKED) for j in range(SLOTS)]
+        for i in range(BATCH)
+    ]
+    units = [(i, head * HEAD) for i in range(BATCH) for head in range(COLS // HEAD)]
+    tokens = [slice(i * GROUP, (i + 1) * GROUP) for i in range(BATCH)]
+    of_slot = [slice(j * LAT, (j + 1) * LAT) for j in range(SLOTS)]
+
+    def rows_of(i, lo):
         return jnp.concatenate(
-            [kv_ref[part, r, :, lo:lo + HEAD] for r in src for part in range(NX)], axis=0
+            [kv_ref[part, r, :, lo:lo + HEAD] for r in src[i] for part in range(NX)], axis=0
         )
 
-    keys = [rows_of(lo) for lo in heads]
-    values = [rows_of(COLS + lo) for lo in heads]
-    queries = [q_ref[:, lo:lo + HEAD] for lo in heads]
-    grads = [g_ref[:, lo:lo + HEAD] for lo in heads]
+    keys = [rows_of(i, lo) for i, lo in units]
+    values = [rows_of(i, COLS + lo) for i, lo in units]
+    queries = [q_ref[tokens[i], lo:lo + HEAD] for i, lo in units]
+    grads = [g_ref[tokens[i], lo:lo + HEAD] for i, lo in units]
     scores = [
         lax.dot_general(k, q, NT_DIMS, preferred_element_type=jnp.float32)
         for k, q in zip(keys, queries)
@@ -64,27 +69,27 @@
         for v, g in zip(values, grads)
     ]
     lows, score_grads = [], []
-    for s, dp in zip(scores, prob_grads):
-        s = s + bias
+    for (i, _), s, dp in zip(units, scores, prob_grads):
+        s = jnp.concatenate([s[of_slot[j]] + bias[i][j] for j in range(SLOTS)], axis=0)
         top = jnp.max(s, axis=0, keepdims=True)
         e = jnp.exp2((s - top) * (SCALE * LOG2E))
-        p = e * (1.0 / jnp.sum(e, axis=0, keepdims=True))
+        inverse = 1.0 / jnp.sum(e, axis=0, keepdims=True)
+        centre = jnp.sum(e * dp, axis=0, keepdims=True) * inverse
+        p = e * inverse
         lows.append(p.astype(jnp.bfloat16))
-        centre = jnp.sum(p * dp, axis=0, keepdims=True)
         score_grads.append((p * (dp - centre) * SCALE).astype(jnp.bfloat16))
-    for i, lo in enumerate(heads):
-        att = lax.dot_general(lows[i], values[i], TN_DIMS, preferred_element_type=jnp.float32)
-        dq = lax.dot_general(score_grads[i], keys[i], TN_DIMS, preferred_element_type=jnp.float32)
-        att_ref[:, lo:lo + HEAD] = att.astype(jnp.bfloat16)
-        dq_ref[:, lo:lo + HEAD] = dq.astype(jnp.bfloat16)
-        dk = jnp.dot(score_grads[i], queries[i], preferred_element_type=jnp.float32)
-        dv = jnp.dot(lows[i], grads[i], preferred_element_type=jnp.float32)
+    for u, (i, lo) in enumerate(units):
+        att = lax.dot_general(lows[u], values[u], TN_DIMS, preferred_element_type=jnp.float32)
+        dq = lax.dot_general(score_grads[u], keys[u], TN_DIMS, preferred_element_type=jnp.float32)
+        att_ref[tokens[i], lo:lo + HEAD] = att.astype(jnp.bfloat16)
+        dq_ref[tokens[i], lo:lo + HEAD] = dq.astype(jnp.bfloat16)
+        dk = jnp.dot(score_grads[u], queries[u], preferred_element_type=jnp.float32)
+        dv = jnp.dot(lows[u], grads[u], preferred_element_type=jnp.float32)
         for j in range(SLOTS):
-            rows = slice(j * LAT, (j + 1) * LAT)
-            acc[src[j], :, lo:lo + HEAD] += dk[rows]
-            acc[src[j], :, COLS + lo:COLS + lo + HEAD] += dv[rows]
-
-    @pl.when(group == GROUPS - 1)
+            acc[src[i][j], :, lo:lo + HEAD] += dk[of_slot[j]]
+            acc[src[i][j], :, COLS + lo:COLS + lo + HEAD] += dv[of_slot[j]]
+
+    @pl.when(step == GROUPS // BATCH - 1)
     def _():
         for part in range(NX):
             rows = slice(part * QUARTER, (part + 1) * QUARTER)
@@ -94,14 +99,14 @@
 def attention(src, docs, tok, queries, grad_out, kv):
     tokens = queries.shape[0]
     held = kv.shape[1]
-    block = pl.BlockSpec((GROUP, COLS), lambda g, *_: (g, 0))
+    block = pl.BlockSpec((BATCH * GROUP, COLS), lambda g, *_: (g, 0))
     whole = pl.BlockSpec((NX, held, QUARTER, WIDE), lambda g, *_: (0, 0, 0, 0))
     return pl.pallas_call(
         attention_kernel,
         grid_spec=pltpu.PrefetchScalarGridSpec(
             num_scalar_prefetch=2,
-            grid=(GROUPS,),
-            in_specs=[pl.BlockSpec((1, 1, GROUP), lambda g, *_: (g, 0, 0)), block, block, whole],
+            grid=(GROUPS // BATCH,),
+            in_specs=[pl.BlockSpec((BATCH, 1, GROUP), lambda g, *_: (g, 0, 0)), block, block, whole],
             out_specs=[block, block, whole],
             scratch_shapes=[pltpu.VMEM((held, LAT, WIDE), jnp.float32)],
         ),
@@ -158,34 +163,32 @@
 
 def local(queries, latents, key_weight, value_weight, grad_out, pairs, image_slot, token_doc):
     z = lax.axis_index("z")
-    low_doc, high_doc = jnp.min(token_doc), jnp.max(token_doc)
-    start = jnp.minimum(low_doc, DOCS - SPAN)
-    note = jnp.stack([start, high_doc - start + 1]).astype(jnp.bfloat16)
-
+
+    tok = token_doc.reshape(TOKENS // WIDE, WIDE)
+    note = jnp.stack([jnp.min(tok, axis=0), jnp.max(tok, axis=0)]).astype(jnp.bfloat16)
     weight = jnp.concatenate([key_weight, value_weight], axis=1)
-    extra = jnp.broadcast_to(jnp.tile(note, COLS)[None], (8, WIDE))
-    column = gather(jnp.concatenate([weight, extra]), "z", NZ)
-    notes = column[:, WROWS, :2].reshape(2 * NZ)
+    column = jnp.concatenate([weight, jnp.pad(note, ((0, 6), (0, 0)))])
+    column = gather(column, "z", NZ)
+    notes = column[:, WROWS:WROWS + 2].reshape(2 * NZ, WIDE)
+
     column = column[:, :WROWS].reshape(NZ * WROWS, WIDE)
-
-    own = latents[0].reshape(LAT, NZ, NX, WROWS).transpose(0, 2, 1, 3).reshape(NX, QUARTER, VIS)
-    notes = jnp.broadcast_to(jnp.tile(notes, COLS // (2 * NZ)), (NX, QUARTER, COLS))
-    own = jnp.concatenate([own, notes], axis=2)
-    sent = [jnp.broadcast_to(column[None], (NX,) + column.shape)]
-    sent += [own[:, :, i * WIDE:(i + 1) * WIDE] for i in range(3)]
-    row = lax.all_to_all(jnp.concatenate(sent, axis=1), "x", 0, 0, tiled=True)
-    tall = NZ * WROWS
-    weight = row[:, :tall].reshape(VIS, WIDE)
-    images = [row[:, tall + i * QUARTER:tall + (i + 1) * QUARTER] for i in range(3)]
-    images = jnp.concatenate(images, axis=2).reshape(LAT, 3 * WIDE)
-    notes = row[:, tall + 2 * QUARTER, COLS:COLS + 2 * NZ].reshape(NX, NZ, 2).astype(jnp.int32)
-
-    kv = jnp.dot(images[:, :VIS], weight, preferred_element_type=jnp.float32).astype(jnp.bfloat16)
-    kv = gather(kv, "z", NZ).reshape(IMAGES, QUARTER, WIDE)
+    row = gather(jnp.concatenate([column, notes]), "x", NX)
+    weight = row[:, :NZ * WROWS].reshape(VIS, WIDE)
+    notes = row[:, NZ * WROWS:].reshape(NX, NZ, 2, WIDE)
+    low_doc = jnp.min(notes[:, :, 0], axis=-1).astype(jnp.int32)
+    high_doc = jnp.max(notes[:, :, 1], axis=-1).astype(jnp.int32)
+    starts = jnp.minimum(low_doc, DOCS - SPAN)
+    fits = jnp.max(high_doc - starts) < SPAN
+
+    own = latents[0].reshape(LAT, NZ, NX, WROWS).transpose(0, 2, 1, 3).reshape(LAT, VIS)
+    kv = jnp.dot(own, weight, preferred_element_type=jnp.float32).astype(jnp.bfloat16)
+    kv = jnp.broadcast_to(kv.reshape(1, NX, QUARTER, WIDE), (NZ, NX, QUARTER, WIDE))
+    kv = lax.all_to_all(kv.reshape(IMAGES, QUARTER, WIDE), ("z", "x"), 0, 0, tiled=True)
 
     docs = jnp.where(pairs >= 0, pairs // IPD, -1)
     tok = token_doc.reshape(GROUPS, 1, GROUP)
-    starts = lax.dynamic_index_in_dim(notes[:, :, 0], z, axis=1, keepdims=False)
+    starts = lax.dynamic_index_in_dim(starts, z, axis=1, keepdims=False)
+    start = lax.dynamic_index_in_dim(starts, lax.axis_index("x"), keepdims=False)
     wanted = starts[:, None] * IPD + jnp.arange(WINDOW, dtype=jnp.int32)
     wanted = lookup(image_slot, wanted).reshape(NX * WINDOW)
 
@@ -204,7 +207,7 @@
         dkv = lax.all_to_all(dkv, "x", 0, 0, tiled=True)
         return att, dq, jnp.sum(dkv.astype(jnp.float32), axis=0).astype(jnp.bfloat16)
 
-    attended, grad_queries, dkv = lax.cond(jnp.max(notes[:, :, 1]) <= SPAN, narrow, full)
+    attended, grad_queries, dkv = lax.cond(fits, narrow, full)
 
     dkv = lax.all_to_all(dkv, ("z", "x"), 0, 0, tiled=True).reshape(NZ, LAT, WIDE)
     dkv = jnp.sum(dkv.astype(jnp.float32), axis=0).astype(jnp.bfloat16)

time: 164 us -> 160 us (0.976)
  starting transfers between devices: 21.9 us -> 18.1 us
  waiting for transfers between devices: 46.2 us -> 48.4 us
  Pallas kernels: 13.7 us -> 11.7 us
  blocking collectives: 68.6 us -> 70.4 us
    all_to_all x1 -> x2, blocking collectives: 12.3 us -> 36.5 us  [gather(): return lax.all_to_all(copies, axis, 0, 0, tiled=True)]
    all_to_all x1 -> x0, blocking collectives: 21.8 us -> none  [local(): row = lax.all_to_all(jnp.concatenate(sent, axis=1), 'x', 0, 0, tiled=True)]
    all_to_all x0 -> x1, waiting for transfers between devices: none -> 12.7 us  [local(): lax.all_to_all(kv.reshape(IMAGES, QUARTER, WIDE), ('z', 'x'), 0, 0, tiled...]
    all_to_all x2 -> x1, starting transfers between devices: 14.4 us -> 4.14 us  [gather(): return lax.all_to_all(copies, axis, 0, 0, tiled=True)]
    all_to_all x2 -> x1, waiting for transfers between devices: 25.3 us -> 16 us  [gather(): return lax.all_to_all(copies, axis, 0, 0, tiled=True)]
    all_to_all x0 -> x1, starting transfers between devices: none -> 4.75 us  [local(): lax.all_to_all(kv.reshape(IMAGES, QUARTER, WIDE), ('z', 'x'), 0, 0, tiled...]
    pallas_call x1, Pallas kernels: 10.5 us -> 8.43 us  [attention(): pl.pallas_call(attention_kernel, grid_spec=pltpu.PrefetchScalarGridSpec(n...]
  transfers between devices with their start and end apart: 4 -> 4, of which waited for: 4 -> 4; matrix products, arithmetic and copies ran while one was open for 2% -> 1% of each run, Pallas kernels for 0% -> 0%
where the time goes in v6:
time: 160 us; the launch traced here: 159 us
  blocking collectives  70.4 us (44%)
  waiting for transfers between devices  48.4 us (30%)
  starting transfers between devices  18.1 us (11%)
  Pallas kernels  11.7 us (7%)
  local copies, waits for them, and re-layouts  5.1 us (3%)
  other arithmetic  2.21 us (1%)
    all_to_all x2, blocking collectives, gather(): return lax.all_to_all(copies, axis, 0, 0, tiled=True)  36.5 us
    all_to_all x1, blocking collectives, local(): term = lax.all_to_all(term, ('y', 'core'), 0, 0, tiled=True)  23.2 us
    all_to_all x1, waiting for transfers between devices, gather(): return lax.all_to_all(copies, axis, 0, 0, tiled=True)  16 us
    all_to_all x1, waiting for transfers between devices, local(): lax.all_to_all(kv.reshape(IMAGES, QUARTER, WIDE), ('z', 'x'), 0, 0, tiled...  12.7 us
    all_to_all x1, waiting for transfers between devices, local(): lax.all_to_all(dkv, ('z', 'x'), 0, 0, tiled=True).reshape(NZ, LAT, WIDE)  12.7 us
    all_to_all x1, blocking collectives, narrow(): lax.all_to_all(dkv, 'x', 0, 0, tiled=True)  10.7 us
    pallas_call x1, Pallas kernels, attention(): pl.pallas_call(attention_kernel, grid_spec=pltpu.PrefetchScalarGridSpec(n...  8.43 us
    all_to_all x1, waiting for transfers between devices, narrow(): lax.all_to_all(picked.reshape(NX, WINDOW, QUARTER, WIDE), 'x', 0, 0, tile...  7.01 us
  transfers between devices with their start and end apart: 4, of which 4 were waited for; matrix products, arithmetic and copies ran while one was open for 1% of the time, Pallas kernels for 0%

profile of v6, /device:TPU:1, one launch (start us, length us, event | category | flops | bytes accessed | tf_op | source)
XLA Modules:
  0.0 159.0 jit_solution(18340033839050977942)
XLA Ops:
  0.6 0.7 reshape.73
  1.4 0.8 pad_maximum_fusion.1
  2.2 24.2 %all_to_all.48 = bf16[8,48,512]{2,1,0:T(8,128)(2,1)S(1)} all-to-all(bf16[8,48,512]{2,1,0:T(8,128)(2,1)S(1)} %broadcast_in_dim.38), channel_id=1, replica_groups=mesh['z'=8,'x'=4,'y'=8,'core'=2] {'z'}, dimensions={0} | all-to-all | bytes 786432 | tf_op jit(solution)/shard_map/all_to_all | solution.py:156
  26.5 1.2 broadcast_in_dim.39
  27.7 0.0 copy-start
  27.7 4.1 %all-to-all-start.5 = ((bf16[4,336,512]{2,1,0:T(8,128)(2,1)}), bf16[4,336,512]{2,1,0:T(8,128)(2,1)S(1)}, u32[]{:S(2)}, u32[]{:S(2)}) async-start(bf16[4,336,512]{2,1,0:T(8,128)(2,1)} %broadcast_in_dim.39), calls=%async_computation.5 | async-start | bytes 2752512 | tf_op jit(solution)/shard_map/all_to_all | solution.py:156
  31.8 0.0 copy-done
  31.8 0.2 copy.49
  32.1 16.0 %all-to-all-done.5 = bf16[4,336,512]{2,1,0:T(8,128)(2,1)S(1)} async-done(((bf16[4,336,512]{2,1,0:T(8,128)(2,1)}), bf16[4,336,512]{2,1,0:T(8,128)(2,1)S(1)}, u32[]{:S(2)}, u32[]{:S(2)}) %all-to-all-start.5) | async-done | bytes 1376288 | tf_op jit(solution)/shard_map/all_to_all | solution.py:156
  48.1 0.1 slice.29
  48.2 0.0 copy-start.1
  48.2 0.4 convolution_convert_fusion.1
  48.6 0.0 copy-start.2
  48.6 0.0 copy-start.3
  48.6 0.9 broadcast_in_dim.60
  49.5 4.7 %all-to-all-start.6 = ((bf16[32,16,512]{2,1,0:T(8,128)(2,1)}), bf16[32,16,512]{2,1,0:T(8,128)(2,1)S(1)}, u32[]{:S(2)}, u32[]{:S(2)}) async-start(bf16[32,16,512]{2,1,0:T(8,128)(2,1)} %bitcast.33), calls=%async_computation.6 | async-start | bytes 1048576 | tf_op jit(solution)/shard_map/all_to_all | solution.py:186
  54.2 0.0 copy-done.1
  54.2 0.1 copy.51
  54.4 0.3 slice_reduce_fusion
  54.6 0.6 convert_minimum_fusion
  55.9 12.7 %all-to-all-done.6 = bf16[32,16,512]{2,1,0:T(8,128)(2,1)S(1)} async-done(((bf16[32,16,512]{2,1,0:T(8,128)(2,1)}), bf16[32,16,512]{2,1,0:T(8,128)(2,1)S(1)}, u32[]{:S(2)}, u32[]{:S(2)}) %all-to-all-start.6) | async-done | bytes 524320 | tf_op jit(solution)/shard_map/all_to_all | solution.py:186
  68.7 0.0 copy-done.2
  68.7 0.0 copy-done.3
  68.7 35.0 %conditional.1 = (bf16[2048,256]{1,0:T(8,128)(2,1)}, bf16[2048,256]{1,0:T(8,128)(2,1)}, bf16[32,16,512]{2,1,0:T(8,128)(2,1)}) conditional(s32[]{:T(128)} %convert_element_type.29, (s32[8,4]{0,1:T(4,128)S(1)}, s32[32]{0:T(128)S(1)}, bf16[32,16,512]{2,1,0:T(8,128)(2,1)S(1)}, s32[8,4]{1,0:T(8,128)S(1)}, s32[8,1,256]{2,1,0:T(1,128)S(1)}, ...), branch_computations={%region_5.8_spmd, %region_8.10_spmd} | conditional | flops 1611402240 | bytes 25166522 | solution.py:210
  68.7 0.1 copy.56
  68.8 0.1 add_bitcast_fusion
  68.9 0.2 select_reduce_fusion.1
  69.1 0.1 reshape.58.index_ref
  69.2 1.5 branch_1_fun.3
  70.7 3.7 %all-to-all-start.2 = ((bf16[4,12,16,512]{3,2,1,0:T(8,128)(2,1)}), bf16[4,12,16,512]{3,2,1,0:T(8,128)(2,1)S(1)}, u32[]{:S(2)}, u32[]{:S(2)}) async-start(bf16[4,12,16,512]{3,2,1,0:T(8,128)(2,1)} %bitcast.3), calls=%async_computation.2 | async-start | bytes 1572864 | tf_op jit(solution)/shard_map/cond/branch_1_fun/all_to_all | solution.py:197
  74.4 0.1 copy.57
  74.5 0.6 dynamic_slice.12
  75.7 7.0 %all-to-all-done.2.kv_ref = bf16[4,12,16,512]{3,2,1,0:T(8,128)(2,1)S(1)} async-done(((bf16[4,12,16,512]{3,2,1,0:T(8,128)(2,1)}), bf16[4,12,16,512]{3,2,1,0:T(8,128)(2,1)S(1)}, u32[]{:S(2)}, u32[]{:S(2)}) %all-to-all-start.2) | async-done | bytes 786464 | tf_op jit(solution)/shard_map/cond/branch_1_fun/all_to_all | solution.py:197
  82.8 8.4 %branch_1_fun.4 = (bf16[2048,256]{1,0:T(8,128)(2,1)}, bf16[2048,256]{1,0:T(8,128)(2,1)}, bf16[4,12,16,512]{3,2,1,0:T(8,128)(2,1)S(1)}) custom-call(s32[8,4]{1,0:T(8,128)S(1)} %subtract_clamp_fusion.src_ref, s32[8,4]{1,0:T(8,128)S(1)} %get-tuple-element.98.doc_ref, s32[8,1,256]{2,1,0:T(1,128)S(1)} %get-tuple-element.99.tok_ref, ...), custom_call_target="tpu_custom_call" | custom-call | flops 1610612736 | bytes 9437184 | tf_op jit(solution)/shard_map/cond/branch_1_fun/pallas_call | solution.py:104
  91.2 10.7 %all_to_all.47 = bf16[4,12,16,512]{3,2,1,0:T(8,128)(2,1)S(1)} all-to-all(bf16[4,12,16,512]{3,2,1,0:T(8,128)(2,1)S(1)} %get-tuple-element.108), channel_id=1, replica_groups=mesh['z'=8,'x'=4,'y'=8,'core'=2] {'x'}, dimensions={0} | all-to-all | bytes 1572864 | tf_op jit(solution)/shard_map/cond/branch_1_fun/all_to_all | solution.py:200
  101.9 1.7 %branch_1_fun.5 = bf16[32,16,512]{2,1,0:T(8,128)(2,1)} custom-call(s32[48]{0:T(128)S(1)} %reshape.58.index_ref, bf16[48,16,512]{2,1,0:T(8,128)(2,1)S(1)} %bitcast.29), custom_call_target="tpu_custom_call" | custom-call | bytes 2097152 | tf_op jit(solution)/shard_map/cond/branch_1_fun/pallas_call | solution.py:140
  103.7 5.5 %all-to-all-start.7 = ((bf16[32,16,512]{2,1,0:T(8,128)(2,1)}), bf16[32,16,512]{2,1,0:T(8,128)(2,1)S(1)}, u32[]{:S(2)}, u32[]{:S(2)}) async-start(bf16[32,16,512]{2,1,0:T(8,128)(2,1)} %get-tuple-element.117), calls=%async_computation.7 | async-start | bytes 1048576 | tf_op jit(solution)/shard_map/all_to_all | solution.py:212
  109.1 0.1 copy.58
  109.3 12.7 %all-to-all-done.7 = bf16[32,16,512]{2,1,0:T(8,128)(2,1)S(1)} async-done(((bf16[32,16,512]{2,1,0:T(8,128)(2,1)}), bf16[32,16,512]{2,1,0:T(8,128)(2,1)S(1)}, u32[]{:S(2)}, u32[]{:S(2)}) %all-to-all-start.7) | async-done | bytes 524320 | tf_op jit(solution)/shard_map/all_to_all | solution.py:212
  122.0 0.1 bitcast_reduce_fusion
  122.1 0.5 convolution_convert_fusion
  122.6 23.2 %all_to_all.49 = bf16[16,4,1280]{2,1,0:T(4,128)(2,1)S(1)} all-to-all(bf16[16,4,1280]{2,1,0:T(4,128)(2,1)S(1)} %reshape.83), channel_id=1, replica_groups=mesh['z'=8,'x'=4,'y'=8,'core'=2] {'y','core'}, dimensions={0} | all-to-all | bytes 327680 | tf_op jit(solution)/shard_map/all_to_all | solution.py:218
  145.9 0.1 reduce_sum.56
  146.0 12.3 %all_to_all.50 = bf16[16,4,1280]{2,1,0:T(4,128)(2,1)S(1)} all-to-all(bf16[16,4,1280]{2,1,0:T(4,128)(2,1)S(1)} %broadcast_in_dim.61), channel_id=1, replica_groups=mesh['z'=8,'x'=4,'y'=8,'core'=2] {'y','core'}, dimensions={0} | all-to-all | bytes 327680 | tf_op jit(solution)/shard_map/all_to_all | solution.py:156
  158.3 0.7 reshape.84
  (21 shorter events, 0.4 us)
Async XLA Ops:
  27.7 4.1 %copy-start = (bf16[1,64,1280]{2,1,0:T(8,128)(2,1)S(1)}, bf16[1,64,1280]{2,1,0:T(8,128)(2,1)}, u32[]{:S(2)}) copy-start(bf16[1,64,1280]{2,1,0:T(8,128)(2,1)} %param.11) | copy-start | bytes 491524
  27.7 20.4 %all-to-all-start.5 = ((bf16[4,336,512]{2,1,0:T(8,128)(2,1)}), bf16[4,336,512]{2,1,0:T(8,128)(2,1)S(1)}, u32[]{:S(2)}, u32[]{:S(2)}) async-start(bf16[4,336,512]{2,1,0:T(8,128)(2,1)} %broadcast_in_dim.39), calls=%async_computation.5 | async-start | bytes 2752512 | tf_op jit(solution)/shard_map/all_to_all | solution.py:156
  48.2 6.0 %copy-start.1 = (s32[8,4]{0,1:T(4,128)S(1)}, s32[8,4]{0,1:T(4,128)}, u32[]{:S(2)}) copy-start(s32[8,4]{0,1:T(4,128)} %param.15) | copy-start | bytes 388
  48.6 20.1 %copy-start.2 = (s32[2048]{0:T(1024)S(1)}, s32[2048]{0:T(1024)}, u32[]{:S(2)}) copy-start(s32[2048]{0:T(1024)} %param.17) | copy-start | bytes 24580
  48.6 20.1 %copy-start.3 = (s32[32]{0:T(128)S(1)}, s32[32]{0:T(128)}, u32[]{:S(2)}) copy-start(s32[32]{0:T(128)} %param.16) | copy-start | bytes 388
  49.5 19.2 %all-to-all-start.6 = ((bf16[32,16,512]{2,1,0:T(8,128)(2,1)}), bf16[32,16,512]{2,1,0:T(8,128)(2,1)S(1)}, u32[]{:S(2)}, u32[]{:S(2)}) async-start(bf16[32,16,512]{2,1,0:T(8,128)(2,1)} %bitcast.33), calls=%async_computation.6 | async-start | bytes 1048576 | tf_op jit(solution)/shard_map/all_to_all | solution.py:186
  70.7 12.1 %all-to-all-start.2 = ((bf16[4,12,16,512]{3,2,1,0:T(8,128)(2,1)}), bf16[4,12,16,512]{3,2,1,0:T(8,128)(2,1)S(1)}, u32[]{:S(2)}, u32[]{:S(2)}) async-start(bf16[4,12,16,512]{3,2,1,0:T(8,128)(2,1)} %bitcast.3), calls=%async_computation.2 | async-start | bytes 1572864 | tf_op jit(solution)/shard_map/cond/branch_1_fun/all_to_all | solution.py:197
  103.7 18.3 %all-to-all-start.7 = ((bf16[32,16,512]{2,1,0:T(8,128)(2,1)}), bf16[32,16,512]{2,1,0:T(8,128)(2,1)S(1)}, u32[]{:S(2)}, u32[]{:S(2)}) async-start(bf16[32,16,512]{2,1,0:T(8,128)(2,1)} %get-tuple-element.117), calls=%async_computation.7 | async-start | bytes 1048576 | tf_op jit(solution)/shard_map/all_to_all | solution.py:212

commit v7 on v6

--- a/solution.py
+++ b/solution.py
@@ -11,6 +11,7 @@
 GROUP = 256
 GROUPS = 8
 BATCH = 2
+HEADS = 2
 SLOTS = 4
 IPD = 4
 NX = 4
@@ -34,8 +35,14 @@
 TN_DIMS = (((0,), (0,)), ((), ()))
 
 
+def rows_of(kv_ref, places, lo):
+    return jnp.concatenate(
+        [kv_ref[part, r, :, lo:lo + HEAD] for r in places for part in range(NX)], axis=0
+    )
+
+
 def attention_kernel(src_ref, doc_ref, tok_ref, q_ref, g_ref, kv_ref,
-                     att_ref, dq_ref, dkv_ref, acc):
+                     low_ref, sg_ref, dkv_ref, acc):
     step = pl.program_id(0)
 
     @pl.when(step == 0)
@@ -51,13 +58,8 @@
     tokens = [slice(i * GROUP, (i + 1) * GROUP) for i in range(BATCH)]
     of_slot = [slice(j * LAT, (j + 1) * LAT) for j in range(SLOTS)]
 
-    def rows_of(i, lo):
-        return jnp.concatenate(
-            [kv_ref[part, r, :, lo:lo + HEAD] for r in src[i] for part in range(NX)], axis=0
-        )
-
-    keys = [rows_of(i, lo) for i, lo in units]
-    values = [rows_of(i, COLS + lo) for i, lo in units]
+    keys = [rows_of(kv_ref, src[i], lo) for i, lo in units]
+    values = [rows_of(kv_ref, src[i], COLS + lo) for i, lo in units]
     queries = [q_ref[tokens[i], lo:lo + HEAD] for i, lo in units]
     grads = [g_ref[tokens[i], lo:lo + HEAD] for i, lo in units]
     scores = [
@@ -79,10 +81,8 @@
         lows.append(p.astype(jnp.bfloat16))
         score_grads.append((p * (dp - centre) * SCALE).astype(jnp.bfloat16))
     for u, (i, lo) in enumerate(units):
-        att = lax.dot_general(lows[u], values[u], TN_DIMS, preferred_element_type=jnp.float32)
-        dq = lax.dot_general(score_grads[u], keys[u], TN_DIMS, preferred_element_type=jnp.float32)
-        att_ref[tokens[i], lo:lo + HEAD] = att.astype(jnp.bfloat16)
-        dq_ref[tokens[i], lo:lo + HEAD] = dq.astype(jnp.bfloat16)
+        low_ref[i, lo // HEAD] = lows[u]
+        sg_ref[i, lo // HEAD] = score_grads[u]
         dk = jnp.dot(score_grads[u], queries[u], preferred_element_type=jnp.float32)
         dv = jnp.dot(lows[u], grads[u], preferred_element_type=jnp.float32)
         for j in range(SLOTS):
@@ -96,32 +96,71 @@
             dkv_ref[part] = acc[:, rows, :].astype(jnp.bfloat16)
 
 
+def output_kernel(src_ref, low_ref, sg_ref, kv_ref, att_ref, dq_ref):
+    step = pl.program_id(0)
+    for i in range(BATCH):
+        src = [src_ref[step * BATCH + i, j] for j in range(SLOTS)]
+        rows = slice(i * GROUP, (i + 1) * GROUP)
+        for head in range(HEADS):
+            lo = head * HEAD
+            keys = rows_of(kv_ref, src, lo)
+            values = rows_of(kv_ref, src, COLS + lo)
+            att = lax.dot_general(low_ref[i, head], values, TN_DIMS, preferred_element_type=jnp.float32)
+            dq = lax.dot_general(sg_ref[i, head], keys, TN_DIMS, preferred_element_type=jnp.float32)
+            att_ref[rows, lo:lo + HEAD] = att.astype(jnp.bfloat16)
+            dq_ref[rows, lo:lo + HEAD] = dq.astype(jnp.bfloat16)
+
+
+def blocks(held):
+    tokens = pl.BlockSpec((BATCH * GROUP, COLS), lambda g, *_: (g, 0))
+    square = pl.BlockSpec((BATCH, HEADS, SLOTS * LAT, GROUP), lambda g, *_: (g, 0, 0, 0))
+    whole = pl.BlockSpec((NX, held, QUARTER, WIDE), lambda g, *_: (0, 0, 0, 0))
+    return tokens, square, whole
+
+
+PARAMS = pltpu.CompilerParams(
+    dimension_semantics=("arbitrary",), vmem_limit_bytes=40 * 2**20
+)
+
+
 def attention(src, docs, tok, queries, grad_out, kv):
-    tokens = queries.shape[0]
     held = kv.shape[1]
-    block = pl.BlockSpec((BATCH * GROUP, COLS), lambda g, *_: (g, 0))
-    whole = pl.BlockSpec((NX, held, QUARTER, WIDE), lambda g, *_: (0, 0, 0, 0))
+    tokens, square, whole = blocks(held)
+    weights = jax.ShapeDtypeStruct((GROUPS, HEADS, SLOTS * LAT, GROUP), jnp.bfloat16)
     return pl.pallas_call(
         attention_kernel,
         grid_spec=pltpu.PrefetchScalarGridSpec(
             num_scalar_prefetch=2,
             grid=(GROUPS // BATCH,),
-            in_specs=[pl.BlockSpec((BATCH, 1, GROUP), lambda g, *_: (g, 0, 0)), block, block, whole],
-            out_specs=[block, block, whole],
+            in_specs=[pl.BlockSpec((BATCH, 1, GROUP), lambda g, *_: (g, 0, 0)), tokens, tokens, whole],
+            out_specs=[square, square, whole],
             scratch_shapes=[pltpu.VMEM((held, LAT, WIDE), jnp.float32)],
         ),
-        out_shape=[
-            jax.ShapeDtypeStruct((tokens, COLS), jnp.bfloat16),
-            jax.ShapeDtypeStruct((tokens, COLS), jnp.bfloat16),
-            jax.ShapeDtypeStruct((NX, held, QUARTER, WIDE), jnp.bfloat16),
-        ],
-        compiler_params=pltpu.CompilerParams(
-            dimension_semantics=("arbitrary",), vmem_limit_bytes=40 * 2**20
-        ),
+        out_shape=[weights, weights, jax.ShapeDtypeStruct(kv.shape, jnp.bfloat16)],
+        compiler_params=PARAMS,
         cost_estimate=pl.CostEstimate(
-            flops=12 * tokens * GROUP * COLS, bytes_accessed=9 * 2**20, transcendentals=0
+            flops=8 * TOKENS * GROUP * COLS, bytes_accessed=9 * 2**20, transcendentals=0
         ),
     )(src, docs, tok, queries, grad_out, kv)
+
+
+def outputs(src, low, score_grad, kv):
+    tokens, square, whole = blocks(kv.shape[1])
+    out = jax.ShapeDtypeStruct((TOKENS, COLS), jnp.bfloat16)
+    return pl.pallas_call(
+        output_kernel,
+        grid_spec=pltpu.PrefetchScalarGridSpec(
+            num_scalar_prefetch=1,
+            grid=(GROUPS // BATCH,),
+            in_specs=[square, square, whole],
+            out_specs=[tokens, tokens],
+        ),
+        out_shape=[out, out],
+        compiler_params=PARAMS,
+        cost_estimate=pl.CostEstimate(
+            flops=4 * TOKENS * GROUP * COLS, bytes_accessed=8 * 2**20, transcendentals=0
+        ),
+    )(src, low, score_grad, kv)
 
 
 def pick_kernel(index_ref, all_ref, out_ref):
@@ -162,23 +201,16 @@
 
 
 def local(queries, latents, key_weight, value_weight, grad_out, pairs, image_slot, token_doc):
-    z = lax.axis_index("z")
+    weight = jnp.concatenate([key_weight, value_weight], axis=1)
+    column = gather(weight, "z", NZ).reshape(NZ * WROWS, WIDE)
 
     tok = token_doc.reshape(TOKENS // WIDE, WIDE)
     note = jnp.stack([jnp.min(tok, axis=0), jnp.max(tok, axis=0)]).astype(jnp.bfloat16)
-    weight = jnp.concatenate([key_weight, value_weight], axis=1)
-    column = jnp.concatenate([weight, jnp.pad(note, ((0, 6), (0, 0)))])
-    column = gather(column, "z", NZ)
-    notes = column[:, WROWS:WROWS + 2].reshape(2 * NZ, WIDE)
-
-    column = column[:, :WROWS].reshape(NZ * WROWS, WIDE)
-    row = gather(jnp.concatenate([column, notes]), "x", NX)
+    row = gather(jnp.concatenate([column, jnp.pad(note, ((0, 6), (0, 0)))]), "x", NX)
     weight = row[:, :NZ * WROWS].reshape(VIS, WIDE)
-    notes = row[:, NZ * WROWS:].reshape(NX, NZ, 2, WIDE)
-    low_doc = jnp.min(notes[:, :, 0], axis=-1).astype(jnp.int32)
-    high_doc = jnp.max(notes[:, :, 1], axis=-1).astype(jnp.int32)
-    starts = jnp.minimum(low_doc, DOCS - SPAN)
-    fits = jnp.max(high_doc - starts) < SPAN
+    notes = row[:, NZ * WROWS:NZ * WROWS + 2]
+    starts = jnp.minimum(jnp.min(notes[:, 0], axis=-1).astype(jnp.int32), DOCS - SPAN)
+    fits = jnp.max(jnp.max(notes[:, 1], axis=-1).astype(jnp.int32) - starts) < SPAN
 
     own = latents[0].reshape(LAT, NZ, NX, WROWS).transpose(0, 2, 1, 3).reshape(LAT, VIS)
     kv = jnp.dot(own, weight, preferred_element_type=jnp.float32).astype(jnp.bfloat16)
@@ -187,7 +219,6 @@
 
     docs = jnp.where(pairs >= 0, pairs // IPD, -1)
     tok = token_doc.reshape(GROUPS, 1, GROUP)
-    starts = lax.dynamic_index_in_dim(starts, z, axis=1, keepdims=False)
     start = lax.dynamic_index_in_dim(starts, lax.axis_index("x"), keepdims=False)
     wanted = starts[:, None] * IPD + jnp.arange(WINDOW, dtype=jnp.int32)
     wanted = lookup(image_slot, wanted).reshape(NX * WINDOW)
@@ -196,14 +227,17 @@
         picked = by_index(pick_kernel, wanted, kv, NX * WINDOW, [])
         held = lax.all_to_all(picked.reshape(NX, WINDOW, QUARTER, WIDE), "x", 0, 0, tiled=True)
         src = jnp.clip(pairs - start * IPD, 0, WINDOW - 1)
-        att, dq, dkv = attention(src, docs, tok, queries, grad_out, held)
+        low, score_grad, dkv = attention(src, docs, tok, queries, grad_out, held)
         dkv = lax.all_to_all(dkv, "x", 0, 0, tiled=True).reshape(NX * WINDOW, QUARTER, WIDE)
+        att, dq = outputs(src, low, score_grad, held)
         total = pltpu.VMEM((IMAGES, QUARTER, WIDE), jnp.float32)
         return att, dq, by_index(add_kernel, wanted, dkv, IMAGES, [total])
 
     def full():
         held = gather(kv, "x", NX)
-        att, dq, dkv = attention(lookup(image_slot, pairs), docs, tok, queries, grad_out, held)
+        src = lookup(image_slot, pairs)
+        low, score_grad, dkv = attention(src, docs, tok, queries, grad_out, held)
+        att, dq = outputs(src, low, score_grad, held)
         dkv = lax.all_to_all(dkv, "x", 0, 0, tiled=True)
         return att, dq, jnp.sum(dkv.astype(jnp.float32), axis=0).astype(jnp.bfloat16)
 

time: 160 us -> 159 us (level)
  blocking collectives: 70.4 us -> 35.6 us
  starting transfers between devices: 18.1 us -> 32.2 us
  waiting for transfers between devices: 48.4 us -> 60 us
  local copies, waits for them, and re-layouts: 5.1 us -> 11.5 us
  Pallas kernels: 11.7 us -> 14.2 us
    all_to_all x2 -> x1, blocking collectives: 36.5 us -> 12.3 us  [gather(): return lax.all_to_all(copies, axis, 0, 0, tiled=True)]
    all_to_all x1 -> x2, starting transfers between devices: 4.14 us -> 15 us  [gather(): return lax.all_to_all(copies, axis, 0, 0, tiled=True)]
    all_to_all x1 -> x0, blocking collectives: 10.7 us -> none  [narrow(): lax.all_to_all(dkv, 'x', 0, 0, tiled=True)]
    all_to_all x1 -> x2, waiting for transfers between devices: 16 us -> 26.5 us  [gather(): return lax.all_to_all(copies, axis, 0, 0, tiled=True)]
    cond x0 -> x10, local copies, waits for them, and re-layouts: none -> 5.83 us
    pallas_call x0 -> x1, Pallas kernels: none -> 3.68 us  [outputs(): pl.pallas_call(output_kernel, grid_spec=pltpu.PrefetchScalarGridSpec(num_...]
    all_to_all x0 -> x1, starting transfers between devices: none -> 3.49 us  [narrow(): lax.all_to_all(dkv, 'x', 0, 0, tiled=True)]
  transfers between devices with their start and end apart: 4 -> 6, of which waited for: 4 -> 6; matrix products, arithmetic and copies ran while one was open for 1% -> 2% of each run, Pallas kernels for 0% -> 2%
where the time goes in v7:
time: 159 us
  waiting for transfers between devices  60 us (38%)
  blocking collectives  35.6 us (22%)
  starting transfers between devices  32.2 us (20%)
  Pallas kernels  14.2 us (9%)
  local copies, waits for them, and re-layouts  11.5 us (7%)
  other arithmetic  2.05 us (1%)
    all_to_all x2, waiting for transfers between devices, gather(): return lax.all_to_all(copies, axis, 0, 0, tiled=True)  26.5 us
    all_to_all x1, blocking collectives, local(): term = lax.all_to_all(term, ('y', 'core'), 0, 0, tiled=True)  23.3 us
    all_to_all x2, starting transfers between devices, gather(): return lax.all_to_all(copies, axis, 0, 0, tiled=True)  15 us
    all_to_all x1, waiting for transfers between devices, local(): lax.all_to_all(dkv, ('z', 'x'), 0, 0, tiled=True).reshape(NZ, LAT, WIDE)  12.6 us
    all_to_all x1, waiting for transfers between devices, local(): lax.all_to_all(kv.reshape(IMAGES, QUARTER, WIDE), ('z', 'x'), 0, 0, tiled...  12.4 us
    all_to_all x1, blocking collectives, gather(): return lax.all_to_all(copies, axis, 0, 0, tiled=True)  12.3 us
    pallas_call x1, Pallas kernels, attention(): pl.pallas_call(attention_kernel, grid_spec=pltpu.PrefetchScalarGridSpec(n...  7.3 us
    all_to_all x1, waiting for transfers between devices, narrow(): lax.all_to_all(picked.reshape(NX, WINDOW, QUARTER, WIDE), 'x', 0, 0, tile...  7.01 us
  transfers between devices with their start and end apart: 6, of which 6 were waited for; matrix products, arithmetic and copies ran while one was open for 2% of the time, Pallas kernels for 2%

profile of v7, /device:TPU:1, one launch (start us, length us, event | category | flops | bytes accessed | tf_op | source)
XLA Modules:
  0.0 158.6 jit_solution(8728336451807635374)
XLA Ops:
  0.6 0.8 pad_maximum_fusion.1
  1.4 0.7 broadcast_in_dim.38
  2.1 10.9 %all-to-all-start.4 = ((bf16[8,40,512]{2,1,0:T(8,128)(2,1)}), bf16[8,40,512]{2,1,0:T(8,128)(2,1)S(1)}, u32[]{:S(2)}, u32[]{:S(2)}) async-start(bf16[8,40,512]{2,1,0:T(8,128)(2,1)} %broadcast_in_dim.38), calls=%async_computation.4 | async-start | bytes 655360 | tf_op jit(solution)/shard_map/all_to_all | solution.py:195
  13.0 0.7 reshape.73
  13.8 11.1 %all-to-all-done.4 = bf16[8,40,512]{2,1,0:T(8,128)(2,1)S(1)} async-done(((bf16[8,40,512]{2,1,0:T(8,128)(2,1)}), bf16[8,40,512]{2,1,0:T(8,128)(2,1)S(1)}, u32[]{:S(2)}, u32[]{:S(2)}) %all-to-all-start.4) | async-done | bytes 327712 | tf_op jit(solution)/shard_map/all_to_all | solution.py:195
  24.9 1.2 broadcast_in_dim.39
  26.1 0.0 copy-start.10
  26.1 4.1 %all-to-all-start.5 = ((bf16[4,328,512]{2,1,0:T(8,128)(2,1)}), bf16[4,328,512]{2,1,0:T(8,128)(2,1)S(1)}, u32[]{:S(2)}, u32[]{:S(2)}) async-start(bf16[4,328,512]{2,1,0:T(8,128)(2,1)} %broadcast_in_dim.39), calls=%async_computation.5 | async-start | bytes 2686976 | tf_op jit(solution)/shard_map/all_to_all | solution.py:195
  30.3 0.0 copy-done.10
  30.3 0.2 copy.39
  30.5 15.4 %all-to-all-done.5 = bf16[4,328,512]{2,1,0:T(8,128)(2,1)S(1)} async-done(((bf16[4,328,512]{2,1,0:T(8,128)(2,1)}), bf16[4,328,512]{2,1,0:T(8,128)(2,1)S(1)}, u32[]{:S(2)}, u32[]{:S(2)}) %all-to-all-start.5) | async-done | bytes 1343520 | tf_op jit(solution)/shard_map/all_to_all | solution.py:195
  46.0 0.1 slice.17
  46.1 0.0 copy-start.12
  46.1 0.0 copy-start.11
  46.1 0.0 copy-start.13
  46.1 0.4 convolution_convert_fusion.1
  46.5 0.9 broadcast_in_dim.60
  47.4 4.5 %all-to-all-start.6 = ((bf16[32,16,512]{2,1,0:T(8,128)(2,1)}), bf16[32,16,512]{2,1,0:T(8,128)(2,1)S(1)}, u32[]{:S(2)}, u32[]{:S(2)}) async-start(bf16[32,16,512]{2,1,0:T(8,128)(2,1)} %bitcast.31), calls=%async_computation.6 | async-start | bytes 1048576 | tf_op jit(solution)/shard_map/all_to_all | solution.py:218
  51.9 0.0 copy-done.12
  51.9 0.1 copy.41
  52.0 0.1 slice_reduce_fusion
  52.1 0.6 convert_minimum_fusion
  53.4 12.4 %all-to-all-done.6 = bf16[32,16,512]{2,1,0:T(8,128)(2,1)S(1)} async-done(((bf16[32,16,512]{2,1,0:T(8,128)(2,1)}), bf16[32,16,512]{2,1,0:T(8,128)(2,1)S(1)}, u32[]{:S(2)}, u32[]{:S(2)}) %all-to-all-start.6) | async-done | bytes 524320 | tf_op jit(solution)/shard_map/all_to_all | solution.py:218
  65.8 0.0 copy-done.11
  65.8 0.0 copy-done.13
  65.8 37.8 %conditional.1 = (bf16[2048,256]{1,0:T(8,128)(2,1)}, bf16[2048,256]{1,0:T(8,128)(2,1)}, bf16[32,16,512]{2,1,0:T(8,128)(2,1)}) conditional(s32[]{:T(128)} %convert_element_type.34, (s32[8,4]{0,1:T(4,128)S(1)}, s32[32]{0:T(128)S(1)}, bf16[32,16,512]{2,1,0:T(8,128)(2,1)S(1)}, s32[8,4]{1,0:T(8,128)S(1)}, s32[8,1,256]{2,1,0:T(1,128)S(1)}, ...), branch_computations={%region_5.8_spmd, %region_8.10_spmd} | conditional | flops 1611402240 | bytes 77595496 | solution.py:244
  65.8 0.1 add_bitcast_fusion
  65.9 0.2 select_reduce_fusion.1
  66.1 0.1 reshape.59.index_ref
  66.2 1.5 branch_1_fun.4
  67.7 0.0 copy-start.9
  67.7 4.0 %all-to-all-start.2 = ((bf16[4,12,16,512]{3,2,1,0:T(8,128)(2,1)}), bf16[4,12,16,512]{3,2,1,0:T(8,128)(2,1)S(1)}, u32[]{:S(2)}, u32[]{:S(2)}) async-start(bf16[4,12,16,512]{3,2,1,0:T(8,128)(2,1)} %bitcast.2), calls=%async_computation.2 | async-start | bytes 1572864 | tf_op jit(solution)/shard_map/cond/branch_1_fun/all_to_all | solution.py:228
  71.7 0.1 copy.46
  71.8 0.6 dynamic_slice.4
  73.1 7.0 %all-to-all-done.2.kv_ref = bf16[4,12,16,512]{3,2,1,0:T(8,128)(2,1)S(1)} async-done(((bf16[4,12,16,512]{3,2,1,0:T(8,128)(2,1)}), bf16[4,12,16,512]{3,2,1,0:T(8,128)(2,1)S(1)}, u32[]{:S(2)}, u32[]{:S(2)}) %all-to-all-start.2) | async-done | bytes 786464 | tf_op jit(solution)/shard_map/cond/branch_1_fun/all_to_all | solution.py:228
  80.1 0.0 copy-done.9
  80.1 7.3 %branch_1_fun.5 = (bf16[8,2,256,256]{3,2,1,0:T(8,128)(2,1)S(1)}, bf16[8,2,256,256]{3,2,1,0:T(8,128)(2,1)S(1)}, bf16[4,12,16,512]{3,2,1,0:T(8,128)(2,1)}) custom-call(s32[8,4]{1,0:T(8,128)S(1)} %subtract_clamp_fusion.src_ref, s32[8,4]{1,0:T(8,128)S(1)} %get-tuple-element.83.doc_ref, s32[8,1,256]{2,1,0:T(1,128)S(1)} %get-tuple-element.84.tok_ref, ...), custom_call_target="tpu_custom_call" | custom-call | flops 1073741824 | bytes 9437184 | tf_op jit(solution)/shard_map/cond/branch_1_fun/pallas_call | solution.py:130
  87.4 0.0 copy-start.1
  87.4 1.3 copy-done.1
  88.7 0.0 copy-start.3
  88.7 1.3 copy-done.3
  90.0 3.5 %all-to-all-start.3 = ((bf16[4,12,16,512]{3,2,1,0:T(8,128)(2,1)}), bf16[4,12,16,512]{3,2,1,0:T(8,128)(2,1)S(1)}, u32[]{:S(2)}, u32[]{:S(2)}) async-start(bf16[4,12,16,512]{3,2,1,0:T(8,128)(2,1)} %get-tuple-element.96), calls=%async_computation.3 | async-start | bytes 1572864 | tf_op jit(solution)/shard_map/cond/branch_1_fun/all_to_all | solution.py:231
  93.5 0.0 copy-start.2
  93.6 1.6 copy-done.2
  95.1 0.0 copy-start.4
  95.1 1.6 %copy-done.4 = bf16[8,2,256,256]{3,2,1,0:T(8,128)(2,1)S(1)} copy-done((bf16[8,2,256,256]{3,2,1,0:T(8,128)(2,1)S(1)}, bf16[8,2,256,256]{3,2,1,0:T(8,128)(2,1)}, u32[]{:S(2)}) %copy-start.4) | copy-done | bytes 2097176 | tf_op jit(solution)/shard_map/cond
  96.7 3.7 %branch_1_fun.6 = (bf16[2048,256]{1,0:T(8,128)(2,1)}, bf16[2048,256]{1,0:T(8,128)(2,1)}) custom-call(s32[8,4]{1,0:T(8,128)S(1)} %subtract_clamp_fusion.src_ref, bf16[8,2,256,256]{3,2,1,0:T(8,128)(2,1)S(1)} %copy-done.2, bf16[8,2,256,256]{3,2,1,0:T(8,128)(2,1)S(1)} %copy-done.4, bf16[4,12,16,512]{3,2,1,0:T(8,128)(2,1)S(1)} %all-to-all-done.2.kv_ref), custom_call_target="tpu_custom_call" | custom-call | flops 536870912 | bytes 8388608 | tf_op jit(solution)/shard_map/cond/branch_1_fun/pallas_call | solution.py:150
  100.4 1.4 all-to-all-done.3
  101.8 1.8 %branch_1_fun.7 = bf16[32,16,512]{2,1,0:T(8,128)(2,1)} custom-call(s32[48]{0:T(128)S(1)} %reshape.59.index_ref, bf16[48,16,512]{2,1,0:T(8,128)(2,1)S(1)} %bitcast.27), custom_call_target="tpu_custom_call" | custom-call | bytes 2097152 | tf_op jit(solution)/shard_map/cond/branch_1_fun/pallas_call | solution.py:179
  103.6 5.2 %all-to-all-start.7 = ((bf16[32,16,512]{2,1,0:T(8,128)(2,1)}), bf16[32,16,512]{2,1,0:T(8,128)(2,1)S(1)}, u32[]{:S(2)}, u32[]{:S(2)}) async-start(bf16[32,16,512]{2,1,0:T(8,128)(2,1)} %get-tuple-element.105), calls=%async_computation.7 | async-start | bytes 1048576 | tf_op jit(solution)/shard_map/all_to_all | solution.py:246
  108.8 0.1 copy.47
  108.9 12.6 %all-to-all-done.7 = bf16[32,16,512]{2,1,0:T(8,128)(2,1)S(1)} async-done(((bf16[32,16,512]{2,1,0:T(8,128)(2,1)}), bf16[32,16,512]{2,1,0:T(8,128)(2,1)S(1)}, u32[]{:S(2)}, u32[]{:S(2)}) %all-to-all-start.7) | async-done | bytes 524320 | tf_op jit(solution)/shard_map/all_to_all | solution.py:246
  121.6 0.1 bitcast_reduce_fusion
  121.6 0.5 convolution_convert_fusion
  122.2 23.3 %all_to_all.46 = bf16[16,4,1280]{2,1,0:T(4,128)(2,1)S(1)} all-to-all(bf16[16,4,1280]{2,1,0:T(4,128)(2,1)S(1)} %reshape.80), channel_id=1, replica_groups=mesh['z'=8,'x'=4,'y'=8,'core'=2] {'y','core'}, dimensions={0} | all-to-all | bytes 327680 | tf_op jit(solution)/shard_map/all_to_all | solution.py:252
  145.5 0.1 reduce_sum.56
  145.6 12.3 %all_to_all.47 = bf16[16,4,1280]{2,1,0:T(4,128)(2,1)S(1)} all-to-all(bf16[16,4,1280]{2,1,0:T(4,128)(2,1)S(1)} %broadcast_in_dim.61), channel_id=1, replica_groups=mesh['z'=8,'x'=4,'y'=8,'core'=2] {'y','core'}, dimensions={0} | all-to-all | bytes 327680 | tf_op jit(solution)/shard_map/all_to_all | solution.py:195
  157.9 0.7 reshape.81
  (15 shorter events, 0.2 us)
Async XLA Ops:
  2.1 22.8 %all-to-all-start.4 = ((bf16[8,40,512]{2,1,0:T(8,128)(2,1)}), bf16[8,40,512]{2,1,0:T(8,128)(2,1)S(1)}, u32[]{:S(2)}, u32[]{:S(2)}) async-start(bf16[8,40,512]{2,1,0:T(8,128)(2,1)} %broadcast_in_dim.38), calls=%async_computation.4 | async-start | bytes 655360 | tf_op jit(solution)/shard_map/all_to_all | solution.py:195
  26.1 4.1 %copy-start.10 = (bf16[1,64,1280]{2,1,0:T(8,128)(2,1)S(1)}, bf16[1,64,1280]{2,1,0:T(8,128)(2,1)}, u32[]{:S(2)}) copy-start(bf16[1,64,1280]{2,1,0:T(8,128)(2,1)} %param.11) | copy-start | bytes 491524
  26.1 19.8 %all-to-all-start.5 = ((bf16[4,328,512]{2,1,0:T(8,128)(2,1)}), bf16[4,328,512]{2,1,0:T(8,128)(2,1)S(1)}, u32[]{:S(2)}, u32[]{:S(2)}) async-start(bf16[4,328,512]{2,1,0:T(8,128)(2,1)} %broadcast_in_dim.39), calls=%async_computation.5 | async-start | bytes 2686976 | tf_op jit(solution)/shard_map/all_to_all | solution.py:195
  46.1 5.8 %copy-start.12 = (s32[8,4]{0,1:T(4,128)S(1)}, s32[8,4]{0,1:T(4,128)}, u32[]{:S(2)}) copy-start(s32[8,4]{0,1:T(4,128)} %param.15) | copy-start | bytes 388
  46.1 19.7 %copy-start.11 = (s32[2048]{0:T(1024)S(1)}, s32[2048]{0:T(1024)}, u32[]{:S(2)}) copy-start(s32[2048]{0:T(1024)} %param.17) | copy-start | bytes 24580
  46.1 19.7 %copy-start.13 = (s32[32]{0:T(128)S(1)}, s32[32]{0:T(128)}, u32[]{:S(2)}) copy-start(s32[32]{0:T(128)} %param.16) | copy-start | bytes 388
  47.4 18.4 %all-to-all-start.6 = ((bf16[32,16,512]{2,1,0:T(8,128)(2,1)}), bf16[32,16,512]{2,1,0:T(8,128)(2,1)S(1)}, u32[]{:S(2)}, u32[]{:S(2)}) async-start(bf16[32,16,512]{2,1,0:T(8,128)(2,1)} %bitcast.31), calls=%async_computation.6 | async-start | bytes 1048576 | tf_op jit(solution)/shard_map/all_to_all | solution.py:218
  67.7 12.4 %copy-start.9 = (bf16[2048,256]{1,0:T(8,128)(2,1)S(1)}, bf16[2048,256]{1,0:T(8,128)(2,1)}, u32[]{:S(2)}) copy-start(bf16[2048,256]{1,0:T(8,128)(2,1)} %get-tuple-element.85.q_ref) | copy-start | bytes 3145732 | tf_op jit(solution)/shard_map/cond
  67.7 12.4 %all-to-all-start.2 = ((bf16[4,12,16,512]{3,2,1,0:T(8,128)(2,1)}), bf16[4,12,16,512]{3,2,1,0:T(8,128)(2,1)S(1)}, u32[]{:S(2)}, u32[]{:S(2)}) async-start(bf16[4,12,16,512]{3,2,1,0:T(8,128)(2,1)} %bitcast.2), calls=%async_computation.2 | async-start | bytes 1572864 | tf_op jit(solution)/shard_map/cond/branch_1_fun/all_to_all | solution.py:228
  87.4 1.3 copy-start.1
  88.7 1.3 copy-start.3
  90.0 11.8 %all-to-all-start.3 = ((bf16[4,12,16,512]{3,2,1,0:T(8,128)(2,1)}), bf16[4,12,16,512]{3,2,1,0:T(8,128)(2,1)S(1)}, u32[]{:S(2)}, u32[]{:S(2)}) async-start(bf16[4,12,16,512]{3,2,1,0:T(8,128)(2,1)} %get-tuple-element.96), calls=%async_computation.3 | async-start | bytes 1572864 | tf_op jit(solution)/shard_map/cond/branch_1_fun/all_to_all | solution.py:231
  93.5 1.6 %copy-start.2 = (bf16[8,2,256,256]{3,2,1,0:T(8,128)(2,1)S(1)}, bf16[8,2,256,256]{3,2,1,0:T(8,128)(2,1)}, u32[]{:S(2)}) copy-start(bf16[8,2,256,256]{3,2,1,0:T(8,128)(2,1)} %copy-done.1) | copy-start | bytes 6291460 | tf_op jit(solution)/shard_map/cond
  95.1 1.6 %copy-start.4 = (bf16[8,2,256,256]{3,2,1,0:T(8,128)(2,1)S(1)}, bf16[8,2,256,256]{3,2,1,0:T(8,128)(2,1)}, u32[]{:S(2)}) copy-start(bf16[8,2,256,256]{3,2,1,0:T(8,128)(2,1)} %copy-done.3) | copy-start | bytes 6291460 | tf_op jit(solution)/shard_map/cond
  103.6 18.0 %all-to-all-start.7 = ((bf16[32,16,512]{2,1,0:T(8,128)(2,1)}), bf16[32,16,512]{2,1,0:T(8,128)(2,1)S(1)}, u32[]{:S(2)}, u32[]{:S(2)}) async-start(bf16[32,16,512]{2,1,0:T(8,128)(2,1)} %get-tuple-element.105), calls=%async_computation.7 | async-start | bytes 1048576 | tf_op jit(solution)/shard_map/all_to_all | solution.py:246

commit v8 on v7

--- a/solution.py
+++ b/solution.py
@@ -10,7 +10,7 @@
 LAT = 64
 GROUP = 256
 GROUPS = 8
-BATCH = 2
+BATCH = 4
 HEADS = 2
 SLOTS = 4
 IPD = 4
@@ -118,9 +118,10 @@
     return tokens, square, whole
 
 
-PARAMS = pltpu.CompilerParams(
-    dimension_semantics=("arbitrary",), vmem_limit_bytes=40 * 2**20
-)
+def params(mebibytes):
+    return pltpu.CompilerParams(
+        dimension_semantics=("arbitrary",), vmem_limit_bytes=mebibytes * 2**20
+    )
 
 
 def attention(src, docs, tok, queries, grad_out, kv):
@@ -137,7 +138,7 @@
             scratch_shapes=[pltpu.VMEM((held, LAT, WIDE), jnp.float32)],
         ),
         out_shape=[weights, weights, jax.ShapeDtypeStruct(kv.shape, jnp.bfloat16)],
-        compiler_params=PARAMS,
+        compiler_params=params(30),
         cost_estimate=pl.CostEstimate(
             flops=8 * TOKENS * GROUP * COLS, bytes_accessed=9 * 2**20, transcendentals=0
         ),
@@ -156,7 +157,7 @@
             out_specs=[tokens, tokens],
         ),
         out_shape=[out, out],
-        compiler_params=PARAMS,
+        compiler_params=params(20),
         cost_estimate=pl.CostEstimate(
             flops=4 * TOKENS * GROUP * COLS, bytes_accessed=8 * 2**20, transcendentals=0
         ),
@@ -185,7 +186,7 @@
         out_specs=pl.BlockSpec(memory_space=pltpu.VMEM),
         out_shape=jax.ShapeDtypeStruct((count, QUARTER, WIDE), jnp.bfloat16),
         scratch_shapes=scratch,
-        compiler_params=pltpu.CompilerParams(vmem_limit_bytes=16 * 2**20),
+        compiler_params=pltpu.CompilerParams(vmem_limit_bytes=8 * 2**20),
         cost_estimate=pl.CostEstimate(flops=0, bytes_accessed=2**21, transcendentals=0),
     )(index, operand)
 

time: 159 us -> 159 us (level)
  no operation moved by 1% of the time
where the time goes in v8:
time: 159 us; the launch traced here: 158 us
  waiting for transfers between devices  60.6 us (38%)
  blocking collectives  36.1 us (23%)
  starting transfers between devices  31.7 us (20%)
  Pallas kernels  13.3 us (8%)
  local copies, waits for them, and re-layouts  11.5 us (7%)
  other arithmetic  2.05 us (1%)
    all_to_all x2, waiting for transfers between devices, gather(): return lax.all_to_all(copies, axis, 0, 0, tiled=True)  26.5 us
    all_to_all x1, blocking collectives, local(): term = lax.all_to_all(term, ('y', 'core'), 0, 0, tiled=True)  23.8 us
    all_to_all x2, starting transfers between devices, gather(): return lax.all_to_all(copies, axis, 0, 0, tiled=True)  15 us
    all_to_all x1, waiting for transfers between devices, local(): lax.all_to_all(dkv, ('z', 'x'), 0, 0, tiled=True).reshape(NZ, LAT, WIDE)  12.7 us
    all_to_all x1, waiting for transfers between devices, local(): lax.all_to_all(kv.reshape(IMAGES, QUARTER, WIDE), ('z', 'x'), 0, 0, tiled...  12.4 us
    all_to_all x1, blocking collectives, gather(): return lax.all_to_all(copies, axis, 0, 0, tiled=True)  12.3 us
    all_to_all x1, waiting for transfers between devices, narrow(): lax.all_to_all(picked.reshape(NX, WINDOW, QUARTER, WIDE), 'x', 0, 0, tile...  7.01 us
    pallas_call x1, Pallas kernels, attention(): pl.pallas_call(attention_kernel, grid_spec=pltpu.PrefetchScalarGridSpec(n...  6.94 us
  transfers between devices with their start and end apart: 6, of which 6 were waited for; matrix products, arithmetic and copies ran while one was open for 2% of the time, Pallas kernels for 2%

profile of v8, /device:TPU:1, one launch (start us, length us, event | category | flops | bytes accessed | tf_op | source)
XLA Modules:
  0.0 158.3 jit_solution(18057096215583827335)
XLA Ops:
  0.6 0.8 pad_maximum_fusion.1
  1.4 0.7 broadcast_in_dim.38
  2.1 10.9 %all-to-all-start.4 = ((bf16[8,40,512]{2,1,0:T(8,128)(2,1)}), bf16[8,40,512]{2,1,0:T(8,128)(2,1)S(1)}, u32[]{:S(2)}, u32[]{:S(2)}) async-start(bf16[8,40,512]{2,1,0:T(8,128)(2,1)} %broadcast_in_dim.38), calls=%async_computation.4 | async-start | bytes 655360 | tf_op jit(solution)/shard_map/all_to_all | solution.py:196
  13.0 0.7 reshape.73
  13.8 11.1 %all-to-all-done.4 = bf16[8,40,512]{2,1,0:T(8,128)(2,1)S(1)} async-done(((bf16[8,40,512]{2,1,0:T(8,128)(2,1)}), bf16[8,40,512]{2,1,0:T(8,128)(2,1)S(1)}, u32[]{:S(2)}, u32[]{:S(2)}) %all-to-all-start.4) | async-done | bytes 327712 | tf_op jit(solution)/shard_map/all_to_all | solution.py:196
  24.9 1.2 broadcast_in_dim.39
  26.1 0.0 copy-start.10
  26.1 4.1 %all-to-all-start.5 = ((bf16[4,328,512]{2,1,0:T(8,128)(2,1)}), bf16[4,328,512]{2,1,0:T(8,128)(2,1)S(1)}, u32[]{:S(2)}, u32[]{:S(2)}) async-start(bf16[4,328,512]{2,1,0:T(8,128)(2,1)} %broadcast_in_dim.39), calls=%async_computation.5 | async-start | bytes 2686976 | tf_op jit(solution)/shard_map/all_to_all | solution.py:196
  30.3 0.0 copy-done.10
  30.3 0.2 copy.39
  30.5 15.4 %all-to-all-done.5 = bf16[4,328,512]{2,1,0:T(8,128)(2,1)S(1)} async-done(((bf16[4,328,512]{2,1,0:T(8,128)(2,1)}), bf16[4,328,512]{2,1,0:T(8,128)(2,1)S(1)}, u32[]{:S(2)}, u32[]{:S(2)}) %all-to-all-start.5) | async-done | bytes 1343520 | tf_op jit(solution)/shard_map/all_to_all | solution.py:196
  46.0 0.1 slice.17
  46.1 0.0 copy-start.12
  46.1 0.0 copy-start.11
  46.1 0.0 copy-start.13
  46.1 0.4 convolution_convert_fusion.1
  46.5 0.9 broadcast_in_dim.60
  47.4 4.5 %all-to-all-start.6 = ((bf16[32,16,512]{2,1,0:T(8,128)(2,1)}), bf16[32,16,512]{2,1,0:T(8,128)(2,1)S(1)}, u32[]{:S(2)}, u32[]{:S(2)}) async-start(bf16[32,16,512]{2,1,0:T(8,128)(2,1)} %bitcast.31), calls=%async_computation.6 | async-start | bytes 1048576 | tf_op jit(solution)/shard_map/all_to_all | solution.py:219
  51.9 0.0 copy-done.12
  51.9 0.1 copy.41
  52.0 0.1 slice_reduce_fusion
  52.1 0.6 convert_minimum_fusion
  53.4 12.4 %all-to-all-done.6 = bf16[32,16,512]{2,1,0:T(8,128)(2,1)S(1)} async-done(((bf16[32,16,512]{2,1,0:T(8,128)(2,1)}), bf16[32,16,512]{2,1,0:T(8,128)(2,1)S(1)}, u32[]{:S(2)}, u32[]{:S(2)}) %all-to-all-start.6) | async-done | bytes 524320 | tf_op jit(solution)/shard_map/all_to_all | solution.py:219
  65.8 0.0 copy-done.11
  65.8 0.0 copy-done.13
  65.8 37.4 %conditional.1 = (bf16[2048,256]{1,0:T(8,128)(2,1)}, bf16[2048,256]{1,0:T(8,128)(2,1)}, bf16[32,16,512]{2,1,0:T(8,128)(2,1)}) conditional(s32[]{:T(128)} %convert_element_type.34, (s32[8,4]{0,1:T(4,128)S(1)}, s32[32]{0:T(128)S(1)}, bf16[32,16,512]{2,1,0:T(8,128)(2,1)S(1)}, s32[8,4]{1,0:T(8,128)S(1)}, s32[8,1,256]{2,1,0:T(1,128)S(1)}, ...), branch_computations={%region_5.8_spmd, %region_8.10_spmd} | conditional | flops 1611402240 | bytes 77595496 | solution.py:245
  65.8 0.1 add_bitcast_fusion
  65.9 0.2 select_reduce_fusion.1
  66.1 0.1 reshape.59.index_ref
  66.2 1.5 branch_1_fun.4
  67.7 0.0 copy-start.9
  67.7 4.0 %all-to-all-start.2 = ((bf16[4,12,16,512]{3,2,1,0:T(8,128)(2,1)}), bf16[4,12,16,512]{3,2,1,0:T(8,128)(2,1)S(1)}, u32[]{:S(2)}, u32[]{:S(2)}) async-start(bf16[4,12,16,512]{3,2,1,0:T(8,128)(2,1)} %bitcast.2), calls=%async_computation.2 | async-start | bytes 1572864 | tf_op jit(solution)/shard_map/cond/branch_1_fun/all_to_all | solution.py:229
  71.7 0.1 copy.46
  71.8 0.6 dynamic_slice.4
  73.1 7.0 %all-to-all-done.2.kv_ref = bf16[4,12,16,512]{3,2,1,0:T(8,128)(2,1)S(1)} async-done(((bf16[4,12,16,512]{3,2,1,0:T(8,128)(2,1)}), bf16[4,12,16,512]{3,2,1,0:T(8,128)(2,1)S(1)}, u32[]{:S(2)}, u32[]{:S(2)}) %all-to-all-start.2) | async-done | bytes 786464 | tf_op jit(solution)/shard_map/cond/branch_1_fun/all_to_all | solution.py:229
  80.1 0.0 copy-done.9
  80.1 6.9 %branch_1_fun.5 = (bf16[8,2,256,256]{3,2,1,0:T(8,128)(2,1)S(1)}, bf16[8,2,256,256]{3,2,1,0:T(8,128)(2,1)S(1)}, bf16[4,12,16,512]{3,2,1,0:T(8,128)(2,1)}) custom-call(s32[8,4]{1,0:T(8,128)S(1)} %subtract_clamp_fusion.src_ref, s32[8,4]{1,0:T(8,128)S(1)} %get-tuple-element.83.doc_ref, s32[8,1,256]{2,1,0:T(1,128)S(1)} %get-tuple-element.84.tok_ref, ...), custom_call_target="tpu_custom_call" | custom-call | flops 1073741824 | bytes 9437184 | tf_op jit(solution)/shard_map/cond/branch_1_fun/pallas_call | solution.py:131
  87.0 0.0 copy-start.1
  87.0 1.3 copy-done.1
  88.4 0.0 copy-start.3
  88.4 1.3 copy-done.3
  89.7 3.5 %all-to-all-start.3 = ((bf16[4,12,16,512]{3,2,1,0:T(8,128)(2,1)}), bf16[4,12,16,512]{3,2,1,0:T(8,128)(2,1)S(1)}, u32[]{:S(2)}, u32[]{:S(2)}) async-start(bf16[4,12,16,512]{3,2,1,0:T(8,128)(2,1)} %get-tuple-element.96), calls=%async_computation.3 | async-start | bytes 1572864 | tf_op jit(solution)/shard_map/cond/branch_1_fun/all_to_all | solution.py:232
  93.2 0.0 copy-start.2
  93.2 1.6 copy-done.2
  94.8 0.0 copy-start.4
  94.8 1.6 %copy-done.4 = bf16[8,2,256,256]{3,2,1,0:T(8,128)(2,1)S(1)} copy-done((bf16[8,2,256,256]{3,2,1,0:T(8,128)(2,1)S(1)}, bf16[8,2,256,256]{3,2,1,0:T(8,128)(2,1)}, u32[]{:S(2)}) %copy-start.4) | copy-done | bytes 2097176 | tf_op jit(solution)/shard_map/cond
  96.4 3.1 %branch_1_fun.6 = (bf16[2048,256]{1,0:T(8,128)(2,1)}, bf16[2048,256]{1,0:T(8,128)(2,1)}) custom-call(s32[8,4]{1,0:T(8,128)S(1)} %subtract_clamp_fusion.src_ref, bf16[8,2,256,256]{3,2,1,0:T(8,128)(2,1)S(1)} %copy-done.2, bf16[8,2,256,256]{3,2,1,0:T(8,128)(2,1)S(1)} %copy-done.4, bf16[4,12,16,512]{3,2,1,0:T(8,128)(2,1)S(1)} %all-to-all-done.2.kv_ref), custom_call_target="tpu_custom_call" | custom-call | flops 536870912 | bytes 8388608 | tf_op jit(solution)/shard_map/cond/branch_1_fun/pallas_call | solution.py:151
  99.5 2.0 %all-to-all-done.3 = bf16[4,12,16,512]{3,2,1,0:T(8,128)(2,1)S(1)} async-done(((bf16[4,12,16,512]{3,2,1,0:T(8,128)(2,1)}), bf16[4,12,16,512]{3,2,1,0:T(8,128)(2,1)S(1)}, u32[]{:S(2)}, u32[]{:S(2)}) %all-to-all-start.3) | async-done | bytes 786464 | tf_op jit(solution)/shard_map/cond/branch_1_fun/all_to_all | solution.py:232
  101.5 1.8 %branch_1_fun.7 = bf16[32,16,512]{2,1,0:T(8,128)(2,1)} custom-call(s32[48]{0:T(128)S(1)} %reshape.59.index_ref, bf16[48,16,512]{2,1,0:T(8,128)(2,1)S(1)} %bitcast.27), custom_call_target="tpu_custom_call" | custom-call | bytes 2097152 | tf_op jit(solution)/shard_map/cond/branch_1_fun/pallas_call | solution.py:180
  103.2 4.7 %all-to-all-start.7 = ((bf16[32,16,512]{2,1,0:T(8,128)(2,1)}), bf16[32,16,512]{2,1,0:T(8,128)(2,1)S(1)}, u32[]{:S(2)}, u32[]{:S(2)}) async-start(bf16[32,16,512]{2,1,0:T(8,128)(2,1)} %get-tuple-element.105), calls=%async_computation.7 | async-start | bytes 1048576 | tf_op jit(solution)/shard_map/all_to_all | solution.py:247
  107.9 0.1 copy.47
  108.1 12.7 %all-to-all-done.7 = bf16[32,16,512]{2,1,0:T(8,128)(2,1)S(1)} async-done(((bf16[32,16,512]{2,1,0:T(8,128)(2,1)}), bf16[32,16,512]{2,1,0:T(8,128)(2,1)S(1)}, u32[]{:S(2)}, u32[]{:S(2)}) %all-to-all-start.7) | async-done | bytes 524320 | tf_op jit(solution)/shard_map/all_to_all | solution.py:247
  120.7 0.1 bitcast_reduce_fusion
  120.8 0.5 convolution_convert_fusion
  121.4 23.8 %all_to_all.46 = bf16[16,4,1280]{2,1,0:T(4,128)(2,1)S(1)} all-to-all(bf16[16,4,1280]{2,1,0:T(4,128)(2,1)S(1)} %reshape.80), channel_id=1, replica_groups=mesh['z'=8,'x'=4,'y'=8,'core'=2] {'y','core'}, dimensions={0} | all-to-all | bytes 327680 | tf_op jit(solution)/shard_map/all_to_all | solution.py:253
  145.1 0.1 reduce_sum.56
  145.3 12.3 %all_to_all.47 = bf16[16,4,1280]{2,1,0:T(4,128)(2,1)S(1)} all-to-all(bf16[16,4,1280]{2,1,0:T(4,128)(2,1)S(1)} %broadcast_in_dim.61), channel_id=1, replica_groups=mesh['z'=8,'x'=4,'y'=8,'core'=2] {'y','core'}, dimensions={0} | all-to-all | bytes 327680 | tf_op jit(solution)/shard_map/all_to_all | solution.py:196
  157.6 0.7 reshape.81
  (15 shorter events, 0.2 us)
Async XLA Ops:
  2.1 22.8 %all-to-all-start.4 = ((bf16[8,40,512]{2,1,0:T(8,128)(2,1)}), bf16[8,40,512]{2,1,0:T(8,128)(2,1)S(1)}, u32[]{:S(2)}, u32[]{:S(2)}) async-start(bf16[8,40,512]{2,1,0:T(8,128)(2,1)} %broadcast_in_dim.38), calls=%async_computation.4 | async-start | bytes 655360 | tf_op jit(solution)/shard_map/all_to_all | solution.py:196
  26.1 4.1 %copy-start.10 = (bf16[1,64,1280]{2,1,0:T(8,128)(2,1)S(1)}, bf16[1,64,1280]{2,1,0:T(8,128)(2,1)}, u32[]{:S(2)}) copy-start(bf16[1,64,1280]{2,1,0:T(8,128)(2,1)} %param.11) | copy-start | bytes 491524
  26.1 19.8 %all-to-all-start.5 = ((bf16[4,328,512]{2,1,0:T(8,128)(2,1)}), bf16[4,328,512]{2,1,0:T(8,128)(2,1)S(1)}, u32[]{:S(2)}, u32[]{:S(2)}) async-start(bf16[4,328,512]{2,1,0:T(8,128)(2,1)} %broadcast_in_dim.39), calls=%async_computation.5 | async-start | bytes 2686976 | tf_op jit(solution)/shard_map/all_to_all | solution.py:196
  46.1 5.8 %copy-start.12 = (s32[8,4]{0,1:T(4,128)S(1)}, s32[8,4]{0,1:T(4,128)}, u32[]{:S(2)}) copy-start(s32[8,4]{0,1:T(4,128)} %param.15) | copy-start | bytes 388
  46.1 19.7 %copy-start.11 = (s32[2048]{0:T(1024)S(1)}, s32[2048]{0:T(1024)}, u32[]{:S(2)}) copy-start(s32[2048]{0:T(1024)} %param.17) | copy-start | bytes 24580
  46.1 19.7 %copy-start.13 = (s32[32]{0:T(128)S(1)}, s32[32]{0:T(128)}, u32[]{:S(2)}) copy-start(s32[32]{0:T(128)} %param.16) | copy-start | bytes 388
  47.4 18.4 %all-to-all-start.6 = ((bf16[32,16,512]{2,1,0:T(8,128)(2,1)}), bf16[32,16,512]{2,1,0:T(8,128)(2,1)S(1)}, u32[]{:S(2)}, u32[]{:S(2)}) async-start(bf16[32,16,512]{2,1,0:T(8,128)(2,1)} %bitcast.31), calls=%async_computation.6 | async-start | bytes 1048576 | tf_op jit(solution)/shard_map/all_to_all | solution.py:219
  67.7 12.4 %copy-start.9 = (bf16[2048,256]{1,0:T(8,128)(2,1)S(1)}, bf16[2048,256]{1,0:T(8,128)(2,1)}, u32[]{:S(2)}) copy-start(bf16[2048,256]{1,0:T(8,128)(2,1)} %get-tuple-element.85.q_ref) | copy-start | bytes 3145732 | tf_op jit(solution)/shard_map/cond
  67.7 12.4 %all-to-all-start.2 = ((bf16[4,12,16,512]{3,2,1,0:T(8,128)(2,1)}), bf16[4,12,16,512]{3,2,1,0:T(8,128)(2,1)S(1)}, u32[]{:S(2)}, u32[]{:S(2)}) async-start(bf16[4,12,16,512]{3,2,1,0:T(8,128)(2,1)} %bitcast.2), calls=%async_computation.2 | async-start | bytes 1572864 | tf_op jit(solution)/shard_map/cond/branch_1_fun/all_to_all | solution.py:229
  87.0 1.3 copy-start.1
  88.4 1.3 copy-start.3
  89.7 11.8 %all-to-all-start.3 = ((bf16[4,12,16,512]{3,2,1,0:T(8,128)(2,1)}), bf16[4,12,16,512]{3,2,1,0:T(8,128)(2,1)S(1)}, u32[]{:S(2)}, u32[]{:S(2)}) async-start(bf16[4,12,16,512]{3,2,1,0:T(8,128)(2,1)} %get-tuple-element.96), calls=%async_computation.3 | async-start | bytes 1572864 | tf_op jit(solution)/shard_map/cond/branch_1_fun/all_to_all | solution.py:232
  93.2 1.6 %copy-start.2 = (bf16[8,2,256,256]{3,2,1,0:T(8,128)(2,1)S(1)}, bf16[8,2,256,256]{3,2,1,0:T(8,128)(2,1)}, u32[]{:S(2)}) copy-start(bf16[8,2,256,256]{3,2,1,0:T(8,128)(2,1)} %copy-done.1) | copy-start | bytes 6291460 | tf_op jit(solution)/shard_map/cond
  94.8 1.6 %copy-start.4 = (bf16[8,2,256,256]{3,2,1,0:T(8,128)(2,1)S(1)}, bf16[8,2,256,256]{3,2,1,0:T(8,128)(2,1)}, u32[]{:S(2)}) copy-start(bf16[8,2,256,256]{3,2,1,0:T(8,128)(2,1)} %copy-done.3) | copy-start | bytes 6291460 | tf_op jit(solution)/shard_map/cond
  103.2 17.5 %all-to-all-start.7 = ((bf16[32,16,512]{2,1,0:T(8,128)(2,1)}), bf16[32,16,512]{2,1,0:T(8,128)(2,1)S(1)}, u32[]{:S(2)}, u32[]{:S(2)}) async-start(bf16[32,16,512]{2,1,0:T(8,128)(2,1)} %get-tuple-element.105), calls=%async_computation.7 | async-start | bytes 1048576 | tf_op jit(solution)/shard_map/all_to_all | solution.py:247

commit v9 on v8

--- a/solution.py
+++ b/solution.py
@@ -127,7 +127,7 @@
 def attention(src, docs, tok, queries, grad_out, kv):
     held = kv.shape[1]
     tokens, square, whole = blocks(held)
-    weights = jax.ShapeDtypeStruct((GROUPS, HEADS, SLOTS * LAT, GROUP), jnp.bfloat16)
+    weights = pltpu.HBM((GROUPS, HEADS, SLOTS * LAT, GROUP), jnp.bfloat16)
     return pl.pallas_call(
         attention_kernel,
         grid_spec=pltpu.PrefetchScalarGridSpec(

time: 159 us -> 157 us (0.987)
  local copies, waits for them, and re-layouts: 11.5 us -> 8.82 us
    cond x10 -> x6, local copies, waits for them, and re-layouts: 5.83 us -> 3.18 us
where the time goes in v9:
time: 157 us; the launch traced here: 156 us
  waiting for transfers between devices  60.6 us (39%)
  blocking collectives  36.1 us (23%)
  starting transfers between devices  31.7 us (20%)
  Pallas kernels  14 us (9%)
  local copies, waits for them, and re-layouts  8.82 us (6%)
  other arithmetic  2.05 us (1%)
    all_to_all x2, waiting for transfers between devices, gather(): return lax.all_to_all(copies, axis, 0, 0, tiled=True)  26.5 us
    all_to_all x1, blocking collectives, local(): term = lax.all_to_all(term, ('y', 'core'), 0, 0, tiled=True)  23.8 us
    all_to_all x2, starting transfers between devices, gather(): return lax.all_to_all(copies, axis, 0, 0, tiled=True)  15 us
    all_to_all x1, waiting for transfers between devices, local(): lax.all_to_all(dkv, ('z', 'x'), 0, 0, tiled=True).reshape(NZ, LAT, WIDE)  12.7 us
    all_to_all x1, waiting for transfers between devices, local(): lax.all_to_all(kv.reshape(IMAGES, QUARTER, WIDE), ('z', 'x'), 0, 0, tiled...  12.4 us
    all_to_all x1, blocking collectives, gather(): return lax.all_to_all(copies, axis, 0, 0, tiled=True)  12.3 us
    pallas_call x1, Pallas kernels, attention(): pl.pallas_call(attention_kernel, grid_spec=pltpu.PrefetchScalarGridSpec(n...  7.67 us
    all_to_all x1, waiting for transfers between devices, narrow(): lax.all_to_all(picked.reshape(NX, WINDOW, QUARTER, WIDE), 'x', 0, 0, tile...  7.01 us
  transfers between devices with their start and end apart: 6, of which 6 were waited for; matrix products, arithmetic and copies ran while one was open for 2% of the time, Pallas kernels for 2%

profile of v9, /device:TPU:1, one launch (start us, length us, event | category | flops | bytes accessed | tf_op | source)
XLA Modules:
  0.0 156.3 jit_solution(12702210798151101216)
XLA Ops:
  0.6 0.8 pad_maximum_fusion.1
  1.4 0.7 broadcast_in_dim.38
  2.1 10.9 %all-to-all-start.4 = ((bf16[8,40,512]{2,1,0:T(8,128)(2,1)}), bf16[8,40,512]{2,1,0:T(8,128)(2,1)S(1)}, u32[]{:S(2)}, u32[]{:S(2)}) async-start(bf16[8,40,512]{2,1,0:T(8,128)(2,1)} %broadcast_in_dim.38), calls=%async_computation.4 | async-start | bytes 655360 | tf_op jit(solution)/shard_map/all_to_all | solution.py:196
  13.0 0.7 reshape.73
  13.8 11.1 %all-to-all-done.4 = bf16[8,40,512]{2,1,0:T(8,128)(2,1)S(1)} async-done(((bf16[8,40,512]{2,1,0:T(8,128)(2,1)}), bf16[8,40,512]{2,1,0:T(8,128)(2,1)S(1)}, u32[]{:S(2)}, u32[]{:S(2)}) %all-to-all-start.4) | async-done | bytes 327712 | tf_op jit(solution)/shard_map/all_to_all | solution.py:196
  24.9 1.2 broadcast_in_dim.39
  26.1 0.0 copy-start.6
  26.1 4.1 %all-to-all-start.5 = ((bf16[4,328,512]{2,1,0:T(8,128)(2,1)}), bf16[4,328,512]{2,1,0:T(8,128)(2,1)S(1)}, u32[]{:S(2)}, u32[]{:S(2)}) async-start(bf16[4,328,512]{2,1,0:T(8,128)(2,1)} %broadcast_in_dim.39), calls=%async_computation.5 | async-start | bytes 2686976 | tf_op jit(solution)/shard_map/all_to_all | solution.py:196
  30.3 0.0 copy-done.6
  30.3 0.2 copy.39
  30.5 15.4 %all-to-all-done.5 = bf16[4,328,512]{2,1,0:T(8,128)(2,1)S(1)} async-done(((bf16[4,328,512]{2,1,0:T(8,128)(2,1)}), bf16[4,328,512]{2,1,0:T(8,128)(2,1)S(1)}, u32[]{:S(2)}, u32[]{:S(2)}) %all-to-all-start.5) | async-done | bytes 1343520 | tf_op jit(solution)/shard_map/all_to_all | solution.py:196
  45.9 0.1 slice.17
  46.1 0.0 copy-start.8
  46.1 0.0 copy-start.7
  46.1 0.0 copy-start.9
  46.1 0.4 convolution_convert_fusion.1
  46.5 0.9 broadcast_in_dim.60
  47.3 4.5 %all-to-all-start.6 = ((bf16[32,16,512]{2,1,0:T(8,128)(2,1)}), bf16[32,16,512]{2,1,0:T(8,128)(2,1)S(1)}, u32[]{:S(2)}, u32[]{:S(2)}) async-start(bf16[32,16,512]{2,1,0:T(8,128)(2,1)} %bitcast.31), calls=%async_computation.6 | async-start | bytes 1048576 | tf_op jit(solution)/shard_map/all_to_all | solution.py:219
  51.9 0.0 copy-done.8
  51.9 0.1 copy.41
  52.0 0.1 slice_reduce_fusion
  52.1 0.6 convert_minimum_fusion
  53.4 12.4 %all-to-all-done.6 = bf16[32,16,512]{2,1,0:T(8,128)(2,1)S(1)} async-done(((bf16[32,16,512]{2,1,0:T(8,128)(2,1)}), bf16[32,16,512]{2,1,0:T(8,128)(2,1)S(1)}, u32[]{:S(2)}, u32[]{:S(2)}) %all-to-all-start.6) | async-done | bytes 524320 | tf_op jit(solution)/shard_map/all_to_all | solution.py:219
  65.8 0.0 copy-done.7
  65.8 0.0 copy-done.9
  65.8 35.5 %conditional.1 = (bf16[2048,256]{1,0:T(8,128)(2,1)}, bf16[2048,256]{1,0:T(8,128)(2,1)}, bf16[32,16,512]{2,1,0:T(8,128)(2,1)}) conditional(s32[]{:T(128)} %convert_element_type.34, (s32[8,4]{0,1:T(4,128)S(1)}, s32[32]{0:T(128)S(1)}, bf16[32,16,512]{2,1,0:T(8,128)(2,1)S(1)}, s32[8,4]{1,0:T(8,128)S(1)}, s32[8,1,256]{2,1,0:T(1,128)S(1)}, ...), branch_computations={%region_5.8_spmd, %region_8.10_spmd} | conditional | flops 1611402240 | bytes 60818224 | solution.py:245
  65.8 0.1 add_bitcast_fusion
  65.9 0.2 select_reduce_fusion.1
  66.1 0.1 reshape.59.index_ref
  66.2 1.5 branch_1_fun.4
  67.7 0.0 copy-start.5
  67.7 4.0 %all-to-all-start.2 = ((bf16[4,12,16,512]{3,2,1,0:T(8,128)(2,1)}), bf16[4,12,16,512]{3,2,1,0:T(8,128)(2,1)S(1)}, u32[]{:S(2)}, u32[]{:S(2)}) async-start(bf16[4,12,16,512]{3,2,1,0:T(8,128)(2,1)} %bitcast.2), calls=%async_computation.2 | async-start | bytes 1572864 | tf_op jit(solution)/shard_map/cond/branch_1_fun/all_to_all | solution.py:229
  71.7 0.1 copy.46
  71.8 0.6 dynamic_slice.4
  73.1 7.0 %all-to-all-done.2.kv_ref = bf16[4,12,16,512]{3,2,1,0:T(8,128)(2,1)S(1)} async-done(((bf16[4,12,16,512]{3,2,1,0:T(8,128)(2,1)}), bf16[4,12,16,512]{3,2,1,0:T(8,128)(2,1)S(1)}, u32[]{:S(2)}, u32[]{:S(2)}) %all-to-all-start.2) | async-done | bytes 786464 | tf_op jit(solution)/shard_map/cond/branch_1_fun/all_to_all | solution.py:229
  80.1 0.0 copy-done.5
  80.1 7.7 %branch_1_fun.5 = (bf16[8,2,256,256]{3,2,1,0:T(8,128)(2,1)}, bf16[8,2,256,256]{3,2,1,0:T(8,128)(2,1)}, bf16[4,12,16,512]{3,2,1,0:T(8,128)(2,1)}) custom-call(s32[8,4]{1,0:T(8,128)S(1)} %subtract_clamp_fusion.src_ref, s32[8,4]{1,0:T(8,128)S(1)} %get-tuple-element.83.doc_ref, s32[8,1,256]{2,1,0:T(1,128)S(1)} %get-tuple-element.84.tok_ref, ...), custom_call_target="tpu_custom_call" | custom-call | flops 1073741824 | bytes 9437184 | tf_op jit(solution)/shard_map/cond/branch_1_fun/pallas_call | solution.py:131
  87.7 3.5 %all-to-all-start.3 = ((bf16[4,12,16,512]{3,2,1,0:T(8,128)(2,1)}), bf16[4,12,16,512]{3,2,1,0:T(8,128)(2,1)S(1)}, u32[]{:S(2)}, u32[]{:S(2)}) async-start(bf16[4,12,16,512]{3,2,1,0:T(8,128)(2,1)} %get-tuple-element.96), calls=%async_computation.3 | async-start | bytes 1572864 | tf_op jit(solution)/shard_map/cond/branch_1_fun/all_to_all | solution.py:232
  91.2 0.0 copy-start.1
  91.3 1.6 %copy-done.1 = bf16[8,2,256,256]{3,2,1,0:T(8,128)(2,1)S(1)} copy-done((bf16[8,2,256,256]{3,2,1,0:T(8,128)(2,1)S(1)}, bf16[8,2,256,256]{3,2,1,0:T(8,128)(2,1)}, u32[]{:S(2)}) %copy-start.1) | copy-done | bytes 2097176 | tf_op jit(solution)/shard_map/cond
  92.8 0.0 copy-start.2
  92.8 1.6 %copy-done.2 = bf16[8,2,256,256]{3,2,1,0:T(8,128)(2,1)S(1)} copy-done((bf16[8,2,256,256]{3,2,1,0:T(8,128)(2,1)S(1)}, bf16[8,2,256,256]{3,2,1,0:T(8,128)(2,1)}, u32[]{:S(2)}) %copy-start.2) | copy-done | bytes 2097176 | tf_op jit(solution)/shard_map/cond
  94.4 3.1 %branch_1_fun.6 = (bf16[2048,256]{1,0:T(8,128)(2,1)}, bf16[2048,256]{1,0:T(8,128)(2,1)}) custom-call(s32[8,4]{1,0:T(8,128)S(1)} %subtract_clamp_fusion.src_ref, bf16[8,2,256,256]{3,2,1,0:T(8,128)(2,1)S(1)} %copy-done.1, bf16[8,2,256,256]{3,2,1,0:T(8,128)(2,1)S(1)} %copy-done.2, bf16[4,12,16,512]{3,2,1,0:T(8,128)(2,1)S(1)} %all-to-all-done.2.kv_ref), custom_call_target="tpu_custom_call" | custom-call | flops 536870912 | bytes 8388608 | tf_op jit(solution)/shard_map/cond/branch_1_fun/pallas_call | solution.py:151
  97.6 2.0 %all-to-all-done.3 = bf16[4,12,16,512]{3,2,1,0:T(8,128)(2,1)S(1)} async-done(((bf16[4,12,16,512]{3,2,1,0:T(8,128)(2,1)}), bf16[4,12,16,512]{3,2,1,0:T(8,128)(2,1)S(1)}, u32[]{:S(2)}, u32[]{:S(2)}) %all-to-all-start.3) | async-done | bytes 786464 | tf_op jit(solution)/shard_map/cond/branch_1_fun/all_to_all | solution.py:232
  99.5 1.8 %branch_1_fun.7 = bf16[32,16,512]{2,1,0:T(8,128)(2,1)} custom-call(s32[48]{0:T(128)S(1)} %reshape.59.index_ref, bf16[48,16,512]{2,1,0:T(8,128)(2,1)S(1)} %bitcast.27), custom_call_target="tpu_custom_call" | custom-call | bytes 2097152 | tf_op jit(solution)/shard_map/cond/branch_1_fun/pallas_call | solution.py:180
  101.3 4.6 %all-to-all-start.7 = ((bf16[32,16,512]{2,1,0:T(8,128)(2,1)}), bf16[32,16,512]{2,1,0:T(8,128)(2,1)S(1)}, u32[]{:S(2)}, u32[]{:S(2)}) async-start(bf16[32,16,512]{2,1,0:T(8,128)(2,1)} %get-tuple-element.105), calls=%async_computation.7 | async-start | bytes 1048576 | tf_op jit(solution)/shard_map/all_to_all | solution.py:247
  106.0 0.1 copy.47
  106.1 12.7 %all-to-all-done.7 = bf16[32,16,512]{2,1,0:T(8,128)(2,1)S(1)} async-done(((bf16[32,16,512]{2,1,0:T(8,128)(2,1)}), bf16[32,16,512]{2,1,0:T(8,128)(2,1)S(1)}, u32[]{:S(2)}, u32[]{:S(2)}) %all-to-all-start.7) | async-done | bytes 524320 | tf_op jit(solution)/shard_map/all_to_all | solution.py:247
  118.8 0.1 bitcast_reduce_fusion
  118.8 0.5 convolution_convert_fusion
  119.4 23.8 %all_to_all.46 = bf16[16,4,1280]{2,1,0:T(4,128)(2,1)S(1)} all-to-all(bf16[16,4,1280]{2,1,0:T(4,128)(2,1)S(1)} %reshape.80), channel_id=1, replica_groups=mesh['z'=8,'x'=4,'y'=8,'core'=2] {'y','core'}, dimensions={0} | all-to-all | bytes 327680 | tf_op jit(solution)/shard_map/all_to_all | solution.py:253
  143.2 0.1 reduce_sum.56
  143.3 12.3 %all_to_all.47 = bf16[16,4,1280]{2,1,0:T(4,128)(2,1)S(1)} all-to-all(bf16[16,4,1280]{2,1,0:T(4,128)(2,1)S(1)} %broadcast_in_dim.61), channel_id=1, replica_groups=mesh['z'=8,'x'=4,'y'=8,'core'=2] {'y','core'}, dimensions={0} | all-to-all | bytes 327680 | tf_op jit(solution)/shard_map/all_to_all | solution.py:196
  155.6 0.7 reshape.81
  (15 shorter events, 0.2 us)
Async XLA Ops:
  2.1 22.8 %all-to-all-start.4 = ((bf16[8,40,512]{2,1,0:T(8,128)(2,1)}), bf16[8,40,512]{2,1,0:T(8,128)(2,1)S(1)}, u32[]{:S(2)}, u32[]{:S(2)}) async-start(bf16[8,40,512]{2,1,0:T(8,128)(2,1)} %broadcast_in_dim.38), calls=%async_computation.4 | async-start | bytes 655360 | tf_op jit(solution)/shard_map/all_to_all | solution.py:196
  26.1 4.1 %copy-start.6 = (bf16[1,64,1280]{2,1,0:T(8,128)(2,1)S(1)}, bf16[1,64,1280]{2,1,0:T(8,128)(2,1)}, u32[]{:S(2)}) copy-start(bf16[1,64,1280]{2,1,0:T(8,128)(2,1)} %param.11) | copy-start | bytes 491524
  26.1 19.8 %all-to-all-start.5 = ((bf16[4,328,512]{2,1,0:T(8,128)(2,1)}), bf16[4,328,512]{2,1,0:T(8,128)(2,1)S(1)}, u32[]{:S(2)}, u32[]{:S(2)}) async-start(bf16[4,328,512]{2,1,0:T(8,128)(2,1)} %broadcast_in_dim.39), calls=%async_computation.5 | async-start | bytes 2686976 | tf_op jit(solution)/shard_map/all_to_all | solution.py:196
  46.1 5.8 %copy-start.8 = (s32[8,4]{0,1:T(4,128)S(1)}, s32[8,4]{0,1:T(4,128)}, u32[]{:S(2)}) copy-start(s32[8,4]{0,1:T(4,128)} %param.15) | copy-start | bytes 388
  46.1 19.7 %copy-start.7 = (s32[2048]{0:T(1024)S(1)}, s32[2048]{0:T(1024)}, u32[]{:S(2)}) copy-start(s32[2048]{0:T(1024)} %param.17) | copy-start | bytes 24580
  46.1 19.7 %copy-start.9 = (s32[32]{0:T(128)S(1)}, s32[32]{0:T(128)}, u32[]{:S(2)}) copy-start(s32[32]{0:T(128)} %param.16) | copy-start | bytes 388
  47.3 18.4 %all-to-all-start.6 = ((bf16[32,16,512]{2,1,0:T(8,128)(2,1)}), bf16[32,16,512]{2,1,0:T(8,128)(2,1)S(1)}, u32[]{:S(2)}, u32[]{:S(2)}) async-start(bf16[32,16,512]{2,1,0:T(8,128)(2,1)} %bitcast.31), calls=%async_computation.6 | async-start | bytes 1048576 | tf_op jit(solution)/shard_map/all_to_all | solution.py:219
  67.7 12.4 %copy-start.5 = (bf16[2048,256]{1,0:T(8,128)(2,1)S(1)}, bf16[2048,256]{1,0:T(8,128)(2,1)}, u32[]{:S(2)}) copy-start(bf16[2048,256]{1,0:T(8,128)(2,1)} %get-tuple-element.85.q_ref) | copy-start | bytes 3145732 | tf_op jit(solution)/shard_map/cond
  67.7 12.4 %all-to-all-start.2 = ((bf16[4,12,16,512]{3,2,1,0:T(8,128)(2,1)}), bf16[4,12,16,512]{3,2,1,0:T(8,128)(2,1)S(1)}, u32[]{:S(2)}, u32[]{:S(2)}) async-start(bf16[4,12,16,512]{3,2,1,0:T(8,128)(2,1)} %bitcast.2), calls=%async_computation.2 | async-start | bytes 1572864 | tf_op jit(solution)/shard_map/cond/branch_1_fun/all_to_all | solution.py:229
  87.7 11.8 %all-to-all-start.3 = ((bf16[4,12,16,512]{3,2,1,0:T(8,128)(2,1)}), bf16[4,12,16,512]{3,2,1,0:T(8,128)(2,1)S(1)}, u32[]{:S(2)}, u32[]{:S(2)}) async-start(bf16[4,12,16,512]{3,2,1,0:T(8,128)(2,1)} %get-tuple-element.96), calls=%async_computation.3 | async-start | bytes 1572864 | tf_op jit(solution)/shard_map/cond/branch_1_fun/all_to_all | solution.py:232
  91.2 1.6 %copy-start.1 = (bf16[8,2,256,256]{3,2,1,0:T(8,128)(2,1)S(1)}, bf16[8,2,256,256]{3,2,1,0:T(8,128)(2,1)}, u32[]{:S(2)}) copy-start(bf16[8,2,256,256]{3,2,1,0:T(8,128)(2,1)} %get-tuple-element.92.low_ref) | copy-start | bytes 6291460 | tf_op jit(solution)/shard_map/cond
  92.8 1.6 %copy-start.2 = (bf16[8,2,256,256]{3,2,1,0:T(8,128)(2,1)S(1)}, bf16[8,2,256,256]{3,2,1,0:T(8,128)(2,1)}, u32[]{:S(2)}) copy-start(bf16[8,2,256,256]{3,2,1,0:T(8,128)(2,1)} %get-tuple-element.93.sg_ref) | copy-start | bytes 6291460 | tf_op jit(solution)/shard_map/cond
  101.3 17.5 %all-to-all-start.7 = ((bf16[32,16,512]{2,1,0:T(8,128)(2,1)}), bf16[32,16,512]{2,1,0:T(8,128)(2,1)S(1)}, u32[]{:S(2)}, u32[]{:S(2)}) async-start(bf16[32,16,512]{2,1,0:T(8,128)(2,1)} %get-tuple-element.105), calls=%async_computation.7 | async-start | bytes 1048576 | tf_op jit(solution)/shard_map/all_to_all | solution.py:247

commit v10 on v9

--- a/solution.py
+++ b/solution.py
@@ -10,7 +10,7 @@
 LAT = 64
 GROUP = 256
 GROUPS = 8
-BATCH = 4
+BATCH = 2
 HEADS = 2
 SLOTS = 4
 IPD = 4
@@ -114,7 +114,9 @@
 def blocks(held):
     tokens = pl.BlockSpec((BATCH * GROUP, COLS), lambda g, *_: (g, 0))
     square = pl.BlockSpec((BATCH, HEADS, SLOTS * LAT, GROUP), lambda g, *_: (g, 0, 0, 0))
-    whole = pl.BlockSpec((NX, held, QUARTER, WIDE), lambda g, *_: (0, 0, 0, 0))
+    whole = pl.BlockSpec(
+        (NX, held, QUARTER, WIDE), lambda g, *_: (0, 0, 0, 0), pipeline_mode=pl.Buffered(1)
+    )
     return tokens, square, whole
 
 

time: 157 us -> 157 us (level)
  no operation moved by 1% of the time
where the time goes in v10:
time: 157 us; the launch traced here: 156 us
  waiting for transfers between devices  60 us (38%)
  blocking collectives  35.6 us (23%)
  starting transfers between devices  32.3 us (21%)
  Pallas kernels  14.6 us (9%)
  local copies, waits for them, and re-layouts  8.82 us (6%)
  other arithmetic  2.05 us (1%)
    all_to_all x2, waiting for transfers between devices, gather(): return lax.all_to_all(copies, axis, 0, 0, tiled=True)  26.5 us
    all_to_all x1, blocking collectives, local(): term = lax.all_to_all(term, ('y', 'core'), 0, 0, tiled=True)  23.3 us
    all_to_all x2, starting transfers between devices, gather(): return lax.all_to_all(copies, axis, 0, 0, tiled=True)  15 us
    all_to_all x1, waiting for transfers between devices, local(): lax.all_to_all(dkv, ('z', 'x'), 0, 0, tiled=True).reshape(NZ, LAT, WIDE)  12.6 us
    all_to_all x1, waiting for transfers between devices, local(): lax.all_to_all(kv.reshape(IMAGES, QUARTER, WIDE), ('z', 'x'), 0, 0, tiled...  12.4 us
    all_to_all x1, blocking collectives, gather(): return lax.all_to_all(copies, axis, 0, 0, tiled=True)  12.3 us
    pallas_call x1, Pallas kernels, attention(): pl.pallas_call(attention_kernel, grid_spec=pltpu.PrefetchScalarGridSpec(n...  7.71 us
    all_to_all x1, waiting for transfers between devices, narrow(): lax.all_to_all(picked.reshape(NX, WINDOW, QUARTER, WIDE), 'x', 0, 0, tile...  7.01 us
  transfers between devices with their start and end apart: 6, of which 6 were waited for; matrix products, arithmetic and copies ran while one was open for 2% of the time, Pallas kernels for 2%

profile of v10, /device:TPU:1, one launch (start us, length us, event | category | flops | bytes accessed | tf_op | source)
XLA Modules:
  0.0 156.4 jit_solution(10329315622033290888)
XLA Ops:
  0.6 0.8 pad_maximum_fusion.1
  1.4 0.7 broadcast_in_dim.38
  2.1 10.9 %all-to-all-start.4 = ((bf16[8,40,512]{2,1,0:T(8,128)(2,1)}), bf16[8,40,512]{2,1,0:T(8,128)(2,1)S(1)}, u32[]{:S(2)}, u32[]{:S(2)}) async-start(bf16[8,40,512]{2,1,0:T(8,128)(2,1)} %broadcast_in_dim.38), calls=%async_computation.4 | async-start | bytes 655360 | tf_op jit(solution)/shard_map/all_to_all | solution.py:198
  13.0 0.7 reshape.73
  13.8 11.1 %all-to-all-done.4 = bf16[8,40,512]{2,1,0:T(8,128)(2,1)S(1)} async-done(((bf16[8,40,512]{2,1,0:T(8,128)(2,1)}), bf16[8,40,512]{2,1,0:T(8,128)(2,1)S(1)}, u32[]{:S(2)}, u32[]{:S(2)}) %all-to-all-start.4) | async-done | bytes 327712 | tf_op jit(solution)/shard_map/all_to_all | solution.py:198
  24.9 1.2 broadcast_in_dim.39
  26.1 0.0 copy-start.6
  26.1 4.1 %all-to-all-start.5 = ((bf16[4,328,512]{2,1,0:T(8,128)(2,1)}), bf16[4,328,512]{2,1,0:T(8,128)(2,1)S(1)}, u32[]{:S(2)}, u32[]{:S(2)}) async-start(bf16[4,328,512]{2,1,0:T(8,128)(2,1)} %broadcast_in_dim.39), calls=%async_computation.5 | async-start | bytes 2686976 | tf_op jit(solution)/shard_map/all_to_all | solution.py:198
  30.3 0.0 copy-done.6
  30.3 0.2 copy.39
  30.5 15.4 %all-to-all-done.5 = bf16[4,328,512]{2,1,0:T(8,128)(2,1)S(1)} async-done(((bf16[4,328,512]{2,1,0:T(8,128)(2,1)}), bf16[4,328,512]{2,1,0:T(8,128)(2,1)S(1)}, u32[]{:S(2)}, u32[]{:S(2)}) %all-to-all-start.5) | async-done | bytes 1343520 | tf_op jit(solution)/shard_map/all_to_all | solution.py:198
  45.9 0.1 slice.17
  46.1 0.0 copy-start.8
  46.1 0.0 copy-start.7
  46.1 0.0 copy-start.9
  46.1 0.4 convolution_convert_fusion.1
  46.5 0.9 broadcast_in_dim.60
  47.3 4.5 %all-to-all-start.6 = ((bf16[32,16,512]{2,1,0:T(8,128)(2,1)}), bf16[32,16,512]{2,1,0:T(8,128)(2,1)S(1)}, u32[]{:S(2)}, u32[]{:S(2)}) async-start(bf16[32,16,512]{2,1,0:T(8,128)(2,1)} %bitcast.31), calls=%async_computation.6 | async-start | bytes 1048576 | tf_op jit(solution)/shard_map/all_to_all | solution.py:221
  51.9 0.0 copy-done.8
  51.9 0.1 copy.41
  52.0 0.1 slice_reduce_fusion
  52.1 0.6 convert_minimum_fusion
  53.4 12.4 %all-to-all-done.6 = bf16[32,16,512]{2,1,0:T(8,128)(2,1)S(1)} async-done(((bf16[32,16,512]{2,1,0:T(8,128)(2,1)}), bf16[32,16,512]{2,1,0:T(8,128)(2,1)S(1)}, u32[]{:S(2)}, u32[]{:S(2)}) %all-to-all-start.6) | async-done | bytes 524320 | tf_op jit(solution)/shard_map/all_to_all | solution.py:221
  65.8 0.0 copy-done.7
  65.8 0.0 copy-done.9
  65.8 35.6 %conditional.1 = (bf16[2048,256]{1,0:T(8,128)(2,1)}, bf16[2048,256]{1,0:T(8,128)(2,1)}, bf16[32,16,512]{2,1,0:T(8,128)(2,1)}) conditional(s32[]{:T(128)} %convert_element_type.34, (s32[8,4]{0,1:T(4,128)S(1)}, s32[32]{0:T(128)S(1)}, bf16[32,16,512]{2,1,0:T(8,128)(2,1)S(1)}, s32[8,4]{1,0:T(8,128)S(1)}, s32[8,1,256]{2,1,0:T(1,128)S(1)}, ...), branch_computations={%region_5.8_spmd, %region_8.10_spmd} | conditional | flops 1611402240 | bytes 60818224 | solution.py:247
  65.8 0.1 add_bitcast_fusion
  65.9 0.2 select_reduce_fusion.1
  66.1 0.1 reshape.59.index_ref
  66.2 1.5 branch_1_fun.4
  67.7 0.0 copy-start.5
  67.7 4.0 %all-to-all-start.2 = ((bf16[4,12,16,512]{3,2,1,0:T(8,128)(2,1)}), bf16[4,12,16,512]{3,2,1,0:T(8,128)(2,1)S(1)}, u32[]{:S(2)}, u32[]{:S(2)}) async-start(bf16[4,12,16,512]{3,2,1,0:T(8,128)(2,1)} %bitcast.2), calls=%async_computation.2 | async-start | bytes 1572864 | tf_op jit(solution)/shard_map/cond/branch_1_fun/all_to_all | solution.py:231
  71.7 0.1 copy.46
  71.8 0.6 dynamic_slice.4
  73.1 7.0 %all-to-all-done.2.kv_ref = bf16[4,12,16,512]{3,2,1,0:T(8,128)(2,1)S(1)} async-done(((bf16[4,12,16,512]{3,2,1,0:T(8,128)(2,1)}), bf16[4,12,16,512]{3,2,1,0:T(8,128)(2,1)S(1)}, u32[]{:S(2)}, u32[]{:S(2)}) %all-to-all-start.2) | async-done | bytes 786464 | tf_op jit(solution)/shard_map/cond/branch_1_fun/all_to_all | solution.py:231
  80.1 0.0 copy-done.5
  80.1 7.7 %branch_1_fun.5 = (bf16[8,2,256,256]{3,2,1,0:T(8,128)(2,1)}, bf16[8,2,256,256]{3,2,1,0:T(8,128)(2,1)}, bf16[4,12,16,512]{3,2,1,0:T(8,128)(2,1)}) custom-call(s32[8,4]{1,0:T(8,128)S(1)} %subtract_clamp_fusion.src_ref, s32[8,4]{1,0:T(8,128)S(1)} %get-tuple-element.83.doc_ref, s32[8,1,256]{2,1,0:T(1,128)S(1)} %get-tuple-element.84.tok_ref, ...), custom_call_target="tpu_custom_call" | custom-call | flops 1073741824 | bytes 9437184 | tf_op jit(solution)/shard_map/cond/branch_1_fun/pallas_call | solution.py:133
  87.8 3.5 %all-to-all-start.3 = ((bf16[4,12,16,512]{3,2,1,0:T(8,128)(2,1)}), bf16[4,12,16,512]{3,2,1,0:T(8,128)(2,1)S(1)}, u32[]{:S(2)}, u32[]{:S(2)}) async-start(bf16[4,12,16,512]{3,2,1,0:T(8,128)(2,1)} %get-tuple-element.96), calls=%async_computation.3 | async-start | bytes 1572864 | tf_op jit(solution)/shard_map/cond/branch_1_fun/all_to_all | solution.py:234
  91.3 0.0 copy-start.1
  91.3 1.6 %copy-done.1 = bf16[8,2,256,256]{3,2,1,0:T(8,128)(2,1)S(1)} copy-done((bf16[8,2,256,256]{3,2,1,0:T(8,128)(2,1)S(1)}, bf16[8,2,256,256]{3,2,1,0:T(8,128)(2,1)}, u32[]{:S(2)}) %copy-start.1) | copy-done | bytes 2097176 | tf_op jit(solution)/shard_map/cond
  92.9 0.0 copy-start.2
  92.9 1.6 %copy-done.2 = bf16[8,2,256,256]{3,2,1,0:T(8,128)(2,1)S(1)} copy-done((bf16[8,2,256,256]{3,2,1,0:T(8,128)(2,1)S(1)}, bf16[8,2,256,256]{3,2,1,0:T(8,128)(2,1)}, u32[]{:S(2)}) %copy-start.2) | copy-done | bytes 2097176 | tf_op jit(solution)/shard_map/cond
  94.5 3.7 %branch_1_fun.6 = (bf16[2048,256]{1,0:T(8,128)(2,1)}, bf16[2048,256]{1,0:T(8,128)(2,1)}) custom-call(s32[8,4]{1,0:T(8,128)S(1)} %subtract_clamp_fusion.src_ref, bf16[8,2,256,256]{3,2,1,0:T(8,128)(2,1)S(1)} %copy-done.1, bf16[8,2,256,256]{3,2,1,0:T(8,128)(2,1)S(1)} %copy-done.2, bf16[4,12,16,512]{3,2,1,0:T(8,128)(2,1)S(1)} %all-to-all-done.2.kv_ref), custom_call_target="tpu_custom_call" | custom-call | flops 536870912 | bytes 8388608 | tf_op jit(solution)/shard_map/cond/branch_1_fun/pallas_call | solution.py:153
  98.2 1.4 all-to-all-done.3
  99.6 1.8 %branch_1_fun.7 = bf16[32,16,512]{2,1,0:T(8,128)(2,1)} custom-call(s32[48]{0:T(128)S(1)} %reshape.59.index_ref, bf16[48,16,512]{2,1,0:T(8,128)(2,1)S(1)} %bitcast.27), custom_call_target="tpu_custom_call" | custom-call | bytes 2097152 | tf_op jit(solution)/shard_map/cond/branch_1_fun/pallas_call | solution.py:182
  101.4 5.2 %all-to-all-start.7 = ((bf16[32,16,512]{2,1,0:T(8,128)(2,1)}), bf16[32,16,512]{2,1,0:T(8,128)(2,1)S(1)}, u32[]{:S(2)}, u32[]{:S(2)}) async-start(bf16[32,16,512]{2,1,0:T(8,128)(2,1)} %get-tuple-element.105), calls=%async_computation.7 | async-start | bytes 1048576 | tf_op jit(solution)/shard_map/all_to_all | solution.py:249
  106.6 0.1 copy.47
  106.7 12.6 %all-to-all-done.7 = bf16[32,16,512]{2,1,0:T(8,128)(2,1)S(1)} async-done(((bf16[32,16,512]{2,1,0:T(8,128)(2,1)}), bf16[32,16,512]{2,1,0:T(8,128)(2,1)S(1)}, u32[]{:S(2)}, u32[]{:S(2)}) %all-to-all-start.7) | async-done | bytes 524320 | tf_op jit(solution)/shard_map/all_to_all | solution.py:249
  119.3 0.1 bitcast_reduce_fusion
  119.4 0.5 convolution_convert_fusion
  119.9 23.3 %all_to_all.46 = bf16[16,4,1280]{2,1,0:T(4,128)(2,1)S(1)} all-to-all(bf16[16,4,1280]{2,1,0:T(4,128)(2,1)S(1)} %reshape.80), channel_id=1, replica_groups=mesh['z'=8,'x'=4,'y'=8,'core'=2] {'y','core'}, dimensions={0} | all-to-all | bytes 327680 | tf_op jit(solution)/shard_map/all_to_all | solution.py:255
  143.3 0.1 reduce_sum.56
  143.4 12.3 %all_to_all.47 = bf16[16,4,1280]{2,1,0:T(4,128)(2,1)S(1)} all-to-all(bf16[16,4,1280]{2,1,0:T(4,128)(2,1)S(1)} %broadcast_in_dim.61), channel_id=1, replica_groups=mesh['z'=8,'x'=4,'y'=8,'core'=2] {'y','core'}, dimensions={0} | all-to-all | bytes 327680 | tf_op jit(solution)/shard_map/all_to_all | solution.py:198
  155.7 0.7 reshape.81
  (15 shorter events, 0.2 us)
Async XLA Ops:
  2.1 22.8 %all-to-all-start.4 = ((bf16[8,40,512]{2,1,0:T(8,128)(2,1)}), bf16[8,40,512]{2,1,0:T(8,128)(2,1)S(1)}, u32[]{:S(2)}, u32[]{:S(2)}) async-start(bf16[8,40,512]{2,1,0:T(8,128)(2,1)} %broadcast_in_dim.38), calls=%async_computation.4 | async-start | bytes 655360 | tf_op jit(solution)/shard_map/all_to_all | solution.py:198
  26.1 4.1 %copy-start.6 = (bf16[1,64,1280]{2,1,0:T(8,128)(2,1)S(1)}, bf16[1,64,1280]{2,1,0:T(8,128)(2,1)}, u32[]{:S(2)}) copy-start(bf16[1,64,1280]{2,1,0:T(8,128)(2,1)} %param.11) | copy-start | bytes 491524
  26.1 19.8 %all-to-all-start.5 = ((bf16[4,328,512]{2,1,0:T(8,128)(2,1)}), bf16[4,328,512]{2,1,0:T(8,128)(2,1)S(1)}, u32[]{:S(2)}, u32[]{:S(2)}) async-start(bf16[4,328,512]{2,1,0:T(8,128)(2,1)} %broadcast_in_dim.39), calls=%async_computation.5 | async-start | bytes 2686976 | tf_op jit(solution)/shard_map/all_to_all | solution.py:198
  46.1 5.8 %copy-start.8 = (s32[8,4]{0,1:T(4,128)S(1)}, s32[8,4]{0,1:T(4,128)}, u32[]{:S(2)}) copy-start(s32[8,4]{0,1:T(4,128)} %param.15) | copy-start | bytes 388
  46.1 19.7 %copy-start.7 = (s32[2048]{0:T(1024)S(1)}, s32[2048]{0:T(1024)}, u32[]{:S(2)}) copy-start(s32[2048]{0:T(1024)} %param.17) | copy-start | bytes 24580
  46.1 19.7 %copy-start.9 = (s32[32]{0:T(128)S(1)}, s32[32]{0:T(128)}, u32[]{:S(2)}) copy-start(s32[32]{0:T(128)} %param.16) | copy-start | bytes 388
  47.3 18.4 %all-to-all-start.6 = ((bf16[32,16,512]{2,1,0:T(8,128)(2,1)}), bf16[32,16,512]{2,1,0:T(8,128)(2,1)S(1)}, u32[]{:S(2)}, u32[]{:S(2)}) async-start(bf16[32,16,512]{2,1,0:T(8,128)(2,1)} %bitcast.31), calls=%async_computation.6 | async-start | bytes 1048576 | tf_op jit(solution)/shard_map/all_to_all | solution.py:221
  67.7 12.4 %copy-start.5 = (bf16[2048,256]{1,0:T(8,128)(2,1)S(1)}, bf16[2048,256]{1,0:T(8,128)(2,1)}, u32[]{:S(2)}) copy-start(bf16[2048,256]{1,0:T(8,128)(2,1)} %get-tuple-element.85.q_ref) | copy-start | bytes 3145732 | tf_op jit(solution)/shard_map/cond
  67.7 12.4 %all-to-all-start.2 = ((bf16[4,12,16,512]{3,2,1,0:T(8,128)(2,1)}), bf16[4,12,16,512]{3,2,1,0:T(8,128)(2,1)S(1)}, u32[]{:S(2)}, u32[]{:S(2)}) async-start(bf16[4,12,16,512]{3,2,1,0:T(8,128)(2,1)} %bitcast.2), calls=%async_computation.2 | async-start | bytes 1572864 | tf_op jit(solution)/shard_map/cond/branch_1_fun/all_to_all | solution.py:231
  87.8 11.8 %all-to-all-start.3 = ((bf16[4,12,16,512]{3,2,1,0:T(8,128)(2,1)}), bf16[4,12,16,512]{3,2,1,0:T(8,128)(2,1)S(1)}, u32[]{:S(2)}, u32[]{:S(2)}) async-start(bf16[4,12,16,512]{3,2,1,0:T(8,128)(2,1)} %get-tuple-element.96), calls=%async_computation.3 | async-start | bytes 1572864 | tf_op jit(solution)/shard_map/cond/branch_1_fun/all_to_all | solution.py:234
  91.3 1.6 %copy-start.1 = (bf16[8,2,256,256]{3,2,1,0:T(8,128)(2,1)S(1)}, bf16[8,2,256,256]{3,2,1,0:T(8,128)(2,1)}, u32[]{:S(2)}) copy-start(bf16[8,2,256,256]{3,2,1,0:T(8,128)(2,1)} %get-tuple-element.92.low_ref) | copy-start | bytes 6291460 | tf_op jit(solution)/shard_map/cond
  92.9 1.6 %copy-start.2 = (bf16[8,2,256,256]{3,2,1,0:T(8,128)(2,1)S(1)}, bf16[8,2,256,256]{3,2,1,0:T(8,128)(2,1)}, u32[]{:S(2)}) copy-start(bf16[8,2,256,256]{3,2,1,0:T(8,128)(2,1)} %get-tuple-element.93.sg_ref) | copy-start | bytes 6291460 | tf_op jit(solution)/shard_map/cond
  101.4 17.9 %all-to-all-start.7 = ((bf16[32,16,512]{2,1,0:T(8,128)(2,1)}), bf16[32,16,512]{2,1,0:T(8,128)(2,1)S(1)}, u32[]{:S(2)}, u32[]{:S(2)}) async-start(bf16[32,16,512]{2,1,0:T(8,128)(2,1)} %get-tuple-element.105), calls=%async_computation.7 | async-start | bytes 1048576 | tf_op jit(solution)/shard_map/all_to_all | solution.py:249
